TPU v7x, 32 devices: a whole 2x2x4 slice. The times are simulated.
32 devices in a mesh: fsdp: 8 (over z, core), tp: 4 (over y, x).
Axes of the slice: x: 2, y: 2, z: 4, core: 2. Of those that a mesh axis runs over, the one named last changes fastest.
Arguments:
- master_qo: float32 [2, 5120, 8192], P(None, ('fsdp', 'tp')), may hold values from -0.078125 to 0.078125
- master_kv: float32 [2, 5120, 1024], P(None, ('fsdp', 'tp')), may hold values from -0.078125 to 0.078125
- moment1_qo: float32 [2, 5120, 8192], P(None, ('fsdp', 'tp')), may hold values from -0.00061035156 to 0.00061035156
- moment1_kv: float32 [2, 5120, 1024], P(None, ('fsdp', 'tp')), may hold values from -0.00061035156 to 0.00061035156
- moment2_qo: float32 [2, 5120, 8192], P(None, ('fsdp', 'tp')), may hold values from 0 to 1, as said below
- moment2_kv: float32 [2, 5120, 1024], P(None, ('fsdp', 'tp')), may hold values from 0 to 1, as said below
- grad_qo: float32 [2, 5120, 8192], P(None, ('fsdp', 'tp')), may hold values from -13 to 13
- grad_kv: float32 [2, 5120, 1024], P(None, ('fsdp', 'tp')), may hold values from -13 to 13
- hidden: bfloat16 [512, 5120], P(('fsdp', 'tp')), may hold values from -3 to 3
- norm_gain: float32 [5120], replicated, may hold values from 0.5 to 1.5
- qk_gain: float32 [2, 128], replicated, may hold values from 0.25 to 1.75
- key_cache: bfloat16 [512, 8, 128, 128], P('fsdp', 'tp'), may hold values from -310 to 310
- cached_value_rows: bfloat16 [512, 8, 128, 128], P('fsdp', 'tp'), may hold values from -18 to 18
- lengths: int32 [512], P('fsdp'), may hold values from 1 to 128, as said below
Outputs:
- new_master_qo: float32 [2, 5120, 8192], P(None, ('fsdp', 'tp'))
- new_master_kv: float32 [2, 5120, 1024], P(None, ('fsdp', 'tp'))
- new_moment1_qo: float32 [2, 5120, 8192], P(None, ('fsdp', 'tp'))
- new_moment1_kv: float32 [2, 5120, 1024], P(None, ('fsdp', 'tp'))
- new_moment2_qo: float32 [2, 5120, 8192], P(None, ('fsdp', 'tp'))
- new_moment2_kv: float32 [2, 5120, 1024], P(None, ('fsdp', 'tp'))
- new_hidden: bfloat16 [512, 5120], P(('fsdp', 'tp'))
- new_key: bfloat16 [512, 8, 128], P('fsdp', 'tp')
- new_value: bfloat16 [512, 8, 128], P('fsdp', 'tp')
Inputs may be any that keep to these rules, and one draw needn't show every extreme that they name: `moment2_qo`: positive. `moment2_kv`: positive. `lengths`: some row holds 128 in every draw.
All inputs are finite; a program needn't handle non-finite values.
Results may differ from a plain program's by a relative error of at most 0.012.
The roundings to bfloat16 on the way count: a program that leaves them out, or rounds other values in their place, can miss the bound.
Values may be sent and summed in bfloat16 or wider, within the bound.
No kernel may reach another device: no remote copies, remote signals or barrier semaphores. Data moves between devices by JAX's collectives and lax.ppermute only.
A program may use at most 320 MiB of HBM per device.

v0:
```python
import math

import jax
import jax.numpy as jnp
from jax import lax
from jax.sharding import PartitionSpec as P

clip_limit = 1.0
beta_one = 0.9
beta_two = 0.95
learn_rate = 0.01
decay_rate = 0.1
adam_step = 10.0
eps_adam = 1e-08
eps_norm = 1e-06
rope_base = 1000000.0


def adam_update(master, moment_one, moment_two, gradient, clip_factor):
    clipped = gradient * clip_factor
    moment_one = beta_one * moment_one + (1.0 - beta_one) * clipped
    moment_two = beta_two * moment_two + (1.0 - beta_two) * clipped * clipped
    fix_one = 1.0 - beta_one**adam_step
    fix_two = 1.0 - beta_two**adam_step
    step_size = moment_one / fix_one / (jnp.sqrt(moment_two / fix_two) + eps_adam)
    master = master - learn_rate * (step_size + decay_rate * master)
    return (master, moment_one, moment_two)


def root_scale(values, gain_vec):
    mean_square = jnp.mean(values * values, axis=-1, keepdims=True)
    return values * lax.rsqrt(mean_square + eps_norm) * gain_vec


def rotate(values, positions):
    half_dim = values.shape[-1] // 2
    frequency = rope_base ** (-(jnp.arange(half_dim, dtype=jnp.float32) * 2.0) / values.shape[-1])
    angles = positions.astype(jnp.float32)[:, None] * frequency[None, :]
    cosine = jnp.cos(angles)[:, None, :]
    sine_part = jnp.sin(angles)[:, None, :]
    first_half = values[..., :half_dim]
    second = values[..., half_dim:]
    return jnp.concatenate(
        [first_half * cosine - second * sine_part, second * cosine + first_half * sine_part],
        axis=-1,
    )


def attend(queries, key_new, value_new, qk_gain, key_cache, cached_value_rows, lengths):
    row_count = queries.shape[0]
    kv_heads = key_cache.shape[1]
    head_dim = key_cache.shape[-1]
    queries = queries.reshape(row_count, -1, head_dim)
    key_new = key_new.reshape(row_count, kv_heads, head_dim)
    rotated = rotate(root_scale(queries, qk_gain[0]), lengths).astype(jnp.bfloat16)
    new_key = rotate(root_scale(key_new, qk_gain[1]), lengths).astype(jnp.bfloat16)
    new_value = value_new.reshape(row_count, kv_heads, head_dim).astype(jnp.bfloat16)
    group_size = rotated.shape[1] // kv_heads
    grouped = rotated.reshape(row_count, kv_heads, group_size, head_dim)
    inv_root = 1.0 / math.sqrt(head_dim)
    scores = (
        jnp.einsum("bkgd,bkcd->bkgc", grouped, key_cache, preferred_element_type=jnp.float32)
        * inv_root
    )
    self_score = (
        jnp.sum(grouped.astype(jnp.float32) * new_key.astype(jnp.float32)[:, :, None, :], axis=-1)
        * inv_root
    )
    slots = jnp.arange(key_cache.shape[2], dtype=jnp.int32)
    visible = (slots[None, :] < lengths[:, None])[:, None, None, :]
    masked = jnp.where(visible, scores, -1e30)
    peak = jnp.maximum(jnp.max(masked, axis=-1), self_score)
    weights = jnp.where(visible, jnp.exp(masked - peak[..., None]), 0.0)
    self_weight = jnp.exp(self_score - peak)
    denominator = jnp.sum(weights, axis=-1) + self_weight
    weights_bf = (weights / denominator[..., None]).astype(jnp.bfloat16)
    self_bf = (self_weight / denominator).astype(jnp.bfloat16)
    mixture = jnp.einsum(
        "bkgc,bkcd->bkgd", weights_bf, cached_value_rows, preferred_element_type=jnp.float32
    )
    mixture = (
        mixture
        + self_bf.astype(jnp.float32)[..., None] * new_value.astype(jnp.float32)[:, :, None, :]
    )
    attended = mixture.reshape(row_count, -1).astype(jnp.bfloat16)
    return (attended, new_key, new_value)


def local(
    master_qo,
    master_kv,
    moment1_qo,
    moment1_kv,
    moment2_qo,
    moment2_kv,
    grad_qo,
    grad_kv,
    hidden,
    norm_gain,
    qk_gain,
    key_cache,
    cached_value_rows,
    lengths,
):
    local_squares = jnp.sum(grad_qo * grad_qo) + jnp.sum(grad_kv * grad_kv)
    grand_total = lax.psum(local_squares, ("fsdp", "tp"))
    clip_factor = jnp.minimum(1.0, clip_limit / (jnp.sqrt(grand_total) + eps_norm))
    fresh_qo = adam_update(master_qo, moment1_qo, moment2_qo, grad_qo, clip_factor)
    fresh_kv = adam_update(master_kv, moment1_kv, moment2_kv, grad_kv, clip_factor)
    cast_qo = fresh_qo[0].astype(jnp.bfloat16)
    cast_kv = fresh_kv[0].astype(jnp.bfloat16)
    band_qo, band_kv = (
        lax.all_gather(cast_qo, "tp", axis=1, tiled=True),
        lax.all_gather(cast_kv, "tp", axis=1, tiled=True),
    )
    member_count = lax.axis_size("tp")
    member_index = lax.axis_index("tp")
    width_qo = band_qo.shape[2] // member_count
    width_kv = band_kv.shape[2] // member_count
    slab_qo = lax.dynamic_slice_in_dim(band_qo, member_index * width_qo, width_qo, 2)
    slab_kv = lax.dynamic_slice_in_dim(band_kv, member_index * width_kv, width_kv, 2)
    normed_own = root_scale(hidden.astype(jnp.float32), norm_gain).astype(jnp.bfloat16)
    normed = lax.all_gather(normed_own, "tp", axis=0, tiled=True)
    full_qo, full_kv = (
        lax.all_gather(slab_qo, "fsdp", axis=1, tiled=True),
        lax.all_gather(slab_kv, "fsdp", axis=1, tiled=True),
    )
    queries = jnp.dot(normed, full_qo[0], preferred_element_type=jnp.float32)
    key_new = jnp.dot(normed, full_kv[0], preferred_element_type=jnp.float32)
    value_new = jnp.dot(normed, full_kv[1], preferred_element_type=jnp.float32)
    attended, new_key, new_value = attend(
        queries, key_new, value_new, qk_gain, key_cache, cached_value_rows, lengths
    )
    row_terms = lax.dot_general(
        attended, full_qo[1], (((1,), (1,)), ((), ())), preferred_element_type=jnp.float32
    )
    own_rows = lax.psum_scatter(row_terms, "tp", scatter_dimension=0, tiled=True)
    new_hidden = (hidden.astype(jnp.float32) + own_rows).astype(jnp.bfloat16)
    return (
        fresh_qo[0],
        fresh_kv[0],
        fresh_qo[1],
        fresh_kv[1],
        fresh_qo[2],
        fresh_kv[2],
        new_hidden,
        new_key,
        new_value,
    )


def solution(mesh):
    return jax.shard_map(
        local,
        mesh=mesh,
        in_specs=(
            P(None, ("fsdp", "tp"), None),
            P(None, ("fsdp", "tp"), None),
            P(None, ("fsdp", "tp"), None),
            P(None, ("fsdp", "tp"), None),
            P(None, ("fsdp", "tp"), None),
            P(None, ("fsdp", "tp"), None),
            P(None, ("fsdp", "tp"), None),
            P(None, ("fsdp", "tp"), None),
            P(("fsdp", "tp"), None),
            P(),
            P(),
            P("fsdp", "tp", None, None),
            P("fsdp", "tp", None, None),
            P("fsdp"),
        ),
        out_specs=(
            P(None, ("fsdp", "tp"), None),
            P(None, ("fsdp", "tp"), None),
            P(None, ("fsdp", "tp"), None),
            P(None, ("fsdp", "tp"), None),
            P(None, ("fsdp", "tp"), None),
            P(None, ("fsdp", "tp"), None),
            P(("fsdp", "tp"), None),
            P("fsdp", "tp", None),
            P("fsdp", "tp", None),
        ),
        check_vma=False,
    )
```

profile of v0, /device:TPU:0, one launch (start us, length us, event | category | flops | bytes accessed | tf_op | source)
XLA Modules:
  0.0 824.3 jit_solution(9273295203425584058)
XLA Ops:
  7.2 0.0 copy-start
  7.2 0.0 copy-start.3
  7.2 0.0 all-gather.9.cloned.1.call-start
  7.2 7.4 multiply_reduce_fusion
  14.7 0.9 multiply_reduce_fusion.1
  16.9 42.0 %psum.7 = f32[]{:T(128)} all-reduce(f32[]{:T(128)S(6)} %add.98), channel_id=1, replica_groups=mesh['fsdp'=8,'tp'=4] {'fsdp','tp'}, use_global_device_ids=true, to_apply=%region_2.0 | all-reduce | flops 1 | bytes 8 | tf_op jit(solution)/shard_map/psum | solution.py:106
  59.7 0.0 copy-done.3
  59.7 4.6 fusion.25
  64.3 0.0 all-gather.9.cloned.1.call-update
  64.3 0.0 all-gather.5.cloned.1.call-start
  64.3 27.1 %fusion.27 = (bf16[2,160,8192]{2,1,0:T(8,128)(2,1)}, f32[2,160,8192]{2,1,0:T(8,128)}, f32[2,160,8192]{2,1,0:T(8,128)}, f32[2,160,8192]{2,1,0:T(8,128)}) fusion(f32[2,160,8192]{2,1,0:T(8,128)} %param.14, f32[2,160,8192]{2,1,0:T(8,128)} %param.20, f32[]{:T(128)S(6)} %min.3, f32[2,160,8192]{2,1,0:T(8,128)} %param.16, f32[2,160,8192]{2,1,0:T(8,128)} %param.18), kind=kLoop, calls=%fused_computation.71 | loop fusion | flops 44564480 | bytes 78643200 | tf_op jit(solution)/shard_map/convert_element_type | solution.py:110
  91.5 0.0 all-gather.5.cloned.1.call-update
  91.5 0.0 all-gather.11.cloned.1.call-start
  91.6 12.5 %all-gather.9.cloned.1.call-done = bf16[2,640,1024]{2,1,0:T(8,128)(2,1)} async-done(((bf16[2,160,1024]{2,1,0:T(8,128)(2,1)}), bf16[2,640,1024]{2,1,0:T(8,128)(2,1)}) %all-gather.9.cloned.1.call-update) | async-done | bytes 2621456 | tf_op jit(solution)/shard_map/all_gather | solution.py:114
  104.1 2.0 constant_dynamic-slice_fusion
  106.1 0.0 all-gather.11.cloned.1.call-update
  106.1 0.0 all-gather.7.cloned.1.call-start
  106.2 192.2 %all-gather.5.cloned.1.call-done = bf16[2,640,8192]{2,1,0:T(8,128)(2,1)} async-done(((bf16[2,160,8192]{2,1,0:T(8,128)(2,1)}), bf16[2,640,8192]{2,1,0:T(8,128)(2,1)}) %all-gather.5.cloned.1.call-update) | async-done | bytes 20971536 | tf_op jit(solution)/shard_map/all_gather | solution.py:113
  298.4 5.7 constant_dynamic-slice_fusion.1
  304.1 0.0 all-gather.7.cloned.1.call-update
  304.1 0.0 reduce-scatter.2.cloned.1.call-start
  304.2 0.6 copy-done.7
  304.8 0.3 copy-done.2
  305.0 0.2 fusion.11
  305.2 0.0 copy-done.5
  305.2 0.1 fusion.13
  305.3 10.5 %all_gather.15 = bf16[64,5120]{1,0:T(8,128)(2,1)S(1)} all-gather(bf16[16,5120]{1,0:T(8,128)(2,1)S(1)} %fusion.13), channel_id=1, replica_groups=mesh['fsdp'=8,'tp'=4] {'tp'}, dimensions={0}, use_global_device_ids=true | all-gather | bytes 819200 | tf_op jit(solution)/shard_map/all_gather | solution.py:123
  315.9 0.1 iota_compare_fusion
  315.9 0.2 multiply_cosine_fusion
  316.1 39.9 %all-gather.11.cloned.1.call-done = bf16[2,5120,256]{2,1,0:T(8,128)(2,1)} async-done(((bf16[2,640,256]{2,1,0:T(8,128)(2,1)}), bf16[2,5120,256]{2,1,0:T(8,128)(2,1)}) %all-gather.11.cloned.1.call-update) | async-done | bytes 5242896 | tf_op jit(solution)/shard_map/all_gather | solution.py:126
  356.0 4.4 slice_bitcast_fusion.4
  360.4 4.5 copy.55
  365.0 3.4 convolution_convert_fusion
  368.4 0.7 copy.56
  369.1 2.8 copy.47
  371.9 3.5 multiply_reduce_fusion.4
  375.4 0.1 multiply_multiply_fusion.3
  375.5 0.1 subtract_convert_fusion.1
  375.6 0.1 pad_maximum_fusion.2
  375.7 338.2 %all-gather.7.cloned.1.call-done = bf16[2,5120,2048]{2,1,0:T(8,128)(2,1)} async-done(((bf16[2,640,2048]{2,1,0:T(8,128)(2,1)}), bf16[2,5120,2048]{2,1,0:T(8,128)(2,1)}) %all-gather.7.cloned.1.call-update) | async-done | bytes 41943056 | tf_op jit(solution)/shard_map/all_gather | solution.py:125
  714.0 17.5 %slice_bitcast_fusion.2 = bf16[2048,5120]{0,1:T(8,128)(2,1)} fusion(bf16[2,5120,2048]{2,1,0:T(8,128)(2,1)} %all-gather.7.cloned.1.call-done), kind=kLoop, calls=%fused_computation.2 | loop fusion | bytes 41943040 | tf_op jit(solution)/shard_map/dot_general | solution.py:128
  731.5 26.1 %copy.44 = bf16[2048,5120]{1,0:T(8,128)(2,1)} copy(bf16[2048,5120]{0,1:T(8,128)(2,1)} %slice_bitcast_fusion.2) | data formatting | bytes 41943040 | tf_op jit(solution)/shard_map/dot_general | solution.py:128
  757.6 10.9 %multiply_reduce_fusion.3 = (f32[64,16]{0,1:T(8,128)S(1)}, f32[64,16,128]{2,0,1:T(8,128)S(1)}) fusion(bf16[16,128,5120]{2,1,0:T(8,128)(2,1)} %bitcast.45, bf16[64,5120]{1,0:T(8,128)(2,1)S(1)} %all_gather.15), kind=kOutput, calls=%fused_computation.31 | convolution fusion | flops 1342438400 | bytes 22155264 | tf_op jit(solution)/shard_map/dot_general | solution.py:128
  768.6 0.2 multiply_multiply_fusion.2
  768.8 0.3 subtract_convert_fusion
  769.0 0.0 copy-start.4
  769.0 0.2 copy.46
  769.2 0.2 copy.45
  769.4 2.4 fusion.29
  771.8 0.1 copy.50
  771.9 0.4 multiply_reduce_fusion.2
  772.3 0.1 copy.49
  772.4 0.1 copy.51
  772.5 0.4 fusion.10
  773.0 0.1 copy.52
  773.1 0.1 copy.54
  773.2 0.1 copy.53
  773.3 3.4 fusion.4
  776.7 11.7 %fusion = f32[64,5120]{1,0:T(8,128)} fusion(bf16[2,5120,2048]{2,1,0:T(8,128)(2,1)} %all-gather.7.cloned.1.call-done, bf16[8,8,16,128]{3,2,1,0:T(8,128)(2,1)S(1)} %bitcast.50), kind=kOutput, calls=%fused_computation.1 | convolution fusion | flops 1342177280 | bytes 22544384 | tf_op jit(solution)/shard_map/dot_general | solution.py:134
  788.4 0.0 reduce-scatter.2.cloned.1.call-update
  788.4 0.6 copy.57
  789.1 0.6 copy.58
  789.7 26.4 %reduce-scatter.2.cloned.1.call-done = f32[16,5120]{1,0:T(8,128)} async-done(((f32[64,5120]{1,0:T(8,128)}), f32[16,5120]{1,0:T(8,128)}) %reduce-scatter.2.cloned.1.call-update) | async-done | bytes 327696 | tf_op jit(solution)/shard_map/reduce_scatter | solution.py:137
  816.1 1.7 fusion.14
  (18 shorter events, 0.1 us)
Async XLA Ops:
  7.2 7.5 copy-start
  7.2 52.5 %copy-start.3 = (f32[2,160,1024]{2,1,0:T(8,128)S(1)}, f32[2,160,1024]{2,1,0:T(8,128)}, u32[]{:S(2)}) copy-start(f32[2,160,1024]{2,1,0:T(8,128)} %param.15) | copy-start | bytes 3932164
  7.2 96.9 %all-gather.9.cloned.1.call-start = ((), (), s32[]{:S(2)}) async-start(), calls=%async_computation.3 | async-start | bytes 3276800 | tf_op jit(solution)/shard_map/all_gather | solution.py:114
  64.3 234.1 %all-gather.5.cloned.1.call-start = ((), (), s32[]{:S(2)}) async-start(), calls=%async_computation.1 | async-start | bytes 26214400 | tf_op jit(solution)/shard_map/all_gather | solution.py:113
  91.5 264.5 %all-gather.11.cloned.1.call-start = ((), (), s32[]{:S(2)}) async-start(), calls=%async_computation.4 | async-start | bytes 5898240 | tf_op jit(solution)/shard_map/all_gather | solution.py:126
  106.1 607.9 %all-gather.7.cloned.1.call-start = ((), (), s32[]{:S(2)}) async-start(), calls=%async_computation.2 | async-start | bytes 47185920 | tf_op jit(solution)/shard_map/all_gather | solution.py:125
  304.1 0.7 copy-start.7
  304.1 0.9 copy-start.2
  304.1 1.1 copy-start.5
  304.1 11.7 %copy-start.6 = (f32[2,128]{1,0:T(2,128)S(1)}, f32[2,128]{1,0:T(2,128)}, u32[]{:S(2)}) copy-start(f32[2,128]{1,0:T(2,128)} %param.24) | copy-start | bytes 3076
  304.1 512.0 %reduce-scatter.2.cloned.1.call-start = ((), (), s32[]{:S(2)}) async-start(), calls=%async_computation.5 | async-start | bytes 1638400 | tf_op jit(solution)/shard_map/reduce_scatter | solution.py:137
  757.6 11.8 %copy-start.1 = (bf16[64,2,128,128]{3,2,1,0:T(8,128)(2,1)S(1)}, bf16[64,2,128,128]{3,2,1,0:T(8,128)(2,1)}, u32[]{:S(2)}) copy-start(bf16[64,2,128,128]{3,2,1,0:T(8,128)(2,1)} %param.25) | copy-start | bytes 12582916
  769.0 4.3 copy-start.4
Sparse Core Ops, SparseCore 0:
  64.4 39.6 all-gather.8
  105.9 192.4 all-gather.4
  300.0 55.9 all-gather.10
  357.5 356.3 all-gather.6
  788.6 27.5 reduce-scatter.1
where the time goes:
time: 826 us; the launch traced here: 824 us
  waiting for transfers between devices  609 us (74%)
  local copies, waits for them, and re-layouts  66.8 us (8%)
  blocking collectives  52.5 us (6%)
  other arithmetic  43.9 us (5%)
  matrix products  35.4 us (4%)
  between operations  16 us (2%)
    all_gather x1, waiting for transfers between devices, local(): lax.all_gather(slab_qo, 'fsdp', axis=1, tiled=True)  338 us
    all_gather x1, waiting for transfers between devices, local(): lax.all_gather(cast_qo, 'tp', axis=1, tiled=True)  192 us
    dot_general x2, local copies, waits for them, and re-layouts, local(): queries = jnp.dot(normed, full_qo[0], preferred_element_type=jnp.float32)  43.6 us
    psum x1, blocking collectives, local(): grand_total = lax.psum(local_squares, ('fsdp', 'tp'))  42 us
    all_gather x1, waiting for transfers between devices, local(): lax.all_gather(slab_kv, 'fsdp', axis=1, tiled=True)  39.9 us
    convert_element_type x1, other arithmetic, local(): cast_qo = fresh_qo[0].astype(jnp.bfloat16)  27.1 us
    reduce_scatter x1, waiting for transfers between devices, local(): lax.psum_scatter(row_terms, 'tp', scatter_dimension=0, tiled=True)  26.4 us
  transfers between devices with their start and end apart: 5, of which 5 were waited for; matrix products, arithmetic and copies ran while one was open for 7% of the time, Pallas kernels for 0%

commit v1 on v0

v1 whole, which is shorter than its diff:
```python
import functools
import math

import jax
import jax.numpy as jnp
from jax import lax
from jax.experimental import pallas as pl
from jax.experimental.pallas import tpu as pltpu
from jax.sharding import PartitionSpec as P

clip_limit = 1.0
beta_one = 0.9
beta_two = 0.95
learn_rate = 0.01
decay_rate = 0.1
adam_step = 10.0
eps_adam = 1e-08
eps_norm = 1e-06
rope_base = 1000000.0
kernel_vmem = 48 * 1024 * 1024

F32 = jnp.float32
BF16 = jnp.bfloat16
ANY = pl.BlockSpec(memory_space=pl.ANY)


def adam_math(master, moment_one, moment_two, gradient, clip_factor):
    clipped = gradient * clip_factor
    moment_one = beta_one * moment_one + (1.0 - beta_one) * clipped
    moment_two = beta_two * moment_two + (1.0 - beta_two) * clipped * clipped
    fix_one = 1.0 - beta_one**adam_step
    fix_two = 1.0 - beta_two**adam_step
    root = jnp.sqrt(moment_two * (1.0 / fix_two)) + eps_adam
    step_size = moment_one * (1.0 / fix_one) / root
    master = master - learn_rate * (step_size + decay_rate * master)
    return (master, moment_one, moment_two)


def xor_perm(count, mask):
    return [(i, i ^ mask) for i in range(count)]


def xor_order(blocks, mask):
    count = blocks.shape[0]
    bit = 1
    while bit < count:
        pairs = blocks.reshape((count // (2 * bit), 2, bit) + blocks.shape[1:])
        swapped = jnp.flip(pairs, axis=1).reshape(blocks.shape)
        blocks = jnp.where((mask & bit) != 0, swapped, blocks)
        bit *= 2
    return blocks


def member_order(slabs, member):
    return xor_order(jnp.stack([slabs[-1]] + list(slabs[:-1])), member)


def row_parts(rows):
    return 2 if rows % 32 == 0 else 1


def slab_spec(place, parts, block_rows, width):
    def index(i, r, _):
        moving = jnp.where(i == place, r, parts - 1)
        return (jnp.where(i < place, 0, moving), 0)

    return pl.BlockSpec((block_rows, width), index)


def input_proj_kernel(members, group, head_dim, me_ref, clip_ref, *refs):
    ins, rest = refs[:8], refs[8:]
    rest = rest[len(rest) - 6 - members:]
    outs, slabs = rest[:6], rest[6:]
    clip = clip_ref[0, 0]
    fresh_q = adam_math(ins[0][0], ins[2][0], ins[4][0], ins[6][0], clip)
    fresh_k = adam_math(ins[1][0], ins[3][0], ins[5][0], ins[7][0], clip)
    fresh_v = adam_math(ins[1][1], ins[3][1], ins[5][1], ins[7][1], clip)
    for n in range(3):
        outs[2 * n][0] = fresh_q[n]
        outs[2 * n + 1][0] = fresh_k[n]
        outs[2 * n + 1][1] = fresh_v[n]
    for place in range(members):

        @pl.when(pl.program_id(0) == place)
        def _(place=place):
            slab = slabs[place]
            slab[:, :group] = fresh_q[0].astype(BF16)
            slab[:, group : group + head_dim] = fresh_k[0].astype(BF16)
            slab[:, group + head_dim :] = fresh_v[0].astype(BF16)


def output_proj_kernel(members, me_ref, clip_ref, *refs):
    ins, rest = refs[:4], refs[4:]
    rest = rest[len(rest) - 3 - members:]
    outs, slabs = rest[:3], rest[3:]
    fresh = adam_math(ins[0][0], ins[1][0], ins[2][0], ins[3][0], clip_ref[0, 0])
    for n in range(3):
        outs[n][0] = fresh[n]
    for place in range(members):

        @pl.when(pl.program_id(0) == place)
        def _(place=place):
            slabs[place][...] = fresh[0].astype(BF16)


def update_input_proj(head, heads, members, me, clip, qo, kv, earlier):
    rows = qo[0].shape[1]
    kv_total = heads * members
    group = qo[0].shape[2] // kv_total
    head_dim = kv[0].shape[2] // kv_total
    parts = row_parts(rows)
    block_rows = rows // parts

    def column(i, me_ref):
        return (me_ref[0] ^ ((i + 1) % members)) * heads + head

    qo_spec = pl.BlockSpec((1, block_rows, group), lambda i, r, m: (0, r, column(i, m)))
    kv_spec = pl.BlockSpec((2, block_rows, head_dim), lambda i, r, m: (0, r, column(i, m)))
    width = group + 2 * head_dim
    ins = [x for pair in zip(qo, kv) for x in pair]
    shapes = [jax.ShapeDtypeStruct(x.shape, F32) for x in ins[:6]]
    slabs = [jax.ShapeDtypeStruct((rows, width), BF16)] * members
    aliases = {}
    if earlier is not None:
        aliases = {10 + n: n for n in range(6)}
    earlier = [] if earlier is None else list(earlier)
    count = rows * members * (group + 2 * head_dim)
    results = pl.pallas_call(
        functools.partial(input_proj_kernel, members, group, head_dim),
        grid_spec=pltpu.PrefetchScalarGridSpec(
            num_scalar_prefetch=1,
            grid=(members, parts),
            in_specs=[pl.BlockSpec(memory_space=pltpu.SMEM)]
            + [qo_spec, kv_spec] * 4
            + [ANY] * len(earlier),
            out_specs=[qo_spec, kv_spec] * 3
            + [slab_spec(n, parts, block_rows, width) for n in range(members)],
        ),
        out_shape=shapes + slabs,
        input_output_aliases=aliases,
        compiler_params=pltpu.CompilerParams(vmem_limit_bytes=kernel_vmem),
        cost_estimate=pl.CostEstimate(
            flops=20 * count, bytes_accessed=30 * count, transcendentals=2 * count
        ),
    )(me, clip, *ins, *earlier)
    return results[:6], results[6:]


def update_output_proj(members, me, clip, qo, earlier):
    rows = qo[0].shape[1]
    width = qo[0].shape[2] // members
    parts = row_parts(rows)
    block_rows = rows // parts

    def column(i, me_ref):
        return me_ref[0] ^ ((i + 1) % members)

    spec = pl.BlockSpec((1, block_rows, width), lambda i, r, m: (1, r, column(i, m)))
    count = rows * members * width
    results = pl.pallas_call(
        functools.partial(output_proj_kernel, members),
        grid_spec=pltpu.PrefetchScalarGridSpec(
            num_scalar_prefetch=1,
            grid=(members, parts),
            in_specs=[pl.BlockSpec(memory_space=pltpu.SMEM)] + [spec] * 4 + [ANY] * 3,
            out_specs=[spec] * 3 + [slab_spec(n, parts, block_rows, width) for n in range(members)],
        ),
        out_shape=[jax.ShapeDtypeStruct(x.shape, F32) for x in qo[:3]]
        + [jax.ShapeDtypeStruct((rows, width), BF16)] * members,
        input_output_aliases={6 + n: n for n in range(3)},
        compiler_params=pltpu.CompilerParams(vmem_limit_bytes=kernel_vmem),
        cost_estimate=pl.CostEstimate(
            flops=20 * count, bytes_accessed=30 * count, transcendentals=2 * count
        ),
    )(me, clip, *qo, *earlier)
    return results[:3], results[3:]


def project_kernel(members, me_ref, x_ref, *refs):
    slabs, (send_ref, keep_ref, weight) = refs[:members], refs[members:]
    rows = slabs[0].shape[0]

    @pl.when(pl.program_id(0) == 0)
    def _():
        for place in range(members):
            owner = me_ref[0] ^ ((place + 1) % members)
            start = pl.multiple_of(owner * rows, rows)
            weight[pl.ds(start, rows), :] = slabs[place][...]

    part = jnp.dot(x_ref[0], weight[...], preferred_element_type=F32)

    @pl.when(pl.program_id(0) == 0)
    def _():
        send_ref[...] = part.astype(BF16)

    @pl.when(pl.program_id(0) == 1)
    def _():
        keep_ref[...] = part


def project(me, x, slabs):
    members = len(slabs)
    _, rows, depth = x.shape
    width = slabs[0].shape[1]
    if slabs[0].shape[0] % 16:
        weight = member_order(slabs, me[0]).reshape(depth, width)
        part = jnp.dot(x, weight, preferred_element_type=F32)
        return part[0].astype(BF16), part[1]
    whole = pl.BlockSpec(slabs[0].shape, lambda i, m: (0, 0))
    out = pl.BlockSpec((rows, width), lambda i, m: (0, 0))
    return pl.pallas_call(
        functools.partial(project_kernel, members),
        grid_spec=pltpu.PrefetchScalarGridSpec(
            num_scalar_prefetch=1,
            grid=(2,),
            in_specs=[pl.BlockSpec((1, rows, depth), lambda i, m: (i, 0, 0))] + [whole] * members,
            out_specs=[out, out],
            scratch_shapes=[pltpu.VMEM((depth, width), BF16)],
        ),
        out_shape=[
            jax.ShapeDtypeStruct((rows, width), BF16),
            jax.ShapeDtypeStruct((rows, width), F32),
        ],
        compiler_params=pltpu.CompilerParams(vmem_limit_bytes=kernel_vmem),
        cost_estimate=pl.CostEstimate(
            flops=4 * rows * depth * width, bytes_accessed=2 * 4 * rows * width, transcendentals=0
        ),
    )(me, x, *slabs)


def expand_kernel(members, zones, me_ref, core_ref, *refs):
    att, refs = refs[:zones], refs[zones:]
    slabs, refs = refs[: 2 * members], refs[2 * members :]
    outs, (weight, total) = refs[:members], refs[members:]
    rows = slabs[0].shape[0]
    row_count = att[0].shape[0]
    share = row_count // members
    for other in range(2):
        for place in range(members):
            owner = (core_ref[0] ^ other) * members + (me_ref[0] ^ ((place + 1) % members))
            start = pl.multiple_of(owner * rows, rows)
            weight[pl.ds(start, rows), :] = slabs[other * members + place][...]
    stacked = jnp.concatenate([a[...] for a in att], axis=0)
    part = lax.dot_general(
        stacked, weight[...], (((1,), (1,)), ((), ())), preferred_element_type=F32
    )
    for zone in range(zones):
        for member in range(members):
            first = zone * row_count + member * share
            total[member, zone * share : (zone + 1) * share, :] = part[first : first + share, :]
    for mask in range(members):
        outs[mask][...] = total[me_ref[0] ^ mask]


def expand(me, core, att, slabs):
    zones, members = len(att), len(slabs) // 2
    row_count, depth = att[0].shape
    rows = slabs[0].shape[0]
    width = 2 * members * rows
    share = zones * row_count // members
    if rows % 16:
        halves = jnp.stack([member_order(slabs[:members], me[0]), member_order(slabs[members:], me[0])])
        weight = xor_order(halves, core[0]).reshape(width, depth)
        part = lax.dot_general(
            jnp.stack(att), weight, (((2,), (1,)), ((), ())), preferred_element_type=F32
        )
        part = part.reshape(zones, members, row_count // members, width).transpose(1, 0, 2, 3)
        part = xor_order(part, me[0]).reshape(members, share, width)
        return [part[k] for k in range(members)]
    vmem = pl.BlockSpec(memory_space=pltpu.VMEM)
    smem = pl.BlockSpec(memory_space=pltpu.SMEM)
    return pl.pallas_call(
        functools.partial(expand_kernel, members, zones),
        in_specs=[smem, smem] + [vmem] * (zones + 2 * members),
        out_specs=[vmem] * members,
        scratch_shapes=[
            pltpu.VMEM((width, depth), BF16),
            pltpu.VMEM((members, share, width), F32),
        ],
        out_shape=[jax.ShapeDtypeStruct((share, width), F32)] * members,
        compiler_params=pltpu.CompilerParams(vmem_limit_bytes=kernel_vmem),
        cost_estimate=pl.CostEstimate(
            flops=2 * zones * row_count * depth * width,
            bytes_accessed=2 * width * depth,
            transcendentals=0,
        ),
    )(me, core, *att, *slabs)


def root_scale(values, gain_vec):
    mean_square = jnp.mean(values * values, axis=-1, keepdims=True)
    return values * lax.rsqrt(mean_square + eps_norm) * gain_vec


def rotate(values, positions):
    half_dim = values.shape[-1] // 2
    frequency = rope_base ** (-(jnp.arange(half_dim, dtype=F32) * 2.0) / values.shape[-1])
    angles = positions.astype(F32)[:, None] * frequency[None, :]
    cosine = jnp.cos(angles)[:, None, :]
    sine_part = jnp.sin(angles)[:, None, :]
    first_half = values[..., :half_dim]
    second = values[..., half_dim:]
    return jnp.concatenate(
        [first_half * cosine - second * sine_part, second * cosine + first_half * sine_part],
        axis=-1,
    )


def attend(queries, key_new, value_new, qk_gain, key_cache, cached_value_rows, lengths):
    row_count = queries.shape[0]
    kv_heads = key_cache.shape[1]
    head_dim = key_cache.shape[-1]
    queries = queries.reshape(row_count, -1, head_dim)
    key_new = key_new.reshape(row_count, kv_heads, head_dim)
    rotated = rotate(root_scale(queries, qk_gain[0]), lengths).astype(BF16)
    new_key = rotate(root_scale(key_new, qk_gain[1]), lengths).astype(BF16)
    new_value = value_new.reshape(row_count, kv_heads, head_dim).astype(BF16)
    group_size = rotated.shape[1] // kv_heads
    grouped = rotated.reshape(row_count, kv_heads, group_size, head_dim)
    inv_root = 1.0 / math.sqrt(head_dim)
    scores = (
        jnp.einsum("bkgd,bkcd->bkgc", grouped, key_cache, preferred_element_type=F32) * inv_root
    )
    self_score = (
        jnp.sum(grouped.astype(F32) * new_key.astype(F32)[:, :, None, :], axis=-1) * inv_root
    )
    slots = jnp.arange(key_cache.shape[2], dtype=jnp.int32)
    visible = (slots[None, :] < lengths[:, None])[:, None, None, :]
    masked = jnp.where(visible, scores, -1e30)
    peak = jnp.maximum(jnp.max(masked, axis=-1), self_score)
    weights = jnp.where(visible, jnp.exp(masked - peak[..., None]), 0.0)
    self_weight = jnp.exp(self_score - peak)
    denominator = jnp.sum(weights, axis=-1) + self_weight
    weights_bf = (weights / denominator[..., None]).astype(BF16)
    self_bf = (self_weight / denominator).astype(BF16)
    mixture = jnp.einsum(
        "bkgc,bkcd->bkgd", weights_bf, cached_value_rows, preferred_element_type=F32
    )
    mixture = mixture + self_bf.astype(F32)[..., None] * new_value.astype(F32)[:, :, None, :]
    attended = mixture.reshape(row_count, -1).astype(BF16)
    return (attended, new_key, new_value)


def local(
    master_qo,
    master_kv,
    moment1_qo,
    moment1_kv,
    moment2_qo,
    moment2_kv,
    grad_qo,
    grad_kv,
    hidden,
    norm_gain,
    qk_gain,
    key_cache,
    cached_value_rows,
    lengths,
):
    shards, members = lax.axis_size("fsdp"), lax.axis_size("tp")
    zones = shards // 2
    shard, member = lax.axis_index("fsdp"), lax.axis_index("tp")
    me = member.astype(jnp.int32).reshape(1)
    core = (shard & 1).astype(jnp.int32).reshape(1)
    own_rows, width = hidden.shape
    rows = master_qo.shape[1]
    slab_depth = members * rows
    heads = key_cache.shape[1]
    head_dim = key_cache.shape[3]
    group_rows = members * own_rows

    def swap_member(x, mask):
        return lax.ppermute(x, "tp", xor_perm(members, mask))

    def swap_zone(x, mask):
        return lax.ppermute(x, "fsdp", xor_perm(shards, 2 * mask))

    def swap_core(x):
        return lax.ppermute(x, "fsdp", xor_perm(shards, 1))

    local_squares = jnp.sum(grad_qo * grad_qo) + jnp.sum(grad_kv * grad_kv)
    spread = jnp.broadcast_to(local_squares, (shards * members, 1, 128))
    gathered = lax.all_to_all(spread, ("fsdp", "tp"), 0, 0)
    grand_total = jnp.sum(gathered[:, 0, 0])
    clip = jnp.minimum(1.0, clip_limit / (jnp.sqrt(grand_total) + eps_norm)).reshape(1, 1)

    normed_own = root_scale(hidden.astype(F32), norm_gain).astype(BF16)
    blocks = normed_own.reshape(own_rows, shards, slab_depth).transpose(1, 0, 2)
    mine = lax.all_to_all(blocks, "fsdp", 0, 0)
    parts = jnp.stack([mine] + [swap_member(mine, k) for k in range(1, members)])
    parts = xor_order(parts, member).transpose(1, 0, 2, 3)
    parts = xor_order(parts.reshape(shards, group_rows, slab_depth), shard)
    parts = parts.reshape(zones, 2, group_rows, slab_depth)
    x = jnp.flip(parts.transpose(1, 0, 2, 3), axis=0).reshape(2, zones * group_rows, slab_depth)

    qo = (master_qo, moment1_qo, moment2_qo, grad_qo)
    kv = (master_kv, moment1_kv, moment2_kv, grad_kv)
    fresh, received = None, []
    for head in range(heads):
        fresh, slabs = update_input_proj(head, heads, members, me, clip, qo, kv, fresh)
        received.append(
            [swap_member(slabs[n], n + 1) for n in range(members - 1)] + [slabs[members - 1]]
        )
    fresh_qo, slabs = update_output_proj(members, me, clip, qo, fresh[0::2])
    out_slabs = [swap_member(slabs[n], n + 1) for n in range(members - 1)] + [slabs[members - 1]]
    out_slabs = out_slabs + [swap_core(s) for s in out_slabs]

    summed = []
    for head in range(heads):
        send, keep = project(me, x, received[head])
        both = (keep + swap_core(send).astype(F32)).reshape(zones, group_rows, -1)
        total = both[0]
        for k in range(1, zones):
            total = total + swap_zone(both[k].astype(BF16), k).astype(F32)
        summed.append(total)
    q_width = summed[0].shape[1] - 2 * head_dim
    queries = jnp.concatenate([s[:, :q_width] for s in summed], axis=1)
    key_new = jnp.concatenate([s[:, q_width : q_width + head_dim] for s in summed], axis=1)
    value_new = jnp.concatenate([s[:, q_width + head_dim :] for s in summed], axis=1)
    attended, new_key, new_value = attend(
        queries, key_new, value_new, qk_gain, key_cache, cached_value_rows, lengths
    )

    att = [attended] + [swap_zone(attended, k) for k in range(1, zones)]
    shares = expand(me, core, att, out_slabs)
    own = shares[0]
    for k in range(1, members):
        own = own + swap_member(shares[k], k)
    own = own.reshape(zones, own_rows, 2 * slab_depth)
    pieces = jnp.stack([own[0]] + [swap_zone(own[k], k) for k in range(1, zones)])
    row_terms = xor_order(pieces, shard // 2).transpose(1, 0, 2).reshape(own_rows, width)
    new_hidden = (hidden.astype(F32) + row_terms).astype(BF16)
    return (
        fresh_qo[0],
        fresh[1],
        fresh_qo[1],
        fresh[3],
        fresh_qo[2],
        fresh[5],
        new_hidden,
        new_key,
        new_value,
    )


def solution(mesh):
    state = P(None, ("fsdp", "tp"), None)
    return jax.shard_map(
        local,
        mesh=mesh,
        in_specs=(
            state,
            state,
            state,
            state,
            state,
            state,
            state,
            state,
            P(("fsdp", "tp"), None),
            P(),
            P(),
            P("fsdp", "tp", None, None),
            P("fsdp", "tp", None, None),
            P("fsdp"),
        ),
        out_specs=(
            state,
            state,
            state,
            state,
            state,
            state,
            P(("fsdp", "tp"), None),
            P("fsdp", "tp", None),
            P("fsdp", "tp", None),
        ),
        check_vma=False,
    )
```

time: 826 us -> 234 us (0.28)
  waiting for transfers between devices: 609 us -> 60.8 us
  starting transfers between devices: 0.21 us -> 53.3 us
  blocking collectives: 52.5 us -> 0 us
  Pallas kernels: 0 us -> 46.8 us
  local copies, waits for them, and re-layouts: 66.8 us -> 23.7 us
  matrix products: 35.4 us -> 9.69 us
  between operations: 16 us -> 3.26 us
  other arithmetic: 43.9 us -> 34.8 us
    all_gather x4 -> x0, waiting for transfers between devices: 583 us -> none  [the longest x1 338 us: local(): lax.all_gather(slab_qo, 'fsdp', axis=1, tiled=True)]
    dot_general x5 -> x0, local copies, waits for them, and re-layouts: 55.4 us -> none  [the longest x2 43.6 us: local(): queries = jnp.dot(normed, full_qo[0], preferred_element_type=jnp.float32)]
    ppermute x0 -> x33, waiting for transfers between devices: none -> 53.7 us  [the longest x12 33.3 us: swap_zone(): return lax.ppermute(x, 'fsdp', xor_perm(shards, 2 * mask))]
    pallas_call x0 -> x6, Pallas kernels: none -> 46.8 us  [the longest x2 22.4 us: update_input_proj(): pl.pallas_call(functools.partial(input_proj_kernel, members, group, head_...]
    psum x1 -> x0, blocking collectives: 42 us -> none  [local(): grand_total = lax.psum(local_squares, ('fsdp', 'tp'))]
    ppermute x0 -> x33, starting transfers between devices: none -> 40.9 us  [the longest x12 22.5 us: swap_zone(): return lax.ppermute(x, 'fsdp', xor_perm(shards, 2 * mask))]
    convert_element_type x5, other arithmetic: 33.5 us -> 2.49 us  [the longest x1 1.03 us: local(): normed_own = root_scale(hidden.astype(F32), norm_gain).astype(BF16)]
    dot_general x4 -> x0, matrix products: 29.6 us -> none  [the longest x1 11.7 us: local(): lax.dot_general(attended, full_qo[1], (((1,), (1,)), ((), ())), preferred...]
  transfers between devices with their start and end apart: 5 -> 35, of which waited for: 5 -> 12; matrix products, arithmetic and copies ran while one was open for 7% -> 26% of each run, Pallas kernels for 0% -> 17%
where the time goes in v1:
time: 234 us; the launch traced here: 232 us
  waiting for transfers between devices  60.8 us (26%)
  starting transfers between devices  53.3 us (23%)
  Pallas kernels  46.8 us (20%)
  other arithmetic  34.8 us (15%)
  local copies, waits for them, and re-layouts  23.7 us (10%)
  matrix products  9.69 us (4%)
  between operations  3.26 us (1%)
    ppermute x12, waiting for transfers between devices, swap_zone(): return lax.ppermute(x, 'fsdp', xor_perm(shards, 2 * mask))  33.3 us
    ppermute x12, starting transfers between devices, swap_zone(): return lax.ppermute(x, 'fsdp', xor_perm(shards, 2 * mask))  22.5 us
    pallas_call x2, Pallas kernels, update_input_proj(): pl.pallas_call(functools.partial(input_proj_kernel, members, group, head_...  22.4 us
    ppermute x15, waiting for transfers between devices, swap_member(): return lax.ppermute(x, 'tp', xor_perm(members, mask))  19.4 us
    ppermute x15, starting transfers between devices, swap_member(): return lax.ppermute(x, 'tp', xor_perm(members, mask))  17.6 us
    pallas_call x1, Pallas kernels, update_output_proj(): pl.pallas_call(functools.partial(output_proj_kernel, members), grid_spec=...  16.1 us
    rev x7, local copies, waits for them, and re-layouts, xor_order(): swapped = jnp.flip(pairs, axis=1).reshape(blocks.shape)  10 us
    reduce_sum x2, other arithmetic, local(): local_squares = jnp.sum(grad_qo * grad_qo) + jnp.sum(grad_kv * grad_kv)  9.64 us
  transfers between devices with their start and end apart: 35, of which 12 were waited for; matrix products, arithmetic and copies ran while one was open for 26% of the time, Pallas kernels for 17%

profile of v1, /device:TPU:0, one launch (start us, length us, event | category | flops | bytes accessed | tf_op | source)
XLA Modules:
  0.0 232.3 jit_solution(6363343755019921766)
XLA Ops:
  0.6 1.1 fusion.6
  1.7 1.0 fusion.8
  3.5 6.3 %all-to-all-start.1 = ((bf16[8,16,640]{2,1,0:T(8,128)(2,1)}), bf16[8,16,640]{2,1,0:T(8,128)(2,1)}, u32[]{:S(2)}, u32[]{:S(2)}) async-start(bf16[8,16,640]{2,1,0:T(8,128)(2,1)} %copy.63), calls=%async_computation.1 | async-start | bytes 327680 | tf_op jit(solution)/shard_map/all_to_all | solution.py:389
  9.8 7.4 %multiply_reduce_fusion = f32[]{:T(128)} fusion(f32[2,160,8192]{2,1,0:T(8,128)} %refs_3_.5), kind=kLoop, calls=%fused_computation | loop fusion | flops 5242879 | bytes 10485764 | tf_op jit(solution)/shard_map/reduce_sum | solution.py:381
  17.2 1.5 collective-permute-start
  18.7 1.5 collective-permute-start.1
  20.7 2.3 multiply_reduce_fusion.1
  24.9 6.1 %all-to-all-start = ((f32[32,1,128]{2,1,0:T(1,128)}), f32[32,1,128]{2,1,0:T(1,128)S(1)}, u32[]{:S(2)}, u32[]{:S(2)}) async-start(f32[32,1,128]{2,1,0:T(1,128)} %broadcast_in_dim.16), calls=%async_computation | async-start | bytes 32768 | tf_op jit(solution)/shard_map/all_to_all | solution.py:383
  30.9 7.1 %all-to-all-done = f32[32,1,128]{2,1,0:T(1,128)S(1)} async-done(((f32[32,1,128]{2,1,0:T(1,128)}), f32[32,1,128]{2,1,0:T(1,128)S(1)}, u32[]{:S(2)}, u32[]{:S(2)}) %all-to-all-start) | async-done | bytes 16416 | tf_op jit(solution)/shard_map/all_to_all | solution.py:383
  39.4 1.3 copy-done.2
  40.7 11.4 %shard_map.205 = (f32[2,160,8192]{2,1,0:T(8,128)}, f32[2,160,1024]{2,1,0:T(8,128)}, f32[2,160,8192]{2,1,0:T(8,128)}, f32[2,160,1024]{2,1,0:T(8,128)}, f32[2,160,...) custom-call(s32[1]{0:T(128)} %bitcast.me_ref, ...), custom_call_target="tpu_custom_call" | custom-call | flops 16384000 | bytes 24576000 | tf_op jit(solution)/shard_map/pallas_call | solution.py:128
  53.4 2.3 %collective-permute-start.5 = (bf16[160,1280]{1,0:T(8,128)(2,1)S(1)}, bf16[160,1280]{1,0:T(8,128)(2,1)}, u32[]{:S(2)}, u32[]{:S(2)}) collective-permute-start(bf16[160,1280]{1,0:T(8,128)(2,1)S(1)} %get-tuple-element.61), channel_id=1, source_target_pairs={{0,3},{1,2},{2,1},{3,0},{4,7},{5,6},{6,5},{7,4},{8,11},{9,10},{10,... | collective-permute-start | bytes 1228808 | tf_op jit(solution)/shard_map/ppermute | solution.py:373
  55.7 2.1 pad_maximum_fusion
  57.8 2.0 rev.32
  59.8 2.3 %bitcast_select_fusion.1 = bf16[1,2,2,8,16,640]{5,4,2,1,3,0:T(8,128)(2,1)} fusion(bf16[1,2,2,8,16,640]{5,4,2,1,3,0:T(8,128)(2,1)} %bitcast.92, pred[]{:T(512)S(6)} %ne.37, bf16[2,2,1,8,16,640]{5,4,1,0,3,2:T(8,128)(2,1)} %bitcast.93), kind=kLoop, calls=%fused_computation.13 | loop fusion | flops 327680 | bytes 1966081 | tf_op jit(solution)/shard_map/jit(_where)/select_n | solution.py:49
  62.2 2.0 rev.33
  64.1 2.1 select_select_fusion.1
  66.3 2.0 rev.34
  68.3 2.0 broadcast_select_fusion
  70.3 2.0 rev.35
  72.3 2.0 select_select_fusion
  74.4 2.0 rev.36
  76.3 2.7 %fusion.4 = bf16[2,4,64,640]{3,2,0,1:T(8,128)(2,1)} fusion(bf16[4,2,64,640]{3,2,1,0:T(8,128)(2,1)} %bitcast.101, bf16[4,2,64,640]{3,2,1,0:T(8,128)(2,1)} %bitcast.90, bf16[2,2,2,64,640]{4,3,2,1,0:T(8,128)(2,1)} %rev.35, pred[]{:T(512)S(6)} %ne.35, pred[]{:T(512)S(6)} %ne.34, pred[]{:T(512)S(6)} %ne.33, bf16[4,2,1,64,640]{4,3,1,0,2:T(8,128)(2,1)} %bitcast.89), kind=kLoop, calls=%fused_computation.12 | loop fusion | flops 983040 | bytes 3276803 | tf_op jit(solution)/shard_map/transpose | solution.py:394
  79.0 2.0 rev.37
  81.0 1.1 copy.64
  82.2 3.0 %shard_map.208 = (bf16[256,1280]{1,0:T(8,128)(2,1)S(1)}, f32[256,1280]{1,0:T(8,128)S(1)}) custom-call(s32[1]{0:T(128)} %bitcast.me_ref, bf16[2,256,640]{2,1,0:T(8,128)(2,1)S(1)} %bitcast.84, bf16[160,1280]{1,0:T(8,128)(2,1)} %collective-permute-done.3.refs_0_, bf16[160,1280]{1,0:T(8,128)(2,1)} %collective-permute-done.4.refs_1_, ...), custom_call_target="tpu_custom_call" | custom-call | flops 838860800 | bytes 2621440 | tf_op jit(solution)/shard_map/pallas_call | solution.py:211
  85.5 11.0 %shard_map.206 = (f32[2,160,8192]{2,1,0:T(8,128)}, f32[2,160,1024]{2,1,0:T(8,128)}, f32[2,160,8192]{2,1,0:T(8,128)}, f32[2,160,1024]{2,1,0:T(8,128)}, f32[2,160,...) custom-call(s32[1]{0:T(128)} %bitcast.me_ref, ...), custom_call_target="tpu_custom_call", output_to_operand_aliasing={{0}: (10, {}), {1}: (11, {}), {2}: (12, {}), {3}: (13, {}),... | custom-call | flops 16384000 | bytes 24576000 | tf_op jit(solution)/shard_map/pallas_call | solution.py:128
  96.9 0.8 collective-permute-start.11
  97.7 2.3 collective-permute-start.12
  100.0 0.8 multiply_cosine_fusion
  100.9 16.1 %shard_map.207 = (f32[2,160,8192]{2,1,0:T(8,128)}, f32[2,160,8192]{2,1,0:T(8,128)}, f32[2,160,8192]{2,1,0:T(8,128)}, bf16[160,2048]{1,0:T(8,128)(2,1)S(1)}, bf16...) custom-call(s32[1]{0:T(128)} %bitcast.me_ref, ...), custom_call_target="tpu_custom_call", output_to_operand_aliasing={{0}: (6, {}), {1}: (7, {}), {2}: (8, {})} | custom-call | flops 26214400 | bytes 39321600 | tf_op jit(solution)/shard_map/pallas_call | solution.py:160
  117.3 0.8 collective-permute-start.21
  118.1 2.3 collective-permute-start.22
  120.4 1.8 shard_map.209
  122.6 0.8 collective-permute-start.7
  123.4 1.0 collective-permute-done.13
  125.3 9.2 %collective-permute-done.20.refs_4_ = bf16[160,2048]{1,0:T(8,128)(2,1)S(1)} collective-permute-done((bf16[160,2048]{1,0:T(8,128)(2,1)S(1)}, bf16[160,2048]{1,0:T(8,128)(2,1)S(1)}, u32[]{:S(2)}, u32[]{:S(2)}) %collective-permute-start.20) | collective-permute-done | bytes 655392 | tf_op jit(solution)/shard_map/ppermute | solution.py:373
  134.6 0.9 collective-permute-start.9
  136.0 3.1 %collective-permute-start.15 = (bf16[64,1280]{1,0:T(8,128)(2,1)S(1)}, bf16[64,1280]{1,0:T(8,128)(2,1)S(1)}, u32[]{:S(2)}, u32[]{:S(2)}) collective-permute-start(bf16[64,1280]{1,0:T(8,128)(2,1)S(1)} %get-tuple-element.90), channel_id=1, source_target_pairs={{0,16},{4,20},{8,24},{12,28},{16,0},{20,4},{24,8},{28,12},{1,17},{... | collective-permute-start | bytes 491528 | tf_op jit(solution)/shard_map/ppermute | solution.py:376
  139.1 4.5 %collective-permute-done.9 = bf16[64,1280]{1,0:T(8,128)(2,1)S(1)} collective-permute-done((bf16[64,1280]{1,0:T(8,128)(2,1)S(1)}, bf16[64,1280]{1,0:T(8,128)(2,1)S(1)}, u32[]{:S(2)}, u32[]{:S(2)}) %collective-permute-start.9) | collective-permute-done | bytes 163872 | tf_op jit(solution)/shard_map/ppermute | solution.py:376
  143.6 0.9 collective-permute-start.16
  144.7 2.6 %collective-permute-done.22.refs_6_ = bf16[160,2048]{1,0:T(8,128)(2,1)S(1)} collective-permute-done((bf16[160,2048]{1,0:T(8,128)(2,1)S(1)}, bf16[160,2048]{1,0:T(8,128)(2,1)S(1)}, u32[]{:S(2)}, u32[]{:S(2)}) %collective-permute-start.22) | collective-permute-done | bytes 655392 | tf_op jit(solution)/shard_map/ppermute | solution.py:373
  147.9 6.3 %collective-permute-done.15 = bf16[64,1280]{1,0:T(8,128)(2,1)S(1)} collective-permute-done((bf16[64,1280]{1,0:T(8,128)(2,1)S(1)}, bf16[64,1280]{1,0:T(8,128)(2,1)S(1)}, u32[]{:S(2)}, u32[]{:S(2)}) %collective-permute-start.15) | collective-permute-done | bytes 163872 | tf_op jit(solution)/shard_map/ppermute | solution.py:376
  156.4 1.5 reshape.354
  157.9 1.0 multiply_reduce_fusion.4
  158.9 1.0 maximum_bitcast_fusion
  161.9 1.0 multiply_reduce_fusion.2
  162.9 0.9 copy.67
  163.8 6.1 %fusion.30 = (f32[64,2,8]{2,1,0:T(2,128)}, f32[64,2,8,128]{3,2,1,0:T(8,128)}) fusion(bf16[64,2,128,128]{3,2,1,0:T(8,128)(2,1)} %param.25, bf16[64,2,8,64]{3,2,1,0:T(8,128)(2,1)} %copy-done.4, bf16[64,2,8,64]{3,2,1,0:T(8,128)(2,1)S(1)} %get-tuple-element.91, pred[64,128]{1,0:T(8,128)(4,1)S(1)} %iota_compare_fusion), kind=kOutput, calls=%fused_computation.84 | convolution fusion | flops 34470912 | bytes 4993024 | tf_op jit(solution)/shard_map/bkgd,bkcd->bkgc/dot_general | solution.py:322
  169.9 0.9 copy.68
  170.9 1.4 fusion.5
  174.3 3.6 %fusion.1 = bf16[64,2,8,128]{3,2,1,0:T(8,128)(2,1)S(1)} fusion(bf16[64,2,128,128]{3,2,1,0:T(8,128)(2,1)} %param.26, f32[64,2,8,128]{3,2,1,0:T(8,128)} %get-tuple-element.106, f32[64,2,128]{2,1,0:T(2,128)S(1)} %convert_element_type.115, f32[64,2,8]{2,1,0:T(2,128)S(1)} %copy.72, f32[64,2,8]{2,1,0:T(2,128)S(1)} %copy.71, f32[64,2,8]{2,1,0:T(2,128)S(1)} %copy.69, ...), kind=kOutput, calls=%fused_computation.7 | convolution fusion | flops 34471936 | bytes 5066752 | tf_op jit(solution)/shard_map/bkgc,bkcd->bkgd/dot_general | solution.py:336
  178.0 2.6 %collective-permute-start.17 = (bf16[64,2048]{1,0:T(8,128)(2,1)S(1)}, bf16[64,2048]{1,0:T(8,128)(2,1)S(1)}, u32[]{:S(2)}, u32[]{:S(2)}) collective-permute-start(bf16[64,2048]{1,0:T(8,128)(2,1)S(1)} %bitcast.80), channel_id=1, source_target_pairs={{0,8},{4,12},{8,0},{12,4},{16,24},{20,28},{24,16},{28,20},{1,9},{5... | collective-permute-start | bytes 786440 | tf_op jit(solution)/shard_map/ppermute | solution.py:376
  180.6 2.4 %collective-permute-start.19 = (bf16[64,2048]{1,0:T(8,128)(2,1)S(1)}, bf16[64,2048]{1,0:T(8,128)(2,1)S(1)}, u32[]{:S(2)}, u32[]{:S(2)}) collective-permute-start(bf16[64,2048]{1,0:T(8,128)(2,1)S(1)} %bitcast.82), channel_id=1, source_target_pairs={{0,24},{4,28},{8,16},{12,20},{16,8},{20,12},{24,0},{28,4},{1,25},{... | collective-permute-start | bytes 786440 | tf_op jit(solution)/shard_map/ppermute | solution.py:376
  183.0 8.9 %collective-permute-done.17.refs_1_ = bf16[64,2048]{1,0:T(8,128)(2,1)S(1)} collective-permute-done((bf16[64,2048]{1,0:T(8,128)(2,1)S(1)}, bf16[64,2048]{1,0:T(8,128)(2,1)S(1)}, u32[]{:S(2)}, u32[]{:S(2)}) %collective-permute-start.17) | collective-permute-done | bytes 262176 | tf_op jit(solution)/shard_map/ppermute | solution.py:376
  191.9 9.3 %collective-permute-done.18.refs_2_ = bf16[64,2048]{1,0:T(8,128)(2,1)S(1)} collective-permute-done((bf16[64,2048]{1,0:T(8,128)(2,1)S(1)}, bf16[64,2048]{1,0:T(8,128)(2,1)S(1)}, u32[]{:S(2)}, u32[]{:S(2)}) %collective-permute-start.18) | collective-permute-done | bytes 262176 | tf_op jit(solution)/shard_map/ppermute | solution.py:376
  201.2 3.5 %shard_map.210 = (f32[64,1280]{1,0:T(8,128)S(1)}, f32[64,1280]{1,0:T(8,128)S(1)}, f32[64,1280]{1,0:T(8,128)S(1)}, f32[64,1280]{1,0:T(8,128)S(1)}) custom-call(s32[1]{0:T(128)} %bitcast.me_ref, s32[1]{0:T(128)} %bitcast.2.core_ref, bf16[64,2048]{1,0:T(8,128)(2,1)S(1)} %bitcast.83, bf16[64,2048]{1,0:T(8,128)(2,1)S(1)} %collective-permute-done.17.refs_1_, ...), custom_call_target="tpu_custom_call" | custom-call | flops 1342177280 | bytes 5242880 | tf_op jit(solution)/shard_map/pallas_call | solution.py:272
  205.9 2.3 collective-permute-start.29
  208.2 3.6 %collective-permute-done.27 = f32[64,1280]{1,0:T(8,128)S(1)} collective-permute-done((f32[64,1280]{1,0:T(8,128)S(1)}, f32[64,1280]{1,0:T(8,128)S(1)}, u32[]{:S(2)}, u32[]{:S(2)}) %collective-permute-start.27) | collective-permute-done | bytes 327712 | tf_op jit(solution)/shard_map/ppermute | solution.py:373
  211.8 3.9 %collective-permute-done.28 = f32[64,1280]{1,0:T(8,128)S(1)} collective-permute-done((f32[64,1280]{1,0:T(8,128)S(1)}, f32[64,1280]{1,0:T(8,128)S(1)}, u32[]{:S(2)}, u32[]{:S(2)}) %collective-permute-start.28) | collective-permute-done | bytes 327712 | tf_op jit(solution)/shard_map/ppermute | solution.py:373
  215.8 8.1 %collective-permute-start.30 = (f32[16,1280]{1,0:T(8,128)S(1)}, f32[16,1280]{1,0:T(8,128)S(1)}, u32[]{:S(2)}, u32[]{:S(2)}) collective-permute-start(f32[16,1280]{1,0:T(8,128)S(1)} %get-tuple-element.96), channel_id=1, source_target_pairs={{0,8},{4,12},{8,0},{12,4},{16,24},{20,28},{24,16},{28,20},{1,9},{5... | collective-permute-start | bytes 245768 | tf_op jit(solution)/shard_map/ppermute | solution.py:376
  223.9 2.4 %collective-permute-start.32 = (f32[16,1280]{1,0:T(8,128)S(1)}, f32[16,1280]{1,0:T(8,128)S(1)}, u32[]{:S(2)}, u32[]{:S(2)}) collective-permute-start(f32[16,1280]{1,0:T(8,128)S(1)} %get-tuple-element.94), channel_id=1, source_target_pairs={{0,24},{4,28},{8,16},{12,20},{16,8},{20,12},{24,0},{28,4},{1,25},{... | collective-permute-start | bytes 245768 | tf_op jit(solution)/shard_map/ppermute | solution.py:376
  226.4 1.2 collective-permute-done.30
  227.6 2.9 %collective-permute-done.31 = f32[16,1280]{1,0:T(8,128)S(1)} collective-permute-done((f32[16,1280]{1,0:T(8,128)S(1)}, f32[16,1280]{1,0:T(8,128)S(1)}, u32[]{:S(2)}, u32[]{:S(2)}) %collective-permute-start.31) | collective-permute-done | bytes 81952 | tf_op jit(solution)/shard_map/ppermute | solution.py:376
  (117 shorter events, 16.2 us)
Async XLA Ops:
  3.5 13.7 %all-to-all-start.1 = ((bf16[8,16,640]{2,1,0:T(8,128)(2,1)}), bf16[8,16,640]{2,1,0:T(8,128)(2,1)}, u32[]{:S(2)}, u32[]{:S(2)}) async-start(bf16[8,16,640]{2,1,0:T(8,128)(2,1)} %copy.63), calls=%async_computation.1 | async-start | bytes 327680 | tf_op jit(solution)/shard_map/all_to_all | solution.py:389
  9.8 29.6 %copy-start.1 = (f32[2,160,1024]{2,1,0:T(8,128)S(1)}, f32[2,160,1024]{2,1,0:T(8,128)}, u32[]{:S(2)}) copy-start(f32[2,160,1024]{2,1,0:T(8,128)} %refs_3_.4) | copy-start | bytes 3932164
  17.2 22.2 %copy-start = (f32[2,160,1024]{2,1,0:T(8,128)S(1)}, f32[2,160,1024]{2,1,0:T(8,128)}, u32[]{:S(2)}) copy-start(f32[2,160,1024]{2,1,0:T(8,128)} %refs_1_.4) | copy-start | bytes 3932164
  17.2 36.2 %collective-permute-start = (bf16[8,16,640]{2,1,0:T(8,128)(2,1)}, bf16[8,16,640]{2,1,0:T(8,128)(2,1)}, u32[]{:S(2)}, u32[]{:S(2)}) collective-permute-start(bf16[8,16,640]{2,1,0:T(8,128)(2,1)} %all-to-all-done.1), channel_id=1, source_target_pairs={{0,1},{1,0},{2,3},{3,2},{4,5},{5,4},{6,7},{7,6},{8,9},{9,8},{10,11... | collective-permute-start | bytes 491528 | tf_op jit(solution)/shard_map/ppermute | solution.py:373
  18.7 37.0 %collective-permute-start.1 = (bf16[8,16,640]{2,1,0:T(8,128)(2,1)}, bf16[8,16,640]{2,1,0:T(8,128)(2,1)}, u32[]{:S(2)}, u32[]{:S(2)}) collective-permute-start(bf16[8,16,640]{2,1,0:T(8,128)(2,1)} %all-to-all-done.1), channel_id=1, source_target_pairs={{0,2},{1,3},{2,0},{3,1},{4,6},{5,7},{6,4},{7,5},{8,10},{9,11},{10,... | collective-permute-start | bytes 491528 | tf_op jit(solution)/shard_map/ppermute | solution.py:373
  20.2 35.5 %collective-permute-start.2 = (bf16[8,16,640]{2,1,0:T(8,128)(2,1)}, bf16[8,16,640]{2,1,0:T(8,128)(2,1)}, u32[]{:S(2)}, u32[]{:S(2)}) collective-permute-start(bf16[8,16,640]{2,1,0:T(8,128)(2,1)} %all-to-all-done.1), channel_id=1, source_target_pairs={{0,3},{1,2},{2,1},{3,0},{4,7},{5,6},{6,5},{7,4},{8,11},{9,10},{10,... | collective-permute-start | bytes 491528 | tf_op jit(solution)/shard_map/ppermute | solution.py:373
  24.9 13.2 %all-to-all-start = ((f32[32,1,128]{2,1,0:T(1,128)}), f32[32,1,128]{2,1,0:T(1,128)S(1)}, u32[]{:S(2)}, u32[]{:S(2)}) async-start(f32[32,1,128]{2,1,0:T(1,128)} %broadcast_in_dim.16), calls=%async_computation | async-start | bytes 32768 | tf_op jit(solution)/shard_map/all_to_all | solution.py:383
  39.4 1.3 copy-start.2
  52.1 30.0 %collective-permute-start.3 = (bf16[160,1280]{1,0:T(8,128)(2,1)}, bf16[160,1280]{1,0:T(8,128)(2,1)}, u32[]{:S(2)}, u32[]{:S(2)}) collective-permute-start(bf16[160,1280]{1,0:T(8,128)(2,1)} %get-tuple-element.59), channel_id=1, source_target_pairs={{0,1},{1,0},{2,3},{3,2},{4,5},{5,4},{6,7},{7,6},{8,9},{9,8},{10,11... | collective-permute-start | bytes 1228808 | tf_op jit(solution)/shard_map/ppermute | solution.py:373
  52.7 29.5 %collective-permute-start.4 = (bf16[160,1280]{1,0:T(8,128)(2,1)}, bf16[160,1280]{1,0:T(8,128)(2,1)}, u32[]{:S(2)}, u32[]{:S(2)}) collective-permute-start(bf16[160,1280]{1,0:T(8,128)(2,1)} %get-tuple-element.60), channel_id=1, source_target_pairs={{0,2},{1,3},{2,0},{3,1},{4,6},{5,7},{6,4},{7,5},{8,10},{9,11},{10,... | collective-permute-start | bytes 1228808 | tf_op jit(solution)/shard_map/ppermute | solution.py:373
  53.4 28.8 %collective-permute-start.5 = (bf16[160,1280]{1,0:T(8,128)(2,1)S(1)}, bf16[160,1280]{1,0:T(8,128)(2,1)}, u32[]{:S(2)}, u32[]{:S(2)}) collective-permute-start(bf16[160,1280]{1,0:T(8,128)(2,1)S(1)} %get-tuple-element.61), channel_id=1, source_target_pairs={{0,3},{1,2},{2,1},{3,0},{4,7},{5,6},{6,5},{7,4},{8,11},{9,10},{10,... | collective-permute-start | bytes 1228808 | tf_op jit(solution)/shard_map/ppermute | solution.py:373
  82.2 3.1 %copy-start.13 = (s32[64]{0:T(128)S(1)}, s32[64]{0:T(128)}, u32[]{:S(2)}) copy-start(s32[64]{0:T(128)} %param.27) | copy-start | bytes 772
  82.2 3.2 %copy-start.3 = (f32[2,160,1024]{2,1,0:T(8,128)S(1)}, f32[2,160,1024]{2,1,0:T(8,128)}, u32[]{:S(2)}) copy-start(f32[2,160,1024]{2,1,0:T(8,128)} %refs_5_.3) | copy-start | bytes 3932164
  85.3 37.1 %collective-permute-start.6 = (bf16[256,1280]{1,0:T(8,128)(2,1)S(1)}, bf16[256,1280]{1,0:T(8,128)(2,1)S(1)}, u32[]{:S(2)}, u32[]{:S(2)}) collective-permute-start(bf16[256,1280]{1,0:T(8,128)(2,1)S(1)} %get-tuple-element.64), channel_id=1, source_target_pairs={{0,4},{4,0},{8,12},{12,8},{16,20},{20,16},{24,28},{28,24},{1,5},{5... | collective-permute-start | bytes 1966088 | tf_op jit(solution)/shard_map/ppermute | solution.py:379
  85.5 14.6 %copy-start.12 = (f32[2,128]{1,0:T(2,128)S(1)}, f32[2,128]{1,0:T(2,128)}, u32[]{:S(2)}) copy-start(f32[2,128]{1,0:T(2,128)} %param.24) | copy-start | bytes 3076
  96.5 20.8 %collective-permute-start.10 = (bf16[160,1280]{1,0:T(8,128)(2,1)S(1)}, bf16[160,1280]{1,0:T(8,128)(2,1)S(1)}, u32[]{:S(2)}, u32[]{:S(2)}) collective-permute-start(bf16[160,1280]{1,0:T(8,128)(2,1)S(1)} %get-tuple-element.65), channel_id=1, source_target_pairs={{0,1},{1,0},{2,3},{3,2},{4,5},{5,4},{6,7},{7,6},{8,9},{9,8},{10,11... | collective-permute-start | bytes 1228808 | tf_op jit(solution)/shard_map/ppermute | solution.py:373
  96.9 21.2 %collective-permute-start.11 = (bf16[160,1280]{1,0:T(8,128)(2,1)S(1)}, bf16[160,1280]{1,0:T(8,128)(2,1)S(1)}, u32[]{:S(2)}, u32[]{:S(2)}) collective-permute-start(bf16[160,1280]{1,0:T(8,128)(2,1)S(1)} %get-tuple-element.66), channel_id=1, source_target_pairs={{0,2},{1,3},{2,0},{3,1},{4,6},{5,7},{6,4},{7,5},{8,10},{9,11},{10,... | collective-permute-start | bytes 1228808 | tf_op jit(solution)/shard_map/ppermute | solution.py:373
  97.7 22.7 %collective-permute-start.12 = (bf16[160,1280]{1,0:T(8,128)(2,1)S(1)}, bf16[160,1280]{1,0:T(8,128)(2,1)S(1)}, u32[]{:S(2)}, u32[]{:S(2)}) collective-permute-start(bf16[160,1280]{1,0:T(8,128)(2,1)S(1)} %get-tuple-element.67), channel_id=1, source_target_pairs={{0,3},{1,2},{2,1},{3,0},{4,7},{5,6},{6,5},{7,4},{8,11},{9,10},{10,... | collective-permute-start | bytes 1228808 | tf_op jit(solution)/shard_map/ppermute | solution.py:373
  116.9 17.6 %collective-permute-start.20 = (bf16[160,2048]{1,0:T(8,128)(2,1)S(1)}, bf16[160,2048]{1,0:T(8,128)(2,1)S(1)}, u32[]{:S(2)}, u32[]{:S(2)}) collective-permute-start(bf16[160,2048]{1,0:T(8,128)(2,1)S(1)} %get-tuple-element.71), channel_id=1, source_target_pairs={{0,1},{1,0},{2,3},{3,2},{4,5},{5,4},{6,7},{7,6},{8,9},{9,8},{10,11... | collective-permute-start | bytes 1966088 | tf_op jit(solution)/shard_map/ppermute | solution.py:373
  117.3 27.3 %collective-permute-start.21 = (bf16[160,2048]{1,0:T(8,128)(2,1)S(1)}, bf16[160,2048]{1,0:T(8,128)(2,1)S(1)}, u32[]{:S(2)}, u32[]{:S(2)}) collective-permute-start(bf16[160,2048]{1,0:T(8,128)(2,1)S(1)} %get-tuple-element.72), channel_id=1, source_target_pairs={{0,2},{1,3},{2,0},{3,1},{4,6},{5,7},{6,4},{7,5},{8,10},{9,11},{10,... | collective-permute-start | bytes 1966088 | tf_op jit(solution)/shard_map/ppermute | solution.py:373
  118.1 29.2 %collective-permute-start.22 = (bf16[160,2048]{1,0:T(8,128)(2,1)S(1)}, bf16[160,2048]{1,0:T(8,128)(2,1)S(1)}, u32[]{:S(2)}, u32[]{:S(2)}) collective-permute-start(bf16[160,2048]{1,0:T(8,128)(2,1)S(1)} %get-tuple-element.73), channel_id=1, source_target_pairs={{0,3},{1,2},{2,1},{3,0},{4,7},{5,6},{6,5},{7,4},{8,11},{9,10},{10,... | collective-permute-start | bytes 1966088 | tf_op jit(solution)/shard_map/ppermute | solution.py:373
  122.3 2.2 collective-permute-start.13
  122.6 13.0 %collective-permute-start.7 = (bf16[64,1280]{1,0:T(8,128)(2,1)S(1)}, bf16[64,1280]{1,0:T(8,128)(2,1)S(1)}, u32[]{:S(2)}, u32[]{:S(2)}) collective-permute-start(bf16[64,1280]{1,0:T(8,128)(2,1)S(1)} %get-tuple-element.85), channel_id=1, source_target_pairs={{0,8},{4,12},{8,0},{12,4},{16,24},{20,28},{24,16},{28,20},{1,9},{5... | collective-permute-start | bytes 491528 | tf_op jit(solution)/shard_map/ppermute | solution.py:376
  124.4 11.6 %collective-permute-start.8 = (bf16[64,1280]{1,0:T(8,128)(2,1)S(1)}, bf16[64,1280]{1,0:T(8,128)(2,1)S(1)}, u32[]{:S(2)}, u32[]{:S(2)}) collective-permute-start(bf16[64,1280]{1,0:T(8,128)(2,1)S(1)} %get-tuple-element.87), channel_id=1, source_target_pairs={{0,16},{4,20},{8,24},{12,28},{16,0},{20,4},{24,8},{28,12},{1,17},{... | collective-permute-start | bytes 491528 | tf_op jit(solution)/shard_map/ppermute | solution.py:376
  134.6 9.0 %collective-permute-start.9 = (bf16[64,1280]{1,0:T(8,128)(2,1)S(1)}, bf16[64,1280]{1,0:T(8,128)(2,1)S(1)}, u32[]{:S(2)}, u32[]{:S(2)}) collective-permute-start(bf16[64,1280]{1,0:T(8,128)(2,1)S(1)} %get-tuple-element.86), channel_id=1, source_target_pairs={{0,24},{4,28},{8,16},{12,20},{16,8},{20,12},{24,0},{28,4},{1,25},{... | collective-permute-start | bytes 491528 | tf_op jit(solution)/shard_map/ppermute | solution.py:376
  135.5 11.8 %collective-permute-start.14 = (bf16[64,1280]{1,0:T(8,128)(2,1)S(1)}, bf16[64,1280]{1,0:T(8,128)(2,1)S(1)}, u32[]{:S(2)}, u32[]{:S(2)}) collective-permute-start(bf16[64,1280]{1,0:T(8,128)(2,1)S(1)} %get-tuple-element.88), channel_id=1, source_target_pairs={{0,8},{4,12},{8,0},{12,4},{16,24},{20,28},{24,16},{28,20},{1,9},{5... | collective-permute-start | bytes 491528 | tf_op jit(solution)/shard_map/ppermute | solution.py:376
  136.0 18.2 %collective-permute-start.15 = (bf16[64,1280]{1,0:T(8,128)(2,1)S(1)}, bf16[64,1280]{1,0:T(8,128)(2,1)S(1)}, u32[]{:S(2)}, u32[]{:S(2)}) collective-permute-start(bf16[64,1280]{1,0:T(8,128)(2,1)S(1)} %get-tuple-element.90), channel_id=1, source_target_pairs={{0,16},{4,20},{8,24},{12,28},{16,0},{20,4},{24,8},{28,12},{1,17},{... | collective-permute-start | bytes 491528 | tf_op jit(solution)/shard_map/ppermute | solution.py:376
  143.6 10.6 %collective-permute-start.16 = (bf16[64,1280]{1,0:T(8,128)(2,1)S(1)}, bf16[64,1280]{1,0:T(8,128)(2,1)S(1)}, u32[]{:S(2)}, u32[]{:S(2)}) collective-permute-start(bf16[64,1280]{1,0:T(8,128)(2,1)S(1)} %get-tuple-element.89), channel_id=1, source_target_pairs={{0,24},{4,28},{8,16},{12,20},{16,8},{20,12},{24,0},{28,4},{1,25},{... | collective-permute-start | bytes 491528 | tf_op jit(solution)/shard_map/ppermute | solution.py:376
  144.6 9.7 %copy-start.6 = (f32[64,1280]{1,0:T(8,128)}, f32[64,1280]{1,0:T(8,128)S(1)}, u32[]{:S(2)}) copy-start(f32[64,1280]{1,0:T(8,128)S(1)} %fusion.13) | copy-start | bytes 983044
  144.7 35.9 %collective-permute-start.26 = (bf16[160,2048]{1,0:T(8,128)(2,1)S(1)}, bf16[160,2048]{1,0:T(8,128)(2,1)}, u32[]{:S(2)}, u32[]{:S(2)}) collective-permute-start(bf16[160,2048]{1,0:T(8,128)(2,1)S(1)} %get-tuple-element.74.refs_7_), channel_id=1, source_target_pairs={{0,4},{4,0},{8,12},{12,8},{16,20},{20,16},{24,28},{28,24},{1,5},{5... | collective-permute-start | bytes 1966088 | tf_op jit(solution)/shard_map/ppermute | solution.py:379
  147.4 33.2 %collective-permute-start.23 = (bf16[160,2048]{1,0:T(8,128)(2,1)S(1)}, bf16[160,2048]{1,0:T(8,128)(2,1)S(1)}, u32[]{:S(2)}, u32[]{:S(2)}) collective-permute-start(bf16[160,2048]{1,0:T(8,128)(2,1)S(1)} %collective-permute-done.20.refs_4_), channel_id=1, source_target_pairs={{0,4},{4,0},{8,12},{12,8},{16,20},{20,16},{24,28},{28,24},{1,5},{5... | collective-permute-start | bytes 1966088 | tf_op jit(solution)/shard_map/ppermute | solution.py:379
  147.4 35.6 %collective-permute-start.24 = (bf16[160,2048]{1,0:T(8,128)(2,1)S(1)}, bf16[160,2048]{1,0:T(8,128)(2,1)}, u32[]{:S(2)}, u32[]{:S(2)}) collective-permute-start(bf16[160,2048]{1,0:T(8,128)(2,1)S(1)} %collective-permute-done.21.refs_5_), channel_id=1, source_target_pairs={{0,4},{4,0},{8,12},{12,8},{16,20},{20,16},{24,28},{28,24},{1,5},{5... | collective-permute-start | bytes 1966088 | tf_op jit(solution)/shard_map/ppermute | solution.py:379
  154.2 28.8 %collective-permute-start.25 = (bf16[160,2048]{1,0:T(8,128)(2,1)S(1)}, bf16[160,2048]{1,0:T(8,128)(2,1)}, u32[]{:S(2)}, u32[]{:S(2)}) collective-permute-start(bf16[160,2048]{1,0:T(8,128)(2,1)S(1)} %collective-permute-done.22.refs_6_), channel_id=1, source_target_pairs={{0,4},{4,0},{8,12},{12,8},{16,20},{20,16},{24,28},{28,24},{1,5},{5... | collective-permute-start | bytes 1966088 | tf_op jit(solution)/shard_map/ppermute | solution.py:379
  154.3 0.7 copy-start.7
  158.9 1.4 copy-start.8
  159.9 0.8 copy-start.9
  159.9 0.8 copy-start.10
  161.1 0.7 copy-start.4
  174.2 3.7 %copy-start.11 = (bf16[64,2,128]{2,1,0:T(2,128)(2,1)}, bf16[64,2,128]{2,1,0:T(2,128)(2,1)S(1)}, u32[]{:S(2)}) copy-start(bf16[64,2,128]{2,1,0:T(2,128)(2,1)S(1)} %convert_element_type.114) | copy-start | bytes 98308
  178.0 13.9 %collective-permute-start.17 = (bf16[64,2048]{1,0:T(8,128)(2,1)S(1)}, bf16[64,2048]{1,0:T(8,128)(2,1)S(1)}, u32[]{:S(2)}, u32[]{:S(2)}) collective-permute-start(bf16[64,2048]{1,0:T(8,128)(2,1)S(1)} %bitcast.80), channel_id=1, source_target_pairs={{0,8},{4,12},{8,0},{12,4},{16,24},{20,28},{24,16},{28,20},{1,9},{5... | collective-permute-start | bytes 786440 | tf_op jit(solution)/shard_map/ppermute | solution.py:376
  180.5 20.7 %collective-permute-start.18 = (bf16[64,2048]{1,0:T(8,128)(2,1)S(1)}, bf16[64,2048]{1,0:T(8,128)(2,1)S(1)}, u32[]{:S(2)}, u32[]{:S(2)}) collective-permute-start(bf16[64,2048]{1,0:T(8,128)(2,1)S(1)} %bitcast.81), channel_id=1, source_target_pairs={{0,16},{4,20},{8,24},{12,28},{16,0},{20,4},{24,8},{28,12},{1,17},{... | collective-permute-start | bytes 786440 | tf_op jit(solution)/shard_map/ppermute | solution.py:376
  180.6 20.7 %collective-permute-start.19 = (bf16[64,2048]{1,0:T(8,128)(2,1)S(1)}, bf16[64,2048]{1,0:T(8,128)(2,1)S(1)}, u32[]{:S(2)}, u32[]{:S(2)}) collective-permute-start(bf16[64,2048]{1,0:T(8,128)(2,1)S(1)} %bitcast.82), channel_id=1, source_target_pairs={{0,24},{4,28},{8,16},{12,20},{16,8},{20,12},{24,0},{28,4},{1,25},{... | collective-permute-start | bytes 786440 | tf_op jit(solution)/shard_map/ppermute | solution.py:376
  204.7 7.1 %collective-permute-start.27 = (f32[64,1280]{1,0:T(8,128)S(1)}, f32[64,1280]{1,0:T(8,128)S(1)}, u32[]{:S(2)}, u32[]{:S(2)}) collective-permute-start(f32[64,1280]{1,0:T(8,128)S(1)} %get-tuple-element.76), channel_id=1, source_target_pairs={{0,1},{1,0},{2,3},{3,2},{4,5},{5,4},{6,7},{7,6},{8,9},{9,8},{10,11... | collective-permute-start | bytes 983048 | tf_op jit(solution)/shard_map/ppermute | solution.py:373
  205.1 10.6 %collective-permute-start.28 = (f32[64,1280]{1,0:T(8,128)S(1)}, f32[64,1280]{1,0:T(8,128)S(1)}, u32[]{:S(2)}, u32[]{:S(2)}) collective-permute-start(f32[64,1280]{1,0:T(8,128)S(1)} %get-tuple-element.77), channel_id=1, source_target_pairs={{0,2},{1,3},{2,0},{3,1},{4,6},{5,7},{6,4},{7,5},{8,10},{9,11},{10,... | collective-permute-start | bytes 983048 | tf_op jit(solution)/shard_map/ppermute | solution.py:373
  205.9 9.8 %collective-permute-start.29 = (f32[64,1280]{1,0:T(8,128)S(1)}, f32[64,1280]{1,0:T(8,128)S(1)}, u32[]{:S(2)}, u32[]{:S(2)}) collective-permute-start(f32[64,1280]{1,0:T(8,128)S(1)} %get-tuple-element.78), channel_id=1, source_target_pairs={{0,3},{1,2},{2,1},{3,0},{4,7},{5,6},{6,5},{7,4},{8,11},{9,10},{10,... | collective-permute-start | bytes 983048 | tf_op jit(solution)/shard_map/ppermute | solution.py:373
  215.8 11.8 %collective-permute-start.30 = (f32[16,1280]{1,0:T(8,128)S(1)}, f32[16,1280]{1,0:T(8,128)S(1)}, u32[]{:S(2)}, u32[]{:S(2)}) collective-permute-start(f32[16,1280]{1,0:T(8,128)S(1)} %get-tuple-element.96), channel_id=1, source_target_pairs={{0,8},{4,12},{8,0},{12,4},{16,24},{20,28},{24,16},{28,20},{1,9},{5... | collective-permute-start | bytes 245768 | tf_op jit(solution)/shard_map/ppermute | solution.py:376
  223.9 6.6 %collective-permute-start.31 = (f32[16,1280]{1,0:T(8,128)S(1)}, f32[16,1280]{1,0:T(8,128)S(1)}, u32[]{:S(2)}, u32[]{:S(2)}) collective-permute-start(f32[16,1280]{1,0:T(8,128)S(1)} %get-tuple-element.95), channel_id=1, source_target_pairs={{0,16},{4,20},{8,24},{12,28},{16,0},{20,4},{24,8},{28,12},{1,17},{... | collective-permute-start | bytes 245768 | tf_op jit(solution)/shard_map/ppermute | solution.py:376
  223.9 6.6 %collective-permute-start.32 = (f32[16,1280]{1,0:T(8,128)S(1)}, f32[16,1280]{1,0:T(8,128)S(1)}, u32[]{:S(2)}, u32[]{:S(2)}) collective-permute-start(f32[16,1280]{1,0:T(8,128)S(1)} %get-tuple-element.94), channel_id=1, source_target_pairs={{0,24},{4,28},{8,16},{12,20},{16,8},{20,12},{24,0},{28,4},{1,25},{... | collective-permute-start | bytes 245768 | tf_op jit(solution)/shard_map/ppermute | solution.py:376
  230.7 0.9 copy-start.5

commit v2 on v0

v2 whole, which is shorter than its diff:
```python
import functools
import math

import jax
import jax.numpy as jnp
from jax import lax
from jax.experimental import pallas as pl
from jax.experimental.pallas import tpu as pltpu
from jax.sharding import PartitionSpec as P

clip_limit = 1.0
beta_one = 0.9
beta_two = 0.95
learn_rate = 0.01
decay_rate = 0.1
adam_step = 10.0
eps_adam = 1e-08
eps_norm = 1e-06
rope_base = 1000000.0
kernel_vmem = 24 * 1024 * 1024
wide_vmem = 32 * 1024 * 1024

F32 = jnp.float32
BF16 = jnp.bfloat16
ANY = pl.BlockSpec(memory_space=pl.ANY)
small_cost = pl.CostEstimate(flops=1024, bytes_accessed=1024, transcendentals=0)


def adam_math(master, moment_one, moment_two, gradient, clip_factor):
    clipped = gradient * clip_factor
    moment_one = beta_one * moment_one + (1.0 - beta_one) * clipped
    moment_two = beta_two * moment_two + (1.0 - beta_two) * clipped * clipped
    fix_one = 1.0 - beta_one**adam_step
    fix_two = 1.0 - beta_two**adam_step
    root = jnp.sqrt(moment_two * (1.0 / fix_two)) + eps_adam
    step_size = moment_one * (1.0 / fix_one) / root
    master = master - learn_rate * (step_size + decay_rate * master)
    return (master, moment_one, moment_two)


def in_hbm(x):
    return pltpu.with_memory_space_constraint(x, pltpu.HBM)


def xor_perm(count, mask):
    return [(i, i ^ mask) for i in range(count)]


def xor_order(blocks, mask):
    count = blocks.shape[0]
    bit = 1
    while bit < count:
        pairs = blocks.reshape((count // (2 * bit), 2, bit) + blocks.shape[1:])
        swapped = jnp.flip(pairs, axis=1).reshape(blocks.shape)
        blocks = jnp.where((mask & bit) != 0, swapped, blocks)
        bit *= 2
    return blocks


def clip_of(squares):
    total = jnp.sum(squares[:, 0, :], axis=0, keepdims=True)[:, :1]
    return jnp.minimum(1.0, clip_limit / (jnp.sqrt(total) + eps_norm))


def squares_kernel(qo_ref, kv_ref, out_ref, total):
    def folded(block):
        block = (block * block).reshape(-1, 8, block.shape[-1]).sum(0)
        lanes = total.shape[-1]
        return sum(block[:, n : n + lanes] for n in range(0, block.shape[-1], lanes))

    @pl.when(pl.program_id(0) == 0)
    def _():
        total[...] = folded(kv_ref[0]) + folded(kv_ref[1])

    total[...] += folded(qo_ref[0])

    @pl.when(pl.program_id(0) == pl.num_programs(0) - 1)
    def _():
        out_ref[...] = jnp.broadcast_to(jnp.sum(total[...]), out_ref.shape)


def local_squares(count, grad_qo, grad_kv):
    halves, rows, width = grad_qo.shape
    lanes = 1024 if width % 1024 == 0 and grad_kv.shape[2] % 1024 == 0 else 128
    return pl.pallas_call(
        squares_kernel,
        name="grad_squares",
        grid=(halves,),
        in_specs=[
            pl.BlockSpec((1, rows, width), lambda i: (i, 0, 0)),
            pl.BlockSpec(grad_kv.shape, lambda i: (0, 0, 0)),
        ],
        out_specs=pl.BlockSpec((count, 1, 128), lambda i: (0, 0, 0)),
        out_shape=jax.ShapeDtypeStruct((count, 1, 128), F32),
        scratch_shapes=[pltpu.VMEM((8, lanes), F32)],
        compiler_params=pltpu.CompilerParams(vmem_limit_bytes=kernel_vmem),
        cost_estimate=small_cost,
    )(grad_qo, grad_kv)


def norm_kernel(shards, members, hidden_ref, gain_ref, out_ref):
    values = hidden_ref[...].astype(F32)
    mean_square = jnp.mean(values * values, axis=-1, keepdims=True)
    normed = (values * lax.rsqrt(mean_square + eps_norm) * gain_ref[...]).astype(BF16)
    depth = values.shape[1] // shards
    for shard in range(shards):
        for member in range(members):
            out_ref[shard * members + member] = normed[:, shard * depth : (shard + 1) * depth]


def norm_blocks(shards, members, hidden, gain):
    rows, width = hidden.shape
    return pl.pallas_call(
        functools.partial(norm_kernel, shards, members),
        name="norm_rows",
        out_shape=jax.ShapeDtypeStruct((shards * members, rows, width // shards), BF16),
        compiler_params=pltpu.CompilerParams(vmem_limit_bytes=kernel_vmem // 2),
        cost_estimate=small_cost,
    )(hidden, gain.reshape(1, width))


def tie_kernel(*refs):
    pass


def tie(x, *deps):
    return pl.pallas_call(
        tie_kernel,
        name="tie",
        in_specs=[ANY] * (1 + len(deps)),
        out_specs=ANY,
        out_shape=pltpu.HBM(x.shape, x.dtype),
        input_output_aliases={0: 0},
        compiler_params=pltpu.CompilerParams(has_side_effects=True),
        cost_estimate=small_cost,
    )(x, *deps)


def input_proj_kernel(stacked, count, group, head_dim, me_ref, squares_ref, *refs):
    ins, outs, slabs = refs[:8], refs[-6 - count : -count], refs[-count:]
    clip = clip_of(squares_ref)
    fresh_q = adam_math(ins[0][0], ins[2][0], ins[4][0], ins[6][0], clip)
    fresh_k = adam_math(ins[1][0], ins[3][0], ins[5][0], ins[7][0], clip)
    fresh_v = adam_math(ins[1][1], ins[3][1], ins[5][1], ins[7][1], clip)
    for n in range(3):
        outs[2 * n][0] = fresh_q[n]
        outs[2 * n + 1][0] = fresh_k[n]
        outs[2 * n + 1][1] = fresh_v[n]

    def fill(slab):
        slab[:, :group] = fresh_q[0].astype(BF16)
        slab[:, group : group + head_dim] = fresh_k[0].astype(BF16)
        slab[:, group + head_dim :] = fresh_v[0].astype(BF16)

    if stacked:
        fill(slabs[0].at[0])
        return
    for place in range(count):

        @pl.when(pl.program_id(0) == place)
        def _(place=place):
            fill(slabs[place])


def update_input_proj(head, heads, members, first, count, me, squares, qo, kv, earlier):
    rows = qo[0].shape[1]
    kv_total = heads * members
    group = qo[0].shape[2] // kv_total
    head_dim = kv[0].shape[2] // kv_total
    width = group + 2 * head_dim

    def column(i, me_ref):
        member = i if first is None else me_ref[0] ^ ((first + i) % members)
        return member * heads + head

    qo_spec = pl.BlockSpec((1, rows, group), lambda i, m: (0, 0, column(i, m)))
    kv_spec = pl.BlockSpec((2, rows, head_dim), lambda i, m: (0, 0, column(i, m)))
    earlier = [] if earlier is None else list(earlier)
    ins = [x for pair in zip(qo, kv) for x in pair]
    if first is None:
        slabs = [pltpu.HBM((members, rows, width), BF16)]
        slab_specs = [pl.BlockSpec((1, rows, width), lambda i, m: (i, 0, 0))]
    else:
        slabs = [pltpu.HBM((rows, width), BF16)] * count
        slab_specs = [pl.BlockSpec((rows, width), lambda i, m: (0, 0))] * count
    results = pl.pallas_call(
        functools.partial(input_proj_kernel, first is None, len(slabs), group, head_dim),
        name="adam_in",
        grid_spec=pltpu.PrefetchScalarGridSpec(
            num_scalar_prefetch=1,
            grid=(count,),
            in_specs=[pl.BlockSpec(squares.shape, lambda i, m: (0, 0, 0))]
            + [qo_spec, kv_spec] * 4
            + [ANY] * len(earlier),
            out_specs=[qo_spec, kv_spec] * 3 + slab_specs,
        ),
        out_shape=[pltpu.HBM(x.shape, F32) for x in ins[:6]] + slabs,
        input_output_aliases={10 + n: n for n in range(len(earlier))},
        compiler_params=pltpu.CompilerParams(vmem_limit_bytes=wide_vmem),
        cost_estimate=small_cost,
    )(me, squares, *ins, *earlier)
    return results[:6], results[6:]


def output_proj_kernel(squares_ref, *refs):
    ins, (*outs, slab) = refs[:4], refs[-4:]
    clip = clip_of(squares_ref)
    fresh = adam_math(ins[0][0], ins[1][0], ins[2][0], ins[3][0], clip)
    for n in range(3):
        outs[n][0] = fresh[n]
    width = slab.shape[2]
    for member in range(slab.shape[0]):
        slab[member] = fresh[0][:, member * width : (member + 1) * width].astype(BF16)


def update_output_proj(members, squares, qo, earlier, deps):
    rows = qo[0].shape[1]
    width = qo[0].shape[2] // members
    half = members // 2
    untouched = list(earlier) + list(deps)
    spec = pl.BlockSpec((1, rows, half * width), lambda i: (1, 0, i))
    return pl.pallas_call(
        output_proj_kernel,
        name="adam_out",
        grid=(2,),
        in_specs=[pl.BlockSpec(squares.shape, lambda i: (0, 0, 0))]
        + [spec] * 4
        + [ANY] * len(untouched),
        out_specs=[spec] * 3 + [pl.BlockSpec((half, rows, width), lambda i: (i, 0, 0))],
        out_shape=[pltpu.HBM(x.shape, F32) for x in qo[:3]]
        + [pltpu.HBM((members, rows, width), BF16)],
        input_output_aliases={5 + n: n for n in range(len(earlier))},
        compiler_params=pltpu.CompilerParams(vmem_limit_bytes=2 * wide_vmem - kernel_vmem // 6),
        cost_estimate=small_cost,
    )(squares, *qo, *untouched)


def project_kernel(count, me_ref, shard_ref, x_ref, *refs):
    slabs, (send_ref, keep_ref, mine, other, *scratch) = refs[:count], refs[count:]
    weight = slabs[0]
    if count > 1:
        weight = scratch[0]
        rows = slabs[0].shape[0]
        for place in range(count):
            start = pl.multiple_of((me_ref[0] ^ place) * rows, rows)
            weight[pl.ds(start, rows), :] = slabs[place][...]
    shards, group_rows, _ = x_ref.shape
    for mask in range(shards):
        into = other if mask % 2 else mine
        start = mask // 2 * group_rows
        into[start : start + group_rows, :] = x_ref[shard_ref[0] ^ mask]
    send_ref[...] = jnp.dot(other[...], weight[...], preferred_element_type=F32).astype(BF16)
    keep_ref[...] = jnp.dot(mine[...], weight[...], preferred_element_type=F32)


def project(me, shard, x, slabs, deps):
    shards, group_rows, depth = x.shape
    rows, width = slabs[0].shape
    half = shards // 2 * group_rows
    if rows % 16 and len(slabs) > 1:
        slabs = [xor_order(jnp.stack(slabs), me[0]).reshape(depth, width)]
    count = len(slabs)
    vmem = pl.BlockSpec(memory_space=pltpu.VMEM)
    smem = pl.BlockSpec(memory_space=pltpu.SMEM)

    def body(me_ref, shard_ref, x_ref, *refs):
        project_kernel(count, me_ref, shard_ref, x_ref, *refs[:count], *refs[count + len(deps) :])

    scratch = [pltpu.VMEM((half, depth), BF16)] * 2
    if count > 1:
        scratch.append(pltpu.VMEM((depth, width), BF16))
    return pl.pallas_call(
        body,
        name="project",
        in_specs=[smem, smem] + [vmem] * (1 + count) + [ANY] * len(deps),
        out_specs=[vmem, vmem],
        scratch_shapes=scratch,
        out_shape=[pltpu.HBM((half, width), BF16), pltpu.HBM((half, width), F32)],
        compiler_params=pltpu.CompilerParams(vmem_limit_bytes=kernel_vmem),
        cost_estimate=small_cost,
    )(me, shard, x, *slabs, *deps)


def core_sum_kernel(zones, keep_ref, arrived_ref, *refs):
    own_ref, sends = refs[-zones], refs[len(refs) - zones + 1 :]
    rows = own_ref.shape[0]
    for zone in range(zones):
        span = pl.ds(zone * rows, rows)
        total = keep_ref[span, :] + arrived_ref[span, :].astype(F32)
        if zone == 0:
            own_ref[...] = total
        else:
            sends[zone - 1][...] = total.astype(BF16)


def core_sum(zones, keep, arrived, deps):
    rows, width = keep.shape[0] // zones, keep.shape[1]
    vmem = pl.BlockSpec(memory_space=pltpu.VMEM)
    return pl.pallas_call(
        functools.partial(core_sum_kernel, zones),
        name="core_sum",
        in_specs=[vmem, vmem] + [ANY] * len(deps),
        out_specs=[vmem] * zones,
        out_shape=[pltpu.HBM((rows, width), F32)]
        + [jax.ShapeDtypeStruct((rows, width), BF16)] * (zones - 1),
        compiler_params=pltpu.CompilerParams(vmem_limit_bytes=kernel_vmem),
        cost_estimate=small_cost,
    )(in_hbm(keep), arrived, *deps)


def attend_kernel(zones, *refs):
    lens_ref, cos_ref, sin_ref, gain_ref, key_ref, value_ref = refs[:6]
    parts = refs[6 : 6 + zones]
    out_ref, new_key_ref, new_value_ref, query, mixed = refs[-5:]
    head_dim = new_key_ref.shape[1]
    groups = query.shape[1]
    total = parts[0][...]
    for part in parts[1:]:
        total = total + part[...].astype(F32)
    cosine, sine = cos_ref[...], sin_ref[...]

    def placed(values, gain):
        mean_square = jnp.mean(values * values, axis=-1, keepdims=True)
        values = values * lax.rsqrt(mean_square + eps_norm) * gain
        return values * cosine + pltpu.roll(values, head_dim // 2, 1) * sine

    for group in range(groups):
        columns = total[:, group * head_dim : (group + 1) * head_dim]
        query[:, group, :] = placed(columns, gain_ref[0:1, :])
    new_key = placed(total[:, groups * head_dim : (groups + 1) * head_dim], gain_ref[1:2, :])
    new_key = new_key.astype(BF16)
    new_value = total[:, (groups + 1) * head_dim :].astype(BF16)
    new_key_ref[...] = new_key
    new_value_ref[...] = new_value
    inv_root = 1.0 / math.sqrt(head_dim)
    rotated = query[...].astype(BF16)
    scores = inv_root * lax.dot_general(
        rotated, key_ref[:, 0], (((2,), (2,)), ((0,), (0,))), preferred_element_type=F32
    )
    own_score = inv_root * jnp.sum(
        rotated.astype(F32) * new_key.astype(F32)[:, None, :], axis=-1, keepdims=True
    )
    slots = lax.broadcasted_iota(jnp.int32, scores.shape, 2)
    visible = slots < lens_ref[...][:, None, :]
    masked = jnp.where(visible, scores, -1e30)
    peak = jnp.maximum(jnp.max(masked, axis=-1, keepdims=True), own_score)
    weights = jnp.where(visible, jnp.exp(masked - peak), 0.0)
    own_weight = jnp.exp(own_score - peak)
    inverse = 1.0 / (jnp.sum(weights, axis=-1, keepdims=True) + own_weight)
    own_part = (own_weight * inverse).astype(BF16).astype(F32)
    mixed[...] = (
        lax.dot_general(
            (weights * inverse).astype(BF16),
            value_ref[:, 0],
            (((2,), (1,)), ((0,), (0,))),
            preferred_element_type=F32,
        )
        + own_part * new_value.astype(F32)[:, None, :]
    )
    for group in range(groups):
        out_ref[:, group * head_dim : (group + 1) * head_dim] = mixed[:, group, :].astype(BF16)


def attend(head, parts, lens, cosine, sine, qk_gain, cache, deps):
    rows, width = parts[0].shape
    slots, head_dim = cache[0].shape[2:]
    groups = width // head_dim - 2
    block = 16
    row_block = lambda columns: pl.BlockSpec((block, columns), lambda i: (i, 0))
    cache_block = pl.BlockSpec((block, 1, slots, head_dim), lambda i: (i, head, 0, 0))
    return pl.pallas_call(
        functools.partial(attend_kernel, len(parts)),
        name="attend",
        grid=(rows // block,),
        in_specs=[row_block(slots), row_block(head_dim), row_block(head_dim)]
        + [pl.BlockSpec((2, head_dim), lambda i: (0, 0)), cache_block, cache_block]
        + [row_block(width)] * len(parts)
        + [ANY] * len(deps),
        out_specs=[
            row_block(groups * head_dim),
            row_block(head_dim),
            row_block(head_dim),
        ],
        out_shape=[
            pltpu.HBM((rows, groups * head_dim), BF16),
            jax.ShapeDtypeStruct((rows, head_dim), BF16),
            jax.ShapeDtypeStruct((rows, head_dim), BF16),
        ],
        scratch_shapes=[pltpu.VMEM((block, groups, head_dim), F32)] * 2,
        compiler_params=pltpu.CompilerParams(vmem_limit_bytes=kernel_vmem),
        cost_estimate=small_cost,
    )(lens, cosine, sine, qk_gain, *cache, in_hbm(parts[0]), *parts[1:], *deps)


def stack_rows_kernel(count, *refs):
    parts, out, sems = refs[:count], refs[-2], refs[-1]
    rows = parts[0].shape[0]
    copies = [
        pltpu.make_async_copy(parts[n], out.at[pl.ds(n * rows, rows)], sems.at[n])
        for n in range(count)
    ]
    for copy in copies:
        copy.start()
    for copy in copies:
        copy.wait()


def stack_rows(parts, deps):
    rows, width = parts[0].shape
    return pl.pallas_call(
        functools.partial(stack_rows_kernel, len(parts)),
        name="stack_rows",
        in_specs=[ANY] * (len(parts) + len(deps)),
        out_specs=ANY,
        out_shape=pltpu.HBM((len(parts) * rows, width), BF16),
        scratch_shapes=[pltpu.SemaphoreType.DMA((len(parts),))],
        compiler_params=pltpu.CompilerParams(vmem_limit_bytes=kernel_vmem // 8),
        cost_estimate=small_cost,
    )(*parts, *deps)


def expand_kernel(members, heads, shard_ref, me_ref, *refs):
    att, refs = refs[: 2 * heads], refs[2 * heads :]
    slab, outs, total = refs[0], refs[1 : 1 + members], refs[-1]
    depth = att[0].shape[1]
    shards, share, _ = outs[0].shape
    zones = shards // 2
    for other in range(2):
        part = None
        for head in range(heads):
            term = lax.dot_general(
                att[2 * head + other][...],
                slab[:, head * depth : (head + 1) * depth],
                (((1,), (1,)), ((), ())),
                preferred_element_type=F32,
            )
            part = term if part is None else part + term
        for zone in range(zones):
            shard = shard_ref[0] ^ (2 * zone + other)
            for member in range(members):
                first = (zone * members + member) * share
                total[member, shard] = part[first : first + share, :]
    for mask in range(members):
        outs[mask][...] = total[me_ref[0] ^ mask].astype(outs[mask].dtype)


def expand(shard, me, att, slab):
    heads, members = len(att) // 2, lax.axis_size("tp")
    shards = lax.axis_size("fsdp")
    width = slab.shape[0]
    share = 2 * att[0].shape[0] // (shards * members)
    dtypes = [F32] + [BF16] * (members - 1)
    vmem = pl.BlockSpec(memory_space=pltpu.VMEM)
    smem = pl.BlockSpec(memory_space=pltpu.SMEM)
    return pl.pallas_call(
        functools.partial(expand_kernel, members, heads),
        name="expand",
        in_specs=[smem, smem] + [vmem] * (2 * heads + 1),
        out_specs=[vmem] * members,
        scratch_shapes=[pltpu.VMEM((members, shards, share, width), F32)],
        out_shape=[jax.ShapeDtypeStruct((shards, share, width), dtype) for dtype in dtypes],
        compiler_params=pltpu.CompilerParams(vmem_limit_bytes=kernel_vmem),
        cost_estimate=small_cost,
    )(shard, me, *[in_hbm(a) for a in att], slab)


def member_sum_kernel(*refs):
    total = refs[0][...]
    for share in refs[1:-1]:
        total = total + share[...].astype(F32)
    refs[-1][...] = total.astype(BF16)


def member_sum(shares):
    return pl.pallas_call(
        member_sum_kernel,
        name="member_sum",
        out_shape=jax.ShapeDtypeStruct(shares[0].shape, BF16),
        compiler_params=pltpu.CompilerParams(vmem_limit_bytes=kernel_vmem),
        cost_estimate=small_cost,
    )(*shares)


def finish_kernel(hidden_ref, pieces_ref, out_ref):
    row_terms = jnp.concatenate([pieces_ref[n] for n in range(pieces_ref.shape[0])], axis=1)
    out_ref[...] = (hidden_ref[...].astype(F32) + row_terms.astype(F32)).astype(BF16)


def finish(hidden, pieces):
    return pl.pallas_call(
        finish_kernel,
        name="finish",
        out_shape=jax.ShapeDtypeStruct(hidden.shape, BF16),
        compiler_params=pltpu.CompilerParams(vmem_limit_bytes=kernel_vmem),
        cost_estimate=small_cost,
    )(hidden, pieces)


def angles(positions, head_dim, slots):
    half_dim = head_dim // 2
    frequency = rope_base ** (-(jnp.arange(half_dim, dtype=F32) * 2.0) / head_dim)
    turned = positions.astype(F32)[:, None] * frequency[None, :]
    cosine, sine = jnp.cos(turned), jnp.sin(turned)
    lens = jnp.broadcast_to(positions[:, None], (positions.shape[0], slots))
    return (
        jnp.concatenate([cosine, cosine], axis=1),
        jnp.concatenate([-sine, sine], axis=1),
        lens,
    )


def local(
    master_qo,
    master_kv,
    moment1_qo,
    moment1_kv,
    moment2_qo,
    moment2_kv,
    grad_qo,
    grad_kv,
    hidden,
    norm_gain,
    qk_gain,
    key_cache,
    cached_value_rows,
    lengths,
):
    shards, members = lax.axis_size("fsdp"), lax.axis_size("tp")
    zones = shards // 2
    shard, member = lax.axis_index("fsdp"), lax.axis_index("tp")
    me = member.astype(jnp.int32).reshape(1)
    shard = shard.astype(jnp.int32).reshape(1)
    heads, slots, head_dim = key_cache.shape[1:]

    def swap_member(x, mask):
        return lax.ppermute(x, "tp", xor_perm(members, mask))

    def swap_zone(x, mask):
        return lax.ppermute(x, "fsdp", xor_perm(shards, 2 * mask))

    def swap_core(x):
        return lax.ppermute(x, "fsdp", xor_perm(shards, 1))

    qo = [in_hbm(x) for x in (master_qo, moment1_qo, moment2_qo, grad_qo)]
    kv = [in_hbm(x) for x in (master_kv, moment1_kv, moment2_kv, grad_kv)]
    cache = [in_hbm(key_cache), in_hbm(cached_value_rows)]

    blocks = norm_blocks(shards, members, hidden, norm_gain)
    x = lax.all_to_all(blocks, ("fsdp", "tp"), 0, 0)
    x = x.reshape(shards, -1, blocks.shape[2])

    spread = local_squares(shards * members, qo[3], kv[3])
    squares = lax.all_to_all(spread, ("fsdp", "tp"), 0, 0)

    fresh, slabs = update_input_proj(0, heads, members, 1, members - 1, me, squares, qo, kv, None)
    slabs = [list(slabs)]
    for head in range(1, heads):
        fresh, slab = update_input_proj(
            head, heads, members, None, members, me, squares, qo, kv, fresh
        )
        slabs.append(slab[0])
    fresh, slab = update_input_proj(0, heads, members, 0, 1, me, squares, qo, kv, fresh)
    slabs[0] = list(slab) + slabs[0]
    fresh_kv = fresh[1::2]
    fresh_qo = fresh[0::2]

    cosine, sine, lens = angles(lengths, head_dim, slots)
    parts, latest = [], [slabs[0][0]]
    for head in range(heads):
        if head == 0:
            weights = slabs[0][:1]
            weights += [swap_member(slabs[0][k], k) for k in range(1, members)]
        else:
            weights = lax.all_to_all(tie(slabs[head], send), "tp", 0, 0)
            weights = [weights.reshape(-1, weights.shape[2])]
        send, keep = project(me, shard, x, weights, latest)
        own, *sends = core_sum(zones, keep, swap_core(send), [])
        arrived = [swap_zone(sends[k - 1], k) for k in range(1, zones)]
        parts.append([own] + arrived)
        if head == 0:
            fresh_qo = update_output_proj(members, squares, qo, fresh_qo, sends)
            latest = [fresh_qo[3]] + arrived
    new_keys, new_values, attended = [], [], []
    latest = parts[-1][1:2]
    for head in range(heads):
        rows_out, new_key, new_value = attend(
            head, parts[head], lens, cosine, sine, qk_gain, cache, latest
        )
        new_keys.append(new_key)
        new_values.append(new_value)
        gathered = [rows_out] + [swap_zone(rows_out, k) for k in range(1, zones)]
        latest = gathered[1:2]
        attended.append(stack_rows(gathered, []))
    attended = [x for rows in attended for x in (rows, swap_core(rows))]
    out_slab = lax.all_to_all(tie(fresh_qo[3], send), "tp", 0, 0)
    out_slab = out_slab.reshape(-1, out_slab.shape[2])

    shares = expand(shard, me, attended, out_slab)
    shares = [shares[0]] + [swap_member(shares[k], k) for k in range(1, members)]
    pieces = lax.all_to_all(member_sum(shares), "fsdp", 0, 0)
    new_hidden = finish(hidden, pieces)
    return (
        fresh_qo[0],
        fresh_kv[0],
        fresh_qo[1],
        fresh_kv[1],
        fresh_qo[2],
        fresh_kv[2],
        new_hidden,
        jnp.stack(new_keys, axis=1),
        jnp.stack(new_values, axis=1),
    )


def solution(mesh):
    state = P(None, ("fsdp", "tp"), None)
    return jax.shard_map(
        local,
        mesh=mesh,
        in_specs=(
            state,
            state,
            state,
            state,
            state,
            state,
            state,
            state,
            P(("fsdp", "tp"), None),
            P(),
            P(),
            P("fsdp", "tp", None, None),
            P("fsdp", "tp", None, None),
            P("fsdp"),
        ),
        out_specs=(
            state,
            state,
            state,
            state,
            state,
            state,
            P(("fsdp", "tp"), None),
            P("fsdp", "tp", None),
            P("fsdp", "tp", None),
        ),
        check_vma=False,
    )
```

time: 826 us -> 175 us (0.21)
  waiting for transfers between devices: 609 us -> 42.9 us
  Pallas kernels: 0 us -> 76.1 us
  local copies, waits for them, and re-layouts: 66.8 us -> 5.82 us
  blocking collectives: 52.5 us -> 0 us
  starting transfers between devices: 0.21 us -> 47.6 us
  other arithmetic: 43.9 us -> 0.3 us
  matrix products: 35.4 us -> 0 us
  between operations: 16 us -> 0.9 us
    all_gather x4 -> x0, waiting for transfers between devices: 583 us -> none  [the longest x1 338 us: local(): lax.all_gather(slab_qo, 'fsdp', axis=1, tiled=True)]
    pallas_call x0 -> x19, Pallas kernels: none -> 76.1 us  [the longest x3 25.3 us: update_input_proj(): pl.pallas_call(functools.partial(input_proj_kernel, first is None, len(sl...]
    dot_general x5 -> x0, local copies, waits for them, and re-layouts: 55.4 us -> none  [the longest x2 43.6 us: local(): queries = jnp.dot(normed, full_qo[0], preferred_element_type=jnp.float32)]
    psum x1 -> x0, blocking collectives: 42 us -> none  [local(): grand_total = lax.psum(local_squares, ('fsdp', 'tp'))]
    dot_general x6 -> x0, matrix products: 35.4 us -> none  [the longest x1 11.7 us: local(): lax.dot_general(attended, full_qo[1], (((1,), (1,)), ((), ())), preferred...]
    convert_element_type x5 -> x1, other arithmetic: 33.5 us -> 0.01 us  [angles(): turned = positions.astype(F32)[:, None] * frequency[None, :]]
    ppermute x0 -> x22, waiting for transfers between devices: none -> 31 us  [the longest x12 12.9 us: swap_zone(): return lax.ppermute(x, 'fsdp', xor_perm(shards, 2 * mask))]
    reduce_scatter x1 -> x0, waiting for transfers between devices: 26.4 us -> none  [local(): lax.psum_scatter(row_terms, 'tp', scatter_dimension=0, tiled=True)]
  transfers between devices with their start and end apart: 5 -> 27, of which waited for: 5 -> 13; matrix products, arithmetic and copies ran while one was open for 7% -> 1% of each run, Pallas kernels for 0% -> 35%
where the time goes in v2:
time: 175 us; the launch traced here: 174 us
  Pallas kernels  76.1 us (43%)
  starting transfers between devices  47.6 us (27%)
  waiting for transfers between devices  42.9 us (25%)
  local copies, waits for them, and re-layouts  5.82 us (3%)
    pallas_call x3, Pallas kernels, update_input_proj(): pl.pallas_call(functools.partial(input_proj_kernel, first is None, len(sl...  25.3 us
    ppermute x12, starting transfers between devices, swap_zone(): return lax.ppermute(x, 'fsdp', xor_perm(shards, 2 * mask))  17.6 us
    pallas_call x1, Pallas kernels, update_output_proj(): pl.pallas_call(output_proj_kernel, name='adam_out', grid=(2,), in_specs=[...  16.5 us
    ppermute x12, waiting for transfers between devices, swap_zone(): return lax.ppermute(x, 'fsdp', xor_perm(shards, 2 * mask))  12.9 us
    ppermute x6, waiting for transfers between devices, swap_member(): return lax.ppermute(x, 'tp', xor_perm(members, mask))  12.3 us
    pallas_call x2, Pallas kernels, attend(): pl.pallas_call(functools.partial(attend_kernel, len(parts)), name='attend...  11.8 us
    all_to_all x1, starting transfers between devices, local(): squares = lax.all_to_all(spread, ('fsdp', 'tp'), 0, 0)  7.3 us
    ppermute x6, starting transfers between devices, swap_member(): return lax.ppermute(x, 'tp', xor_perm(members, mask))  7.18 us
  transfers between devices with their start and end apart: 27, of which 13 were waited for; matrix products, arithmetic and copies ran while one was open for 1% of the time, Pallas kernels for 35%

profile of v2, /device:TPU:0, one launch (start us, length us, event | category | flops | bytes accessed | tf_op | source)
XLA Modules:
  0.0 173.7 jit_solution(15233144310496452269)
XLA Ops:
  0.7 6.1 %grad_squares.1 = f32[32,1,128]{2,1,0:T(1,128)} custom-call(f32[2,160,8192]{2,1,0:T(8,128)} %refs_3_.9, f32[2,160,1024]{2,1,0:T(8,128)} %refs_7_.5), custom_call_target="tpu_custom_call" | custom-call | flops 1024 | bytes 1024 | tf_op jit(solution)/shard_map/grad_squares/pallas_call | solution.py:85
  6.7 7.3 %all-to-all-start = ((f32[32,1,128]{2,1,0:T(1,128)}), f32[32,1,128]{2,1,0:T(1,128)S(1)}, u32[]{:S(2)}, u32[]{:S(2)}) async-start(f32[32,1,128]{2,1,0:T(1,128)} %grad_squares.1), calls=%async_computation | async-start | bytes 32768 | tf_op jit(solution)/shard_map/all_to_all | solution.py:553
  14.0 1.1 norm_rows.1
  15.1 6.0 %all-to-all-done.squares_ref = f32[32,1,128]{2,1,0:T(1,128)S(1)} async-done(((f32[32,1,128]{2,1,0:T(1,128)}), f32[32,1,128]{2,1,0:T(1,128)S(1)}, u32[]{:S(2)}, u32[]{:S(2)}) %all-to-all-start) | async-done | bytes 16416 | tf_op jit(solution)/shard_map/all_to_all | solution.py:553
  21.1 2.6 %all-to-all-start.1 = ((bf16[32,16,640]{2,1,0:T(8,128)(2,1)}), bf16[32,16,640]{2,1,0:T(8,128)(2,1)S(1)}, u32[]{:S(2)}, u32[]{:S(2)}) async-start(bf16[32,16,640]{2,1,0:T(8,128)(2,1)} %norm_rows.1), calls=%async_computation.1 | async-start | bytes 1310720 | tf_op jit(solution)/shard_map/all_to_all | solution.py:549
  23.7 10.4 %adam_in.3 = (f32[2,160,8192]{2,1,0:T(8,128)}, f32[2,160,1024]{2,1,0:T(8,128)}, f32[2,160,8192]{2,1,0:T(8,128)}, f32[2,160,1024]{2,1,0:T(8,128)}, f32[2,160,8192...) custom-call(s32[1]{0:T(128)} %bitcast.me_ref, ...), custom_call_target="tpu_custom_call" | custom-call | flops 1024 | bytes 1024 | tf_op jit(solution)/shard_map/adam_in/pallas_call | solution.py:186
  34.2 1.7 collective-permute-start
  35.9 1.5 collective-permute-start.1
  37.4 0.4 collective-permute-start.2
  37.7 10.5 %adam_in.4 = (f32[2,160,8192]{2,1,0:T(8,128)}, f32[2,160,1024]{2,1,0:T(8,128)}, f32[2,160,8192]{2,1,0:T(8,128)}, f32[2,160,1024]{2,1,0:T(8,128)}, f32[2,160,8192...) custom-call(s32[1]{0:T(128)} %bitcast.me_ref, ...), custom_call_target="tpu_custom_call", output_to_operand_aliasing={{0}: (10, {}), {1}: (11, {}), {2}: (12, {}), {3}: (13, {}),... | custom-call | flops 1024 | bytes 1024 | tf_op jit(solution)/shard_map/adam_in/pallas_call | solution.py:186
  48.3 4.3 %adam_in.5 = (f32[2,160,8192]{2,1,0:T(8,128)}, f32[2,160,1024]{2,1,0:T(8,128)}, f32[2,160,8192]{2,1,0:T(8,128)}, f32[2,160,1024]{2,1,0:T(8,128)}, f32[2,160,8192...) custom-call(s32[1]{0:T(128)} %bitcast.me_ref, ...), custom_call_target="tpu_custom_call", output_to_operand_aliasing={{0}: (10, {}), {1}: (11, {}), {2}: (12, {}), {3}: (13, {}),... | custom-call | flops 1024 | bytes 1024 | tf_op jit(solution)/shard_map/adam_in/pallas_call | solution.py:186
  52.6 3.5 %collective-permute-done.1.refs_2_ = bf16[160,1280]{1,0:T(8,128)(2,1)S(1)} collective-permute-done((bf16[160,1280]{1,0:T(8,128)(2,1)}, bf16[160,1280]{1,0:T(8,128)(2,1)S(1)}, u32[]{:S(2)}, u32[]{:S(2)}) %collective-permute-start.1) | collective-permute-done | bytes 409632 | tf_op jit(solution)/shard_map/ppermute | solution.py:536
  56.1 0.9 collective-permute-done.2.refs_3_
  57.0 0.0 all-to-all-done.1
  57.0 1.0 copy-done.1
  58.0 2.4 %project.2 = (bf16[256,1280]{1,0:T(8,128)(2,1)}, f32[256,1280]{1,0:T(8,128)}) custom-call(s32[1]{0:T(128)} %bitcast.me_ref, s32[1]{0:T(128)} %bitcast.1.shard_ref, bf16[8,64,640]{2,1,0:T(8,128)(2,1)S(1)} %bitcast.12, bf16[160,1280]{1,0:T(8,128)(2,1)S(1)} %copy-done.1, bf16[160,1280]{1,0:T(8,128)(2,1)S(1)} %collective-permute-done.refs_1_, ...), custom_call_target="tpu_custom_call" | custom-call | flops 1024 | bytes 1024 | tf_op jit(solution)/shard_map/project/pallas_call | solution.py:272
  60.4 3.9 %all-to-all-start.2 = ((bf16[4,160,1280]{2,1,0:T(8,128)(2,1)}), bf16[4,160,1280]{2,1,0:T(8,128)(2,1)S(1)}, u32[]{:S(2)}, u32[]{:S(2)}) async-start(bf16[4,160,1280]{2,1,0:T(8,128)(2,1)} %tie.2), calls=%async_computation.2 | async-start | bytes 3276800 | tf_op jit(solution)/shard_map/all_to_all | solution.py:574
  64.3 0.1 collective-permute-start.3
  64.4 2.1 %collective-permute-done.3.arrived_ref = bf16[256,1280]{1,0:T(8,128)(2,1)S(1)} collective-permute-done((bf16[256,1280]{1,0:T(8,128)(2,1)S(1)}, bf16[256,1280]{1,0:T(8,128)(2,1)S(1)}, u32[]{:S(2)}, u32[]{:S(2)}) %collective-permute-start.3) | collective-permute-done | bytes 655392 | tf_op jit(solution)/shard_map/ppermute | solution.py:542
  66.4 2.1 %core_sum.2 = (f32[64,1280]{1,0:T(8,128)}, bf16[64,1280]{1,0:T(8,128)(2,1)S(1)}, bf16[64,1280]{1,0:T(8,128)(2,1)S(1)}, bf16[64,1280]{1,0:T(8,128)(2,1)S(1)}) custom-call(f32[256,1280]{1,0:T(8,128)} %get-tuple-element.77.keep_ref, bf16[256,1280]{1,0:T(8,128)(2,1)S(1)} %collective-permute-done.3.arrived_ref), custom_call_target="tpu_custom_call" | custom-call | flops 1024 | bytes 1024 | tf_op jit(solution)/shard_map/core_sum/pallas_call | solution.py:299
  68.6 1.6 collective-permute-start.4
  70.2 2.1 %collective-permute-start.5 = (bf16[64,1280]{1,0:T(8,128)(2,1)S(1)}, bf16[64,1280]{1,0:T(8,128)(2,1)S(1)}, u32[]{:S(2)}, u32[]{:S(2)}) collective-permute-start(bf16[64,1280]{1,0:T(8,128)(2,1)S(1)} %get-tuple-element.80.refs_8_), channel_id=1, source_target_pairs={{0,16},{4,20},{8,24},{12,28},{16,0},{20,4},{24,8},{28,12},{1,17},{... | collective-permute-start | bytes 491528 | tf_op jit(solution)/shard_map/ppermute | solution.py:539
  72.3 0.7 collective-permute-start.6
  73.0 16.5 %adam_out.1 = (f32[2,160,8192]{2,1,0:T(8,128)}, f32[2,160,8192]{2,1,0:T(8,128)}, f32[2,160,8192]{2,1,0:T(8,128)}, bf16[4,160,2048]{2,1,0:T(8,128)(2,1)}) custom-call(f32[32,1,128]{2,1,0:T(1,128)} %copy-done.3, f32[2,160,8192]{2,1,0:T(8,128)} %refs_0_.7, f32[2,160,8192]{2,1,0:T(8,128)} %refs_1_.7, ...), custom_call_target="tpu_custom_call", output_to_operand_aliasing={{0}: (5, {}), {1}: (6, {}), {2}: (7, {})} | custom-call | flops 1024 | bytes 1024 | tf_op jit(solution)/shard_map/adam_out/pallas_call | solution.py:222
  89.5 1.7 copy-done
  91.2 2.3 %project.3 = (bf16[256,1280]{1,0:T(8,128)(2,1)}, f32[256,1280]{1,0:T(8,128)}) custom-call(s32[1]{0:T(128)} %bitcast.me_ref, s32[1]{0:T(128)} %bitcast.1.shard_ref, bf16[8,64,640]{2,1,0:T(8,128)(2,1)S(1)} %bitcast.13, bf16[640,1280]{1,0:T(8,128)(2,1)S(1)} %bitcast.11, bf16[4,160,2048]{2,1,0:T(8,128)(2,1)S(1)} %copy-done, ...), custom_call_target="tpu_custom_call" | custom-call | flops 1024 | bytes 1024 | tf_op jit(solution)/shard_map/project/pallas_call | solution.py:272
  93.5 4.0 %all-to-all-start.3 = ((bf16[4,160,2048]{2,1,0:T(8,128)(2,1)}), bf16[4,160,2048]{2,1,0:T(8,128)(2,1)S(1)}, u32[]{:S(2)}, u32[]{:S(2)}) async-start(bf16[4,160,2048]{2,1,0:T(8,128)(2,1)} %tie.3), calls=%async_computation.3 | async-start | bytes 5242880 | tf_op jit(solution)/shard_map/all_to_all | solution.py:595
  97.6 2.3 %collective-permute-done.7.arrived_ref = bf16[256,1280]{1,0:T(8,128)(2,1)S(1)} collective-permute-done((bf16[256,1280]{1,0:T(8,128)(2,1)}, bf16[256,1280]{1,0:T(8,128)(2,1)S(1)}, u32[]{:S(2)}, u32[]{:S(2)}) %collective-permute-start.7) | collective-permute-done | bytes 655392 | tf_op jit(solution)/shard_map/ppermute | solution.py:542
  99.8 2.2 %core_sum.3 = (f32[64,1280]{1,0:T(8,128)}, bf16[64,1280]{1,0:T(8,128)(2,1)S(1)}, bf16[64,1280]{1,0:T(8,128)(2,1)S(1)}, bf16[64,1280]{1,0:T(8,128)(2,1)S(1)}) custom-call(f32[256,1280]{1,0:T(8,128)} %get-tuple-element.91.keep_ref, bf16[256,1280]{1,0:T(8,128)(2,1)S(1)} %collective-permute-done.7.arrived_ref), custom_call_target="tpu_custom_call" | custom-call | flops 1024 | bytes 1024 | tf_op jit(solution)/shard_map/core_sum/pallas_call | solution.py:299
  102.0 0.7 collective-permute-start.8
  102.7 0.2 fusion
  102.9 3.1 %collective-permute-start.13 = (bf16[64,1280]{1,0:T(8,128)(2,1)S(1)}, bf16[64,1280]{1,0:T(8,128)(2,1)S(1)}, u32[]{:S(2)}, u32[]{:S(2)}) collective-permute-start(bf16[64,1280]{1,0:T(8,128)(2,1)S(1)} %get-tuple-element.96), channel_id=1, source_target_pairs={{0,16},{4,20},{8,24},{12,28},{16,0},{20,4},{24,8},{28,12},{1,17},{... | collective-permute-start | bytes 491528 | tf_op jit(solution)/shard_map/ppermute | solution.py:539
  105.9 0.7 collective-permute-start.14
  106.7 0.1 pad_maximum_fusion
  106.7 4.4 %collective-permute-done.8.refs_10_.refs_7_ = bf16[64,1280]{1,0:T(8,128)(2,1)S(1)} collective-permute-done((bf16[64,1280]{1,0:T(8,128)(2,1)S(1)}, bf16[64,1280]{1,0:T(8,128)(2,1)S(1)}, u32[]{:S(2)}, u32[]{:S(2)}) %collective-permute-start.8) | collective-permute-done | bytes 163872 | tf_op jit(solution)/shard_map/ppermute | solution.py:539
  111.1 0.1 broadcast_in_dim.2.refs_0_
  111.2 5.9 %attend.2 = (bf16[64,1024]{1,0:T(8,128)(2,1)}, bf16[64,128]{1,0:T(8,128)(2,1)S(1)}, bf16[64,128]{1,0:T(8,128)(2,1)S(1)}) custom-call(s32[64,128]{1,0:T(8,128)S(1)} %broadcast_in_dim.2.refs_0_, f32[64,128]{1,0:T(8,128)S(1)} %get-tuple-element.119.refs_1_, f32[64,128]{1,0:T(8,128)S(1)} %get-tuple-element.120.refs_2_, f32[2,128]{1,0:T(2,128)S(1)} %copy-done.10, ...), custom_call_target="tpu_custom_call" | custom-call | flops 1024 | bytes 1024 | tf_op jit(solution)/shard_map/attend/pallas_call | solution.py:371
  117.0 2.6 %collective-permute-start.10 = (bf16[64,1024]{1,0:T(8,128)(2,1)}, bf16[64,1024]{1,0:T(8,128)(2,1)S(1)}, u32[]{:S(2)}, u32[]{:S(2)}) collective-permute-start(bf16[64,1024]{1,0:T(8,128)(2,1)} %get-tuple-element.94.refs_0_), channel_id=1, source_target_pairs={{0,16},{4,20},{8,24},{12,28},{16,0},{20,4},{24,8},{28,12},{1,17},{... | collective-permute-start | bytes 393224 | tf_op jit(solution)/shard_map/ppermute | solution.py:539
  119.6 1.8 %collective-permute-start.11 = (bf16[64,1024]{1,0:T(8,128)(2,1)}, bf16[64,1024]{1,0:T(8,128)(2,1)S(1)}, u32[]{:S(2)}, u32[]{:S(2)}) collective-permute-start(bf16[64,1024]{1,0:T(8,128)(2,1)} %get-tuple-element.94.refs_0_), channel_id=1, source_target_pairs={{0,24},{4,28},{8,16},{12,20},{16,8},{20,12},{24,0},{28,4},{1,25},{... | collective-permute-start | bytes 393224 | tf_op jit(solution)/shard_map/ppermute | solution.py:539
  121.4 2.0 %collective-permute-done.9.refs_1_.refs_10_ = bf16[64,1024]{1,0:T(8,128)(2,1)S(1)} collective-permute-done((bf16[64,1024]{1,0:T(8,128)(2,1)}, bf16[64,1024]{1,0:T(8,128)(2,1)S(1)}, u32[]{:S(2)}, u32[]{:S(2)}) %collective-permute-start.9) | collective-permute-done | bytes 131104 | tf_op jit(solution)/shard_map/ppermute | solution.py:539
  123.5 5.9 %attend.3 = (bf16[64,1024]{1,0:T(8,128)(2,1)}, bf16[64,128]{1,0:T(8,128)(2,1)S(1)}, bf16[64,128]{1,0:T(8,128)(2,1)S(1)}) custom-call(s32[64,128]{1,0:T(8,128)S(1)} %broadcast_in_dim.2.refs_0_, f32[64,128]{1,0:T(8,128)S(1)} %get-tuple-element.119.refs_1_, f32[64,128]{1,0:T(8,128)S(1)} %get-tuple-element.120.refs_2_, f32[2,128]{1,0:T(2,128)S(1)} %copy-done.10, ...), custom_call_target="tpu_custom_call" | custom-call | flops 1024 | bytes 1024 | tf_op jit(solution)/shard_map/attend/pallas_call | solution.py:371
  129.4 2.0 %collective-permute-start.16 = (bf16[64,1024]{1,0:T(8,128)(2,1)}, bf16[64,1024]{1,0:T(8,128)(2,1)S(1)}, u32[]{:S(2)}, u32[]{:S(2)}) collective-permute-start(bf16[64,1024]{1,0:T(8,128)(2,1)} %get-tuple-element.98.refs_0_), channel_id=1, source_target_pairs={{0,16},{4,20},{8,24},{12,28},{16,0},{20,4},{24,8},{28,12},{1,17},{... | collective-permute-start | bytes 393224 | tf_op jit(solution)/shard_map/ppermute | solution.py:539
  131.4 2.4 %collective-permute-start.17 = (bf16[64,1024]{1,0:T(8,128)(2,1)}, bf16[64,1024]{1,0:T(8,128)(2,1)S(1)}, u32[]{:S(2)}, u32[]{:S(2)}) collective-permute-start(bf16[64,1024]{1,0:T(8,128)(2,1)} %get-tuple-element.98.refs_0_), channel_id=1, source_target_pairs={{0,24},{4,28},{8,16},{12,20},{16,8},{20,12},{24,0},{28,4},{1,25},{... | collective-permute-start | bytes 393224 | tf_op jit(solution)/shard_map/ppermute | solution.py:539
  133.8 0.8 stack_rows.2.refs_0_
  134.6 0.1 collective-permute-start.12
  134.7 2.3 %collective-permute-done.15.refs_1_ = bf16[64,1024]{1,0:T(8,128)(2,1)S(1)} collective-permute-done((bf16[64,1024]{1,0:T(8,128)(2,1)}, bf16[64,1024]{1,0:T(8,128)(2,1)S(1)}, u32[]{:S(2)}, u32[]{:S(2)}) %collective-permute-start.15) | collective-permute-done | bytes 131104 | tf_op jit(solution)/shard_map/ppermute | solution.py:539
  137.0 4.2 %collective-permute-done.16.refs_2_ = bf16[64,1024]{1,0:T(8,128)(2,1)S(1)} collective-permute-done((bf16[64,1024]{1,0:T(8,128)(2,1)}, bf16[64,1024]{1,0:T(8,128)(2,1)S(1)}, u32[]{:S(2)}, u32[]{:S(2)}) %collective-permute-start.16) | collective-permute-done | bytes 131104 | tf_op jit(solution)/shard_map/ppermute | solution.py:539
  141.2 0.9 copy-done.8
  142.1 0.8 stack_rows.3.refs_2_
  142.9 0.1 collective-permute-start.18
  143.0 0.8 copy-done.12
  143.8 1.4 collective-permute-done.18.refs_3_
  145.2 3.4 %expand.1 = (f32[8,16,640]{2,1,0:T(8,128)S(1)}, bf16[8,16,640]{2,1,0:T(8,128)(2,1)S(1)}, bf16[8,16,640]{2,1,0:T(8,128)(2,1)S(1)}, bf16[8,16,640]{2,1,0:T(8,128)(2,1)S(1)}) custom-call(s32[1]{0:T(128)} %bitcast.1.shard_ref, s32[1]{0:T(128)} %bitcast.me_ref, bf16[256,1024]{1,0:T(8,128)(2,1)} %stack_rows.2.refs_0_, bf16[256,1024]{1,0:T(8,128)(2,1)} %copy-done.12, ...), custom_call_target="tpu_custom_call" | custom-call | flops 1024 | bytes 1024 | tf_op jit(solution)/shard_map/expand/pallas_call | solution.py:455
  148.7 2.1 %collective-permute-start.19 = (bf16[8,16,640]{2,1,0:T(8,128)(2,1)S(1)}, bf16[8,16,640]{2,1,0:T(8,128)(2,1)S(1)}, u32[]{:S(2)}, u32[]{:S(2)}) collective-permute-start(bf16[8,16,640]{2,1,0:T(8,128)(2,1)S(1)} %get-tuple-element.100), channel_id=1, source_target_pairs={{0,1},{1,0},{2,3},{3,2},{4,5},{5,4},{6,7},{7,6},{8,9},{9,8},{10,11... | collective-permute-start | bytes 491528 | tf_op jit(solution)/shard_map/ppermute | solution.py:536
  150.7 1.5 collective-permute-start.20
  152.2 0.1 collective-permute-start.21
  152.3 3.4 %collective-permute-done.19.refs_1_ = bf16[8,16,640]{2,1,0:T(8,128)(2,1)S(1)} collective-permute-done((bf16[8,16,640]{2,1,0:T(8,128)(2,1)S(1)}, bf16[8,16,640]{2,1,0:T(8,128)(2,1)S(1)}, u32[]{:S(2)}, u32[]{:S(2)}) %collective-permute-start.19) | collective-permute-done | bytes 163872 | tf_op jit(solution)/shard_map/ppermute | solution.py:536
  155.7 4.5 %collective-permute-done.20.refs_2_ = bf16[8,16,640]{2,1,0:T(8,128)(2,1)S(1)} collective-permute-done((bf16[8,16,640]{2,1,0:T(8,128)(2,1)S(1)}, bf16[8,16,640]{2,1,0:T(8,128)(2,1)S(1)}, u32[]{:S(2)}, u32[]{:S(2)}) %collective-permute-start.20) | collective-permute-done | bytes 163872 | tf_op jit(solution)/shard_map/ppermute | solution.py:536
  160.2 0.7 member_sum.1
  161.0 4.8 %all-to-all-start.4 = ((bf16[8,16,640]{2,1,0:T(8,128)(2,1)}), bf16[8,16,640]{2,1,0:T(8,128)(2,1)S(1)}, u32[]{:S(2)}, u32[]{:S(2)}) async-start(bf16[8,16,640]{2,1,0:T(8,128)(2,1)} %member_sum.1), calls=%async_computation.4 | async-start | bytes 327680 | tf_op jit(solution)/shard_map/all_to_all | solution.py:600
  165.8 0.6 copy.41
  166.4 0.7 copy.40
  167.1 5.9 %all-to-all-done.4.pieces_ref = bf16[8,16,640]{2,1,0:T(8,128)(2,1)S(1)} async-done(((bf16[8,16,640]{2,1,0:T(8,128)(2,1)}), bf16[8,16,640]{2,1,0:T(8,128)(2,1)S(1)}, u32[]{:S(2)}, u32[]{:S(2)}) %all-to-all-start.4) | async-done | bytes 163872 | tf_op jit(solution)/shard_map/all_to_all | solution.py:600
  173.0 0.7 finish.1
  (46 shorter events, 0.1 us)
Async XLA Ops:
  0.6 13.4 %copy-start.9 = (f32[5120]{0:T(1024)S(1)}, f32[5120]{0:T(1024)}, u32[]{:S(2)}) copy-start(f32[5120]{0:T(1024)} %param.23) | copy-start | bytes 61444
  0.7 13.4 %copy-start.2 = (bf16[16,5120]{1,0:T(8,128)(2,1)S(1)}, bf16[16,5120]{1,0:T(8,128)(2,1)}, u32[]{:S(2)}) copy-start(bf16[16,5120]{1,0:T(8,128)(2,1)} %hidden_ref.3) | copy-start | bytes 491524
  6.7 14.4 %all-to-all-start = ((f32[32,1,128]{2,1,0:T(1,128)}), f32[32,1,128]{2,1,0:T(1,128)S(1)}, u32[]{:S(2)}, u32[]{:S(2)}) async-start(f32[32,1,128]{2,1,0:T(1,128)} %grad_squares.1), calls=%async_computation | async-start | bytes 32768 | tf_op jit(solution)/shard_map/all_to_all | solution.py:553
  21.1 27.1 %copy-start.3 = (f32[32,1,128]{2,1,0:T(1,128)}, f32[32,1,128]{2,1,0:T(1,128)S(1)}, u32[]{:S(2)}) copy-start(f32[32,1,128]{2,1,0:T(1,128)S(1)} %all-to-all-done.squares_ref) | copy-start | bytes 49156
  21.1 35.9 %all-to-all-start.1 = ((bf16[32,16,640]{2,1,0:T(8,128)(2,1)}), bf16[32,16,640]{2,1,0:T(8,128)(2,1)S(1)}, u32[]{:S(2)}, u32[]{:S(2)}) async-start(bf16[32,16,640]{2,1,0:T(8,128)(2,1)} %norm_rows.1), calls=%async_computation.1 | async-start | bytes 1310720 | tf_op jit(solution)/shard_map/all_to_all | solution.py:549
  34.2 18.4 %collective-permute-start = (bf16[160,1280]{1,0:T(8,128)(2,1)}, bf16[160,1280]{1,0:T(8,128)(2,1)S(1)}, u32[]{:S(2)}, u32[]{:S(2)}) collective-permute-start(bf16[160,1280]{1,0:T(8,128)(2,1)} %get-tuple-element.74), channel_id=1, source_target_pairs={{0,1},{1,0},{2,3},{3,2},{4,5},{5,4},{6,7},{7,6},{8,9},{9,8},{10,11... | collective-permute-start | bytes 1228808 | tf_op jit(solution)/shard_map/ppermute | solution.py:536
  35.9 20.2 %collective-permute-start.1 = (bf16[160,1280]{1,0:T(8,128)(2,1)}, bf16[160,1280]{1,0:T(8,128)(2,1)S(1)}, u32[]{:S(2)}, u32[]{:S(2)}) collective-permute-start(bf16[160,1280]{1,0:T(8,128)(2,1)} %get-tuple-element.75), channel_id=1, source_target_pairs={{0,2},{1,3},{2,0},{3,1},{4,6},{5,7},{6,4},{7,5},{8,10},{9,11},{10,... | collective-permute-start | bytes 1228808 | tf_op jit(solution)/shard_map/ppermute | solution.py:536
  37.4 19.6 %collective-permute-start.2 = (bf16[160,1280]{1,0:T(8,128)(2,1)}, bf16[160,1280]{1,0:T(8,128)(2,1)S(1)}, u32[]{:S(2)}, u32[]{:S(2)}) collective-permute-start(bf16[160,1280]{1,0:T(8,128)(2,1)} %get-tuple-element.76), channel_id=1, source_target_pairs={{0,3},{1,2},{2,1},{3,0},{4,7},{5,6},{6,5},{7,4},{8,11},{9,10},{10,... | collective-permute-start | bytes 1228808 | tf_op jit(solution)/shard_map/ppermute | solution.py:536
  57.0 1.0 copy-start.1
  60.4 3.9 %copy-start.11 = (bf16[256,1280]{1,0:T(8,128)(2,1)S(1)}, bf16[256,1280]{1,0:T(8,128)(2,1)}, u32[]{:S(2)}) copy-start(bf16[256,1280]{1,0:T(8,128)(2,1)} %get-tuple-element.78.refs_1_) | copy-start | bytes 1966084
  60.4 29.1 %all-to-all-start.2 = ((bf16[4,160,1280]{2,1,0:T(8,128)(2,1)}), bf16[4,160,1280]{2,1,0:T(8,128)(2,1)S(1)}, u32[]{:S(2)}, u32[]{:S(2)}) async-start(bf16[4,160,1280]{2,1,0:T(8,128)(2,1)} %tie.2), calls=%async_computation.2 | async-start | bytes 3276800 | tf_op jit(solution)/shard_map/all_to_all | solution.py:574
  64.3 2.2 %collective-permute-start.3 = (bf16[256,1280]{1,0:T(8,128)(2,1)S(1)}, bf16[256,1280]{1,0:T(8,128)(2,1)S(1)}, u32[]{:S(2)}, u32[]{:S(2)}) collective-permute-start(bf16[256,1280]{1,0:T(8,128)(2,1)S(1)} %copy-done.11), channel_id=1, source_target_pairs={{0,4},{4,0},{8,12},{12,8},{16,20},{20,16},{24,28},{28,24},{1,5},{5... | collective-permute-start | bytes 1966088 | tf_op jit(solution)/shard_map/ppermute | solution.py:542
  68.6 4.4 %copy-start.4 = (bf16[64,1280]{1,0:T(8,128)(2,1)}, bf16[64,1280]{1,0:T(8,128)(2,1)S(1)}, u32[]{:S(2)}) copy-start(bf16[64,1280]{1,0:T(8,128)(2,1)S(1)} %get-tuple-element.81.refs_9_) | copy-start | bytes 491524
  68.6 4.4 %copy-start.5 = (bf16[64,1280]{1,0:T(8,128)(2,1)}, bf16[64,1280]{1,0:T(8,128)(2,1)S(1)}, u32[]{:S(2)}) copy-start(bf16[64,1280]{1,0:T(8,128)(2,1)S(1)} %get-tuple-element.80.refs_8_) | copy-start | bytes 491524
  68.6 4.4 %copy-start.6 = (bf16[64,1280]{1,0:T(8,128)(2,1)}, bf16[64,1280]{1,0:T(8,128)(2,1)S(1)}, u32[]{:S(2)}) copy-start(bf16[64,1280]{1,0:T(8,128)(2,1)S(1)} %get-tuple-element.79.refs_7_) | copy-start | bytes 491524
  68.6 20.9 %collective-permute-start.4 = (bf16[64,1280]{1,0:T(8,128)(2,1)S(1)}, bf16[64,1280]{1,0:T(8,128)(2,1)S(1)}, u32[]{:S(2)}, u32[]{:S(2)}) collective-permute-start(bf16[64,1280]{1,0:T(8,128)(2,1)S(1)} %get-tuple-element.79.refs_7_), channel_id=1, source_target_pairs={{0,8},{4,12},{8,0},{12,4},{16,24},{20,28},{24,16},{28,20},{1,9},{5... | collective-permute-start | bytes 491528 | tf_op jit(solution)/shard_map/ppermute | solution.py:539
  70.2 19.3 %collective-permute-start.5 = (bf16[64,1280]{1,0:T(8,128)(2,1)S(1)}, bf16[64,1280]{1,0:T(8,128)(2,1)S(1)}, u32[]{:S(2)}, u32[]{:S(2)}) collective-permute-start(bf16[64,1280]{1,0:T(8,128)(2,1)S(1)} %get-tuple-element.80.refs_8_), channel_id=1, source_target_pairs={{0,16},{4,20},{8,24},{12,28},{16,0},{20,4},{24,8},{28,12},{1,17},{... | collective-permute-start | bytes 491528 | tf_op jit(solution)/shard_map/ppermute | solution.py:539
  72.3 17.2 %collective-permute-start.6 = (bf16[64,1280]{1,0:T(8,128)(2,1)S(1)}, bf16[64,1280]{1,0:T(8,128)(2,1)S(1)}, u32[]{:S(2)}, u32[]{:S(2)}) collective-permute-start(bf16[64,1280]{1,0:T(8,128)(2,1)S(1)} %get-tuple-element.81.refs_9_), channel_id=1, source_target_pairs={{0,24},{4,28},{8,16},{12,20},{16,8},{20,12},{24,0},{28,4},{1,25},{... | collective-permute-start | bytes 491528 | tf_op jit(solution)/shard_map/ppermute | solution.py:539
  89.5 1.7 %copy-start = (bf16[4,160,2048]{2,1,0:T(8,128)(2,1)S(1)}, bf16[4,160,2048]{2,1,0:T(8,128)(2,1)}, u32[]{:S(2)}) copy-start(bf16[4,160,2048]{2,1,0:T(8,128)(2,1)} %get-tuple-element.90.refs_1_.refs_0_) | copy-start | bytes 7864324
  93.5 4.0 %copy-start.13 = (s32[64]{0:T(128)S(1)}, s32[64]{0:T(128)}, u32[]{:S(2)}) copy-start(s32[64]{0:T(128)} %param.27) | copy-start | bytes 772
  93.5 17.7 %copy-start.10 = (f32[2,128]{1,0:T(2,128)S(1)}, f32[2,128]{1,0:T(2,128)}, u32[]{:S(2)}) copy-start(f32[2,128]{1,0:T(2,128)} %refs_3_.11) | copy-start | bytes 3076
  93.5 51.7 %all-to-all-start.3 = ((bf16[4,160,2048]{2,1,0:T(8,128)(2,1)}), bf16[4,160,2048]{2,1,0:T(8,128)(2,1)S(1)}, u32[]{:S(2)}, u32[]{:S(2)}) async-start(bf16[4,160,2048]{2,1,0:T(8,128)(2,1)} %tie.3), calls=%async_computation.3 | async-start | bytes 5242880 | tf_op jit(solution)/shard_map/all_to_all | solution.py:595
  97.5 2.3 %collective-permute-start.7 = (bf16[256,1280]{1,0:T(8,128)(2,1)}, bf16[256,1280]{1,0:T(8,128)(2,1)S(1)}, u32[]{:S(2)}, u32[]{:S(2)}) collective-permute-start(bf16[256,1280]{1,0:T(8,128)(2,1)} %get-tuple-element.92.refs_1_), channel_id=1, source_target_pairs={{0,4},{4,0},{8,12},{12,8},{16,20},{20,16},{24,28},{28,24},{1,5},{5... | collective-permute-start | bytes 1966088 | tf_op jit(solution)/shard_map/ppermute | solution.py:542
  102.0 9.1 %collective-permute-start.8 = (bf16[64,1280]{1,0:T(8,128)(2,1)S(1)}, bf16[64,1280]{1,0:T(8,128)(2,1)S(1)}, u32[]{:S(2)}, u32[]{:S(2)}) collective-permute-start(bf16[64,1280]{1,0:T(8,128)(2,1)S(1)} %get-tuple-element.93), channel_id=1, source_target_pairs={{0,8},{4,12},{8,0},{12,4},{16,24},{20,28},{24,16},{28,20},{1,9},{5... | collective-permute-start | bytes 491528 | tf_op jit(solution)/shard_map/ppermute | solution.py:539
  102.9 18.5 %collective-permute-start.13 = (bf16[64,1280]{1,0:T(8,128)(2,1)S(1)}, bf16[64,1280]{1,0:T(8,128)(2,1)S(1)}, u32[]{:S(2)}, u32[]{:S(2)}) collective-permute-start(bf16[64,1280]{1,0:T(8,128)(2,1)S(1)} %get-tuple-element.96), channel_id=1, source_target_pairs={{0,16},{4,20},{8,24},{12,28},{16,0},{20,4},{24,8},{28,12},{1,17},{... | collective-permute-start | bytes 491528 | tf_op jit(solution)/shard_map/ppermute | solution.py:539
  105.9 15.5 %collective-permute-start.14 = (bf16[64,1280]{1,0:T(8,128)(2,1)S(1)}, bf16[64,1280]{1,0:T(8,128)(2,1)S(1)}, u32[]{:S(2)}, u32[]{:S(2)}) collective-permute-start(bf16[64,1280]{1,0:T(8,128)(2,1)S(1)} %get-tuple-element.97), channel_id=1, source_target_pairs={{0,24},{4,28},{8,16},{12,20},{16,8},{20,12},{24,0},{28,4},{1,25},{... | collective-permute-start | bytes 491528 | tf_op jit(solution)/shard_map/ppermute | solution.py:539
  117.0 6.4 %collective-permute-start.9 = (bf16[64,1024]{1,0:T(8,128)(2,1)}, bf16[64,1024]{1,0:T(8,128)(2,1)S(1)}, u32[]{:S(2)}, u32[]{:S(2)}) collective-permute-start(bf16[64,1024]{1,0:T(8,128)(2,1)} %get-tuple-element.94.refs_0_), channel_id=1, source_target_pairs={{0,8},{4,12},{8,0},{12,4},{16,24},{20,28},{24,16},{28,20},{1,9},{5... | collective-permute-start | bytes 393224 | tf_op jit(solution)/shard_map/ppermute | solution.py:539
  117.0 16.7 %collective-permute-start.10 = (bf16[64,1024]{1,0:T(8,128)(2,1)}, bf16[64,1024]{1,0:T(8,128)(2,1)S(1)}, u32[]{:S(2)}, u32[]{:S(2)}) collective-permute-start(bf16[64,1024]{1,0:T(8,128)(2,1)} %get-tuple-element.94.refs_0_), channel_id=1, source_target_pairs={{0,16},{4,20},{8,24},{12,28},{16,0},{20,4},{24,8},{28,12},{1,17},{... | collective-permute-start | bytes 393224 | tf_op jit(solution)/shard_map/ppermute | solution.py:539
  119.6 14.1 %collective-permute-start.11 = (bf16[64,1024]{1,0:T(8,128)(2,1)}, bf16[64,1024]{1,0:T(8,128)(2,1)S(1)}, u32[]{:S(2)}, u32[]{:S(2)}) collective-permute-start(bf16[64,1024]{1,0:T(8,128)(2,1)} %get-tuple-element.94.refs_0_), channel_id=1, source_target_pairs={{0,24},{4,28},{8,16},{12,20},{16,8},{20,12},{24,0},{28,4},{1,25},{... | collective-permute-start | bytes 393224 | tf_op jit(solution)/shard_map/ppermute | solution.py:539
  123.5 10.3 %copy-start.7 = (bf16[64,1024]{1,0:T(8,128)(2,1)S(1)}, bf16[64,1024]{1,0:T(8,128)(2,1)}, u32[]{:S(2)}) copy-start(bf16[64,1024]{1,0:T(8,128)(2,1)} %get-tuple-element.94.refs_0_) | copy-start | bytes 393220
  129.4 7.6 %collective-permute-start.15 = (bf16[64,1024]{1,0:T(8,128)(2,1)}, bf16[64,1024]{1,0:T(8,128)(2,1)S(1)}, u32[]{:S(2)}, u32[]{:S(2)}) collective-permute-start(bf16[64,1024]{1,0:T(8,128)(2,1)} %get-tuple-element.98.refs_0_), channel_id=1, source_target_pairs={{0,8},{4,12},{8,0},{12,4},{16,24},{20,28},{24,16},{28,20},{1,9},{5... | collective-permute-start | bytes 393224 | tf_op jit(solution)/shard_map/ppermute | solution.py:539
  129.4 11.8 %collective-permute-start.16 = (bf16[64,1024]{1,0:T(8,128)(2,1)}, bf16[64,1024]{1,0:T(8,128)(2,1)S(1)}, u32[]{:S(2)}, u32[]{:S(2)}) collective-permute-start(bf16[64,1024]{1,0:T(8,128)(2,1)} %get-tuple-element.98.refs_0_), channel_id=1, source_target_pairs={{0,16},{4,20},{8,24},{12,28},{16,0},{20,4},{24,8},{28,12},{1,17},{... | collective-permute-start | bytes 393224 | tf_op jit(solution)/shard_map/ppermute | solution.py:539
  131.4 9.8 %collective-permute-start.17 = (bf16[64,1024]{1,0:T(8,128)(2,1)}, bf16[64,1024]{1,0:T(8,128)(2,1)S(1)}, u32[]{:S(2)}, u32[]{:S(2)}) collective-permute-start(bf16[64,1024]{1,0:T(8,128)(2,1)} %get-tuple-element.98.refs_0_), channel_id=1, source_target_pairs={{0,24},{4,28},{8,16},{12,20},{16,8},{20,12},{24,0},{28,4},{1,25},{... | collective-permute-start | bytes 393224 | tf_op jit(solution)/shard_map/ppermute | solution.py:539
  134.6 8.4 %collective-permute-start.12 = (bf16[256,1024]{1,0:T(8,128)(2,1)}, bf16[256,1024]{1,0:T(8,128)(2,1)S(1)}, u32[]{:S(2)}, u32[]{:S(2)}) collective-permute-start(bf16[256,1024]{1,0:T(8,128)(2,1)} %stack_rows.2.refs_0_), channel_id=1, source_target_pairs={{0,4},{4,0},{8,12},{12,8},{16,20},{20,16},{24,28},{28,24},{1,5},{5... | collective-permute-start | bytes 1572872 | tf_op jit(solution)/shard_map/ppermute | solution.py:542
  141.2 0.9 copy-start.8
  142.9 2.3 %collective-permute-start.18 = (bf16[256,1024]{1,0:T(8,128)(2,1)}, bf16[256,1024]{1,0:T(8,128)(2,1)}, u32[]{:S(2)}, u32[]{:S(2)}) collective-permute-start(bf16[256,1024]{1,0:T(8,128)(2,1)} %stack_rows.3.refs_2_), channel_id=1, source_target_pairs={{0,4},{4,0},{8,12},{12,8},{16,20},{20,16},{24,28},{28,24},{1,5},{5... | collective-permute-start | bytes 1572872 | tf_op jit(solution)/shard_map/ppermute | solution.py:542
  143.0 0.8 copy-start.12
  148.7 7.1 %collective-permute-start.19 = (bf16[8,16,640]{2,1,0:T(8,128)(2,1)S(1)}, bf16[8,16,640]{2,1,0:T(8,128)(2,1)S(1)}, u32[]{:S(2)}, u32[]{:S(2)}) collective-permute-start(bf16[8,16,640]{2,1,0:T(8,128)(2,1)S(1)} %get-tuple-element.100), channel_id=1, source_target_pairs={{0,1},{1,0},{2,3},{3,2},{4,5},{5,4},{6,7},{7,6},{8,9},{9,8},{10,11... | collective-permute-start | bytes 491528 | tf_op jit(solution)/shard_map/ppermute | solution.py:536
  150.7 9.5 %collective-permute-start.20 = (bf16[8,16,640]{2,1,0:T(8,128)(2,1)S(1)}, bf16[8,16,640]{2,1,0:T(8,128)(2,1)S(1)}, u32[]{:S(2)}, u32[]{:S(2)}) collective-permute-start(bf16[8,16,640]{2,1,0:T(8,128)(2,1)S(1)} %get-tuple-element.101), channel_id=1, source_target_pairs={{0,2},{1,3},{2,0},{3,1},{4,6},{5,7},{6,4},{7,5},{8,10},{9,11},{10,... | collective-permute-start | bytes 491528 | tf_op jit(solution)/shard_map/ppermute | solution.py:536
  152.2 8.0 %collective-permute-start.21 = (bf16[8,16,640]{2,1,0:T(8,128)(2,1)S(1)}, bf16[8,16,640]{2,1,0:T(8,128)(2,1)S(1)}, u32[]{:S(2)}, u32[]{:S(2)}) collective-permute-start(bf16[8,16,640]{2,1,0:T(8,128)(2,1)S(1)} %get-tuple-element.102), channel_id=1, source_target_pairs={{0,3},{1,2},{2,1},{3,0},{4,7},{5,6},{6,5},{7,4},{8,11},{9,10},{10,... | collective-permute-start | bytes 491528 | tf_op jit(solution)/shard_map/ppermute | solution.py:536
  161.0 12.0 %all-to-all-start.4 = ((bf16[8,16,640]{2,1,0:T(8,128)(2,1)}), bf16[8,16,640]{2,1,0:T(8,128)(2,1)S(1)}, u32[]{:S(2)}, u32[]{:S(2)}) async-start(bf16[8,16,640]{2,1,0:T(8,128)(2,1)} %member_sum.1), calls=%async_computation.4 | async-start | bytes 327680 | tf_op jit(solution)/shard_map/all_to_all | solution.py:600

commit v3 on v2

--- a/solution.py
+++ b/solution.py
@@ -216,21 +216,20 @@
 def update_output_proj(members, squares, qo, earlier, deps):
     rows = qo[0].shape[1]
     width = qo[0].shape[2] // members
-    half = members // 2
     untouched = list(earlier) + list(deps)
-    spec = pl.BlockSpec((1, rows, half * width), lambda i: (1, 0, i))
+    spec = pl.BlockSpec((1, rows, width), lambda i: (1, 0, i))
     return pl.pallas_call(
         output_proj_kernel,
         name="adam_out",
-        grid=(2,),
+        grid=(members,),
         in_specs=[pl.BlockSpec(squares.shape, lambda i: (0, 0, 0))]
         + [spec] * 4
         + [ANY] * len(untouched),
-        out_specs=[spec] * 3 + [pl.BlockSpec((half, rows, width), lambda i: (i, 0, 0))],
+        out_specs=[spec] * 3 + [pl.BlockSpec((1, rows, width), lambda i: (i, 0, 0))],
         out_shape=[pltpu.HBM(x.shape, F32) for x in qo[:3]]
         + [pltpu.HBM((members, rows, width), BF16)],
         input_output_aliases={5 + n: n for n in range(len(earlier))},
-        compiler_params=pltpu.CompilerParams(vmem_limit_bytes=2 * wide_vmem - kernel_vmem // 6),
+        compiler_params=pltpu.CompilerParams(vmem_limit_bytes=wide_vmem),
         cost_estimate=small_cost,
     )(squares, *qo, *untouched)
 
@@ -365,7 +364,7 @@
     rows, width = parts[0].shape
     slots, head_dim = cache[0].shape[2:]
     groups = width // head_dim - 2
-    block = 16
+    block = 32
     row_block = lambda columns: pl.BlockSpec((block, columns), lambda i: (i, 0))
     cache_block = pl.BlockSpec((block, 1, slots, head_dim), lambda i: (i, head, 0, 0))
     return pl.pallas_call(

time: 175 us -> 174 us (level)
  starting transfers between devices: 47.6 us -> 51.1 us
  Pallas kernels: 76.1 us -> 73.3 us
    ppermute x12, starting transfers between devices: 17.6 us -> 21.7 us  [swap_zone(): return lax.ppermute(x, 'fsdp', xor_perm(shards, 2 * mask))]
    pallas_call x2, Pallas kernels: 11.8 us -> 9.61 us  [attend(): pl.pallas_call(functools.partial(attend_kernel, len(parts)), name='attend...]
    unnamed x30 -> x22, local copies, waits for them, and re-layouts: 5.75 us -> 5.75 us
  transfers between devices with their start and end apart: 27 -> 27, of which waited for: 13 -> 13; matrix products, arithmetic and copies ran while one was open for 1% -> 1% of each run, Pallas kernels for 35% -> 33%
where the time goes in v3:
time: 174 us; the launch traced here: 173 us
  Pallas kernels  73.3 us (42%)
  starting transfers between devices  51.1 us (29%)
  waiting for transfers between devices  41.7 us (24%)
  local copies, waits for them, and re-layouts  5.82 us (3%)
    pallas_call x3, Pallas kernels, update_input_proj(): pl.pallas_call(functools.partial(input_proj_kernel, first is None, len(sl...  25.2 us
    ppermute x12, starting transfers between devices, swap_zone(): return lax.ppermute(x, 'fsdp', xor_perm(shards, 2 * mask))  21.7 us
    pallas_call x1, Pallas kernels, update_output_proj(): pl.pallas_call(output_proj_kernel, name='adam_out', grid=(members,), in_s...  15.9 us
    ppermute x6, waiting for transfers between devices, swap_member(): return lax.ppermute(x, 'tp', xor_perm(members, mask))  12.4 us
    ppermute x12, waiting for transfers between devices, swap_zone(): return lax.ppermute(x, 'fsdp', xor_perm(shards, 2 * mask))  11.6 us
    pallas_call x2, Pallas kernels, attend(): pl.pallas_call(functools.partial(attend_kernel, len(parts)), name='attend...  9.61 us
    all_to_all x1, starting transfers between devices, local(): squares = lax.all_to_all(spread, ('fsdp', 'tp'), 0, 0)  7.3 us
    ppermute x6, starting transfers between devices, swap_member(): return lax.ppermute(x, 'tp', xor_perm(members, mask))  7.18 us
  transfers between devices with their start and end apart: 27, of which 13 were waited for; matrix products, arithmetic and copies ran while one was open for 1% of the time, Pallas kernels for 33%

profile of v3, /device:TPU:0, one launch (start us, length us, event | category | flops | bytes accessed | tf_op | source)
XLA Modules:
  0.0 173.1 jit_solution(17492767282330501043)
XLA Ops:
  0.7 6.1 %grad_squares.1 = f32[32,1,128]{2,1,0:T(1,128)} custom-call(f32[2,160,8192]{2,1,0:T(8,128)} %refs_3_.9, f32[2,160,1024]{2,1,0:T(8,128)} %refs_7_.5), custom_call_target="tpu_custom_call" | custom-call | flops 1024 | bytes 1024 | tf_op jit(solution)/shard_map/grad_squares/pallas_call | solution.py:85
  6.7 7.3 %all-to-all-start = ((f32[32,1,128]{2,1,0:T(1,128)}), f32[32,1,128]{2,1,0:T(1,128)S(1)}, u32[]{:S(2)}, u32[]{:S(2)}) async-start(f32[32,1,128]{2,1,0:T(1,128)} %grad_squares.1), calls=%async_computation | async-start | bytes 32768 | tf_op jit(solution)/shard_map/all_to_all | solution.py:552
  14.0 1.1 norm_rows.1
  15.1 6.0 %all-to-all-done.squares_ref = f32[32,1,128]{2,1,0:T(1,128)S(1)} async-done(((f32[32,1,128]{2,1,0:T(1,128)}), f32[32,1,128]{2,1,0:T(1,128)S(1)}, u32[]{:S(2)}, u32[]{:S(2)}) %all-to-all-start) | async-done | bytes 16416 | tf_op jit(solution)/shard_map/all_to_all | solution.py:552
  21.1 2.6 %all-to-all-start.1 = ((bf16[32,16,640]{2,1,0:T(8,128)(2,1)}), bf16[32,16,640]{2,1,0:T(8,128)(2,1)S(1)}, u32[]{:S(2)}, u32[]{:S(2)}) async-start(bf16[32,16,640]{2,1,0:T(8,128)(2,1)} %norm_rows.1), calls=%async_computation.1 | async-start | bytes 1310720 | tf_op jit(solution)/shard_map/all_to_all | solution.py:548
  23.7 10.4 %adam_in.3 = (f32[2,160,8192]{2,1,0:T(8,128)}, f32[2,160,1024]{2,1,0:T(8,128)}, f32[2,160,8192]{2,1,0:T(8,128)}, f32[2,160,1024]{2,1,0:T(8,128)}, f32[2,160,8192...) custom-call(s32[1]{0:T(128)} %bitcast.me_ref, ...), custom_call_target="tpu_custom_call" | custom-call | flops 1024 | bytes 1024 | tf_op jit(solution)/shard_map/adam_in/pallas_call | solution.py:186
  34.2 1.7 collective-permute-start
  35.9 1.5 collective-permute-start.1
  37.4 0.4 collective-permute-start.2
  37.7 10.5 %adam_in.4 = (f32[2,160,8192]{2,1,0:T(8,128)}, f32[2,160,1024]{2,1,0:T(8,128)}, f32[2,160,8192]{2,1,0:T(8,128)}, f32[2,160,1024]{2,1,0:T(8,128)}, f32[2,160,8192...) custom-call(s32[1]{0:T(128)} %bitcast.me_ref, ...), custom_call_target="tpu_custom_call", output_to_operand_aliasing={{0}: (10, {}), {1}: (11, {}), {2}: (12, {}), {3}: (13, {}),... | custom-call | flops 1024 | bytes 1024 | tf_op jit(solution)/shard_map/adam_in/pallas_call | solution.py:186
  48.2 4.3 %adam_in.5 = (f32[2,160,8192]{2,1,0:T(8,128)}, f32[2,160,1024]{2,1,0:T(8,128)}, f32[2,160,8192]{2,1,0:T(8,128)}, f32[2,160,1024]{2,1,0:T(8,128)}, f32[2,160,8192...) custom-call(s32[1]{0:T(128)} %bitcast.me_ref, ...), custom_call_target="tpu_custom_call", output_to_operand_aliasing={{0}: (10, {}), {1}: (11, {}), {2}: (12, {}), {3}: (13, {}),... | custom-call | flops 1024 | bytes 1024 | tf_op jit(solution)/shard_map/adam_in/pallas_call | solution.py:186
  52.5 3.5 %collective-permute-done.1.refs_2_ = bf16[160,1280]{1,0:T(8,128)(2,1)S(1)} collective-permute-done((bf16[160,1280]{1,0:T(8,128)(2,1)}, bf16[160,1280]{1,0:T(8,128)(2,1)S(1)}, u32[]{:S(2)}, u32[]{:S(2)}) %collective-permute-start.1) | collective-permute-done | bytes 409632 | tf_op jit(solution)/shard_map/ppermute | solution.py:535
  56.1 0.9 collective-permute-done.2.refs_3_
  57.0 1.0 copy-done.1
  58.0 2.4 %project.2 = (bf16[256,1280]{1,0:T(8,128)(2,1)}, f32[256,1280]{1,0:T(8,128)}) custom-call(s32[1]{0:T(128)} %bitcast.me_ref, s32[1]{0:T(128)} %bitcast.1.shard_ref, bf16[8,64,640]{2,1,0:T(8,128)(2,1)S(1)} %bitcast.12, bf16[160,1280]{1,0:T(8,128)(2,1)S(1)} %copy-done.1, bf16[160,1280]{1,0:T(8,128)(2,1)S(1)} %collective-permute-done.refs_1_, ...), custom_call_target="tpu_custom_call" | custom-call | flops 1024 | bytes 1024 | tf_op jit(solution)/shard_map/project/pallas_call | solution.py:271
  60.4 3.7 %all-to-all-start.2 = ((bf16[4,160,1280]{2,1,0:T(8,128)(2,1)}), bf16[4,160,1280]{2,1,0:T(8,128)(2,1)S(1)}, u32[]{:S(2)}, u32[]{:S(2)}) async-start(bf16[4,160,1280]{2,1,0:T(8,128)(2,1)} %tie.2), calls=%async_computation.2 | async-start | bytes 3276800 | tf_op jit(solution)/shard_map/all_to_all | solution.py:573
  64.1 0.1 collective-permute-start.3
  64.2 2.1 %collective-permute-done.3.arrived_ref = bf16[256,1280]{1,0:T(8,128)(2,1)S(1)} collective-permute-done((bf16[256,1280]{1,0:T(8,128)(2,1)S(1)}, bf16[256,1280]{1,0:T(8,128)(2,1)S(1)}, u32[]{:S(2)}, u32[]{:S(2)}) %collective-permute-start.3) | collective-permute-done | bytes 655392 | tf_op jit(solution)/shard_map/ppermute | solution.py:541
  66.3 2.2 %core_sum.2 = (f32[64,1280]{1,0:T(8,128)}, bf16[64,1280]{1,0:T(8,128)(2,1)S(1)}, bf16[64,1280]{1,0:T(8,128)(2,1)S(1)}, bf16[64,1280]{1,0:T(8,128)(2,1)S(1)}) custom-call(f32[256,1280]{1,0:T(8,128)} %get-tuple-element.77.keep_ref, bf16[256,1280]{1,0:T(8,128)(2,1)S(1)} %collective-permute-done.3.arrived_ref), custom_call_target="tpu_custom_call" | custom-call | flops 1024 | bytes 1024 | tf_op jit(solution)/shard_map/core_sum/pallas_call | solution.py:298
  68.4 1.6 collective-permute-start.4
  70.0 2.1 %collective-permute-start.5 = (bf16[64,1280]{1,0:T(8,128)(2,1)S(1)}, bf16[64,1280]{1,0:T(8,128)(2,1)S(1)}, u32[]{:S(2)}, u32[]{:S(2)}) collective-permute-start(bf16[64,1280]{1,0:T(8,128)(2,1)S(1)} %get-tuple-element.80.refs_8_), channel_id=1, source_target_pairs={{0,16},{4,20},{8,24},{12,28},{16,0},{20,4},{24,8},{28,12},{1,17},{... | collective-permute-start | bytes 491528 | tf_op jit(solution)/shard_map/ppermute | solution.py:538
  72.1 0.7 collective-permute-start.6
  72.8 15.9 %adam_out.1 = (f32[2,160,8192]{2,1,0:T(8,128)}, f32[2,160,8192]{2,1,0:T(8,128)}, f32[2,160,8192]{2,1,0:T(8,128)}, bf16[4,160,2048]{2,1,0:T(8,128)(2,1)}) custom-call(f32[32,1,128]{2,1,0:T(1,128)S(1)} %all-to-all-done.squares_ref, f32[2,160,8192]{2,1,0:T(8,128)} %refs_0_.7, ...), custom_call_target="tpu_custom_call", output_to_operand_aliasing={{0}: (5, {}), {1}: (6, {}), {2}: (7, {})} | custom-call | flops 1024 | bytes 1024 | tf_op jit(solution)/shard_map/adam_out/pallas_call | solution.py:221
  88.7 1.7 copy-done
  90.5 2.3 %project.3 = (bf16[256,1280]{1,0:T(8,128)(2,1)}, f32[256,1280]{1,0:T(8,128)}) custom-call(s32[1]{0:T(128)} %bitcast.me_ref, s32[1]{0:T(128)} %bitcast.1.shard_ref, bf16[8,64,640]{2,1,0:T(8,128)(2,1)S(1)} %bitcast.13, bf16[640,1280]{1,0:T(8,128)(2,1)S(1)} %bitcast.11, bf16[4,160,2048]{2,1,0:T(8,128)(2,1)S(1)} %copy-done, ...), custom_call_target="tpu_custom_call" | custom-call | flops 1024 | bytes 1024 | tf_op jit(solution)/shard_map/project/pallas_call | solution.py:271
  92.7 4.2 %all-to-all-start.3 = ((bf16[4,160,2048]{2,1,0:T(8,128)(2,1)}), bf16[4,160,2048]{2,1,0:T(8,128)(2,1)S(1)}, u32[]{:S(2)}, u32[]{:S(2)}) async-start(bf16[4,160,2048]{2,1,0:T(8,128)(2,1)} %tie.3), calls=%async_computation.3 | async-start | bytes 5242880 | tf_op jit(solution)/shard_map/all_to_all | solution.py:594
  97.0 2.3 %collective-permute-done.7.arrived_ref = bf16[256,1280]{1,0:T(8,128)(2,1)S(1)} collective-permute-done((bf16[256,1280]{1,0:T(8,128)(2,1)}, bf16[256,1280]{1,0:T(8,128)(2,1)S(1)}, u32[]{:S(2)}, u32[]{:S(2)}) %collective-permute-start.7) | collective-permute-done | bytes 655392 | tf_op jit(solution)/shard_map/ppermute | solution.py:541
  99.3 2.1 %core_sum.3 = (f32[64,1280]{1,0:T(8,128)}, bf16[64,1280]{1,0:T(8,128)(2,1)S(1)}, bf16[64,1280]{1,0:T(8,128)(2,1)S(1)}, bf16[64,1280]{1,0:T(8,128)(2,1)S(1)}) custom-call(f32[256,1280]{1,0:T(8,128)} %get-tuple-element.91.keep_ref, bf16[256,1280]{1,0:T(8,128)(2,1)S(1)} %collective-permute-done.7.arrived_ref), custom_call_target="tpu_custom_call" | custom-call | flops 1024 | bytes 1024 | tf_op jit(solution)/shard_map/core_sum/pallas_call | solution.py:298
  101.4 0.7 collective-permute-start.8
  102.1 0.2 fusion
  102.3 3.1 %collective-permute-start.13 = (bf16[64,1280]{1,0:T(8,128)(2,1)S(1)}, bf16[64,1280]{1,0:T(8,128)(2,1)S(1)}, u32[]{:S(2)}, u32[]{:S(2)}) collective-permute-start(bf16[64,1280]{1,0:T(8,128)(2,1)S(1)} %get-tuple-element.96), channel_id=1, source_target_pairs={{0,16},{4,20},{8,24},{12,28},{16,0},{20,4},{24,8},{28,12},{1,17},{... | collective-permute-start | bytes 491528 | tf_op jit(solution)/shard_map/ppermute | solution.py:538
  105.4 0.7 collective-permute-start.14
  106.1 0.1 pad_maximum_fusion
  106.2 4.4 %collective-permute-done.8.refs_10_.refs_7_ = bf16[64,1280]{1,0:T(8,128)(2,1)S(1)} collective-permute-done((bf16[64,1280]{1,0:T(8,128)(2,1)S(1)}, bf16[64,1280]{1,0:T(8,128)(2,1)S(1)}, u32[]{:S(2)}, u32[]{:S(2)}) %collective-permute-start.8) | collective-permute-done | bytes 163872 | tf_op jit(solution)/shard_map/ppermute | solution.py:538
  110.5 0.1 broadcast_in_dim.2.refs_0_
  110.6 4.8 %attend.2 = (bf16[64,1024]{1,0:T(8,128)(2,1)}, bf16[64,128]{1,0:T(8,128)(2,1)S(1)}, bf16[64,128]{1,0:T(8,128)(2,1)S(1)}) custom-call(s32[64,128]{1,0:T(8,128)S(1)} %broadcast_in_dim.2.refs_0_, f32[64,128]{1,0:T(8,128)S(1)} %get-tuple-element.119.refs_1_, f32[64,128]{1,0:T(8,128)S(1)} %get-tuple-element.120.refs_2_, f32[2,128]{1,0:T(2,128)S(1)} %copy-done.6, ...), custom_call_target="tpu_custom_call" | custom-call | flops 1024 | bytes 1024 | tf_op jit(solution)/shard_map/attend/pallas_call | solution.py:370
  115.4 2.6 %collective-permute-start.10 = (bf16[64,1024]{1,0:T(8,128)(2,1)}, bf16[64,1024]{1,0:T(8,128)(2,1)S(1)}, u32[]{:S(2)}, u32[]{:S(2)}) collective-permute-start(bf16[64,1024]{1,0:T(8,128)(2,1)} %get-tuple-element.94.refs_0_), channel_id=1, source_target_pairs={{0,16},{4,20},{8,24},{12,28},{16,0},{20,4},{24,8},{28,12},{1,17},{... | collective-permute-start | bytes 393224 | tf_op jit(solution)/shard_map/ppermute | solution.py:538
  118.0 1.8 %collective-permute-start.11 = (bf16[64,1024]{1,0:T(8,128)(2,1)}, bf16[64,1024]{1,0:T(8,128)(2,1)S(1)}, u32[]{:S(2)}, u32[]{:S(2)}) collective-permute-start(bf16[64,1024]{1,0:T(8,128)(2,1)} %get-tuple-element.94.refs_0_), channel_id=1, source_target_pairs={{0,24},{4,28},{8,16},{12,20},{16,8},{20,12},{24,0},{28,4},{1,25},{... | collective-permute-start | bytes 393224 | tf_op jit(solution)/shard_map/ppermute | solution.py:538
  119.8 1.2 collective-permute-done.9.refs_1_.refs_10_
  121.0 4.8 %attend.3 = (bf16[64,1024]{1,0:T(8,128)(2,1)}, bf16[64,128]{1,0:T(8,128)(2,1)S(1)}, bf16[64,128]{1,0:T(8,128)(2,1)S(1)}) custom-call(s32[64,128]{1,0:T(8,128)S(1)} %broadcast_in_dim.2.refs_0_, f32[64,128]{1,0:T(8,128)S(1)} %get-tuple-element.119.refs_1_, f32[64,128]{1,0:T(8,128)S(1)} %get-tuple-element.120.refs_2_, f32[2,128]{1,0:T(2,128)S(1)} %copy-done.6, ...), custom_call_target="tpu_custom_call" | custom-call | flops 1024 | bytes 1024 | tf_op jit(solution)/shard_map/attend/pallas_call | solution.py:370
  125.8 6.1 %collective-permute-start.15 = (bf16[64,1024]{1,0:T(8,128)(2,1)}, bf16[64,1024]{1,0:T(8,128)(2,1)S(1)}, u32[]{:S(2)}, u32[]{:S(2)}) collective-permute-start(bf16[64,1024]{1,0:T(8,128)(2,1)} %get-tuple-element.98.refs_0_), channel_id=1, source_target_pairs={{0,8},{4,12},{8,0},{12,4},{16,24},{20,28},{24,16},{28,20},{1,9},{5... | collective-permute-start | bytes 393224 | tf_op jit(solution)/shard_map/ppermute | solution.py:538
  132.0 0.9 collective-permute-start.16
  132.9 1.5 collective-permute-start.17
  134.3 0.8 stack_rows.2.refs_0_
  135.2 0.1 collective-permute-start.12
  135.3 1.1 collective-permute-done.15.refs_1_
  136.4 4.9 %collective-permute-done.16.refs_2_ = bf16[64,1024]{1,0:T(8,128)(2,1)S(1)} collective-permute-done((bf16[64,1024]{1,0:T(8,128)(2,1)}, bf16[64,1024]{1,0:T(8,128)(2,1)S(1)}, u32[]{:S(2)}, u32[]{:S(2)}) %collective-permute-start.16) | collective-permute-done | bytes 131104 | tf_op jit(solution)/shard_map/ppermute | solution.py:538
  141.2 0.9 copy-done.4
  142.1 0.8 stack_rows.3.refs_2_
  143.0 0.1 collective-permute-start.18
  143.1 0.8 copy-done.8
  143.9 1.4 collective-permute-done.18.refs_3_
  145.3 3.4 %expand.1 = (f32[8,16,640]{2,1,0:T(8,128)S(1)}, bf16[8,16,640]{2,1,0:T(8,128)(2,1)S(1)}, bf16[8,16,640]{2,1,0:T(8,128)(2,1)S(1)}, bf16[8,16,640]{2,1,0:T(8,128)(2,1)S(1)}) custom-call(s32[1]{0:T(128)} %bitcast.1.shard_ref, s32[1]{0:T(128)} %bitcast.me_ref, bf16[256,1024]{1,0:T(8,128)(2,1)} %stack_rows.2.refs_0_, bf16[256,1024]{1,0:T(8,128)(2,1)} %copy-done.8, ...), custom_call_target="tpu_custom_call" | custom-call | flops 1024 | bytes 1024 | tf_op jit(solution)/shard_map/expand/pallas_call | solution.py:454
  148.7 2.1 %collective-permute-start.19 = (bf16[8,16,640]{2,1,0:T(8,128)(2,1)S(1)}, bf16[8,16,640]{2,1,0:T(8,128)(2,1)S(1)}, u32[]{:S(2)}, u32[]{:S(2)}) collective-permute-start(bf16[8,16,640]{2,1,0:T(8,128)(2,1)S(1)} %get-tuple-element.100), channel_id=1, source_target_pairs={{0,1},{1,0},{2,3},{3,2},{4,5},{5,4},{6,7},{7,6},{8,9},{9,8},{10,11... | collective-permute-start | bytes 491528 | tf_op jit(solution)/shard_map/ppermute | solution.py:535
  150.8 1.5 collective-permute-start.20
  152.3 0.1 collective-permute-start.21
  152.4 3.4 %collective-permute-done.19.refs_1_ = bf16[8,16,640]{2,1,0:T(8,128)(2,1)S(1)} collective-permute-done((bf16[8,16,640]{2,1,0:T(8,128)(2,1)S(1)}, bf16[8,16,640]{2,1,0:T(8,128)(2,1)S(1)}, u32[]{:S(2)}, u32[]{:S(2)}) %collective-permute-start.19) | collective-permute-done | bytes 163872 | tf_op jit(solution)/shard_map/ppermute | solution.py:535
  155.8 4.5 %collective-permute-done.20.refs_2_ = bf16[8,16,640]{2,1,0:T(8,128)(2,1)S(1)} collective-permute-done((bf16[8,16,640]{2,1,0:T(8,128)(2,1)S(1)}, bf16[8,16,640]{2,1,0:T(8,128)(2,1)S(1)}, u32[]{:S(2)}, u32[]{:S(2)}) %collective-permute-start.20) | collective-permute-done | bytes 163872 | tf_op jit(solution)/shard_map/ppermute | solution.py:535
  160.3 0.7 member_sum.1
  161.0 4.2 %all-to-all-start.4 = ((bf16[8,16,640]{2,1,0:T(8,128)(2,1)}), bf16[8,16,640]{2,1,0:T(8,128)(2,1)S(1)}, u32[]{:S(2)}, u32[]{:S(2)}) async-start(bf16[8,16,640]{2,1,0:T(8,128)(2,1)} %member_sum.1), calls=%async_computation.4 | async-start | bytes 327680 | tf_op jit(solution)/shard_map/all_to_all | solution.py:599
  165.2 0.6 copy.41
  165.9 0.7 copy.40
  166.5 5.9 %all-to-all-done.4.pieces_ref = bf16[8,16,640]{2,1,0:T(8,128)(2,1)S(1)} async-done(((bf16[8,16,640]{2,1,0:T(8,128)(2,1)}), bf16[8,16,640]{2,1,0:T(8,128)(2,1)S(1)}, u32[]{:S(2)}, u32[]{:S(2)}) %all-to-all-start.4) | async-done | bytes 163872 | tf_op jit(solution)/shard_map/all_to_all | solution.py:599
  172.4 0.7 finish.1
  (38 shorter events, 0.1 us)
Async XLA Ops:
  0.6 13.4 %copy-start.5 = (f32[5120]{0:T(1024)S(1)}, f32[5120]{0:T(1024)}, u32[]{:S(2)}) copy-start(f32[5120]{0:T(1024)} %param.23) | copy-start | bytes 61444
  0.7 13.4 %copy-start.2 = (bf16[16,5120]{1,0:T(8,128)(2,1)S(1)}, bf16[16,5120]{1,0:T(8,128)(2,1)}, u32[]{:S(2)}) copy-start(bf16[16,5120]{1,0:T(8,128)(2,1)} %hidden_ref.3) | copy-start | bytes 491524
  6.7 14.4 %all-to-all-start = ((f32[32,1,128]{2,1,0:T(1,128)}), f32[32,1,128]{2,1,0:T(1,128)S(1)}, u32[]{:S(2)}, u32[]{:S(2)}) async-start(f32[32,1,128]{2,1,0:T(1,128)} %grad_squares.1), calls=%async_computation | async-start | bytes 32768 | tf_op jit(solution)/shard_map/all_to_all | solution.py:552
  21.1 35.8 %all-to-all-start.1 = ((bf16[32,16,640]{2,1,0:T(8,128)(2,1)}), bf16[32,16,640]{2,1,0:T(8,128)(2,1)S(1)}, u32[]{:S(2)}, u32[]{:S(2)}) async-start(bf16[32,16,640]{2,1,0:T(8,128)(2,1)} %norm_rows.1), calls=%async_computation.1 | async-start | bytes 1310720 | tf_op jit(solution)/shard_map/all_to_all | solution.py:548
  34.2 18.4 %collective-permute-start = (bf16[160,1280]{1,0:T(8,128)(2,1)}, bf16[160,1280]{1,0:T(8,128)(2,1)S(1)}, u32[]{:S(2)}, u32[]{:S(2)}) collective-permute-start(bf16[160,1280]{1,0:T(8,128)(2,1)} %get-tuple-element.74), channel_id=1, source_target_pairs={{0,1},{1,0},{2,3},{3,2},{4,5},{5,4},{6,7},{7,6},{8,9},{9,8},{10,11... | collective-permute-start | bytes 1228808 | tf_op jit(solution)/shard_map/ppermute | solution.py:535
  35.9 20.2 %collective-permute-start.1 = (bf16[160,1280]{1,0:T(8,128)(2,1)}, bf16[160,1280]{1,0:T(8,128)(2,1)S(1)}, u32[]{:S(2)}, u32[]{:S(2)}) collective-permute-start(bf16[160,1280]{1,0:T(8,128)(2,1)} %get-tuple-element.75), channel_id=1, source_target_pairs={{0,2},{1,3},{2,0},{3,1},{4,6},{5,7},{6,4},{7,5},{8,10},{9,11},{10,... | collective-permute-start | bytes 1228808 | tf_op jit(solution)/shard_map/ppermute | solution.py:535
  37.4 19.6 %collective-permute-start.2 = (bf16[160,1280]{1,0:T(8,128)(2,1)}, bf16[160,1280]{1,0:T(8,128)(2,1)S(1)}, u32[]{:S(2)}, u32[]{:S(2)}) collective-permute-start(bf16[160,1280]{1,0:T(8,128)(2,1)} %get-tuple-element.76), channel_id=1, source_target_pairs={{0,3},{1,2},{2,1},{3,0},{4,7},{5,6},{6,5},{7,4},{8,11},{9,10},{10,... | collective-permute-start | bytes 1228808 | tf_op jit(solution)/shard_map/ppermute | solution.py:535
  57.0 1.0 copy-start.1
  60.4 3.7 %copy-start.7 = (bf16[256,1280]{1,0:T(8,128)(2,1)S(1)}, bf16[256,1280]{1,0:T(8,128)(2,1)}, u32[]{:S(2)}) copy-start(bf16[256,1280]{1,0:T(8,128)(2,1)} %get-tuple-element.78.refs_1_) | copy-start | bytes 1966084
  60.4 28.3 %all-to-all-start.2 = ((bf16[4,160,1280]{2,1,0:T(8,128)(2,1)}), bf16[4,160,1280]{2,1,0:T(8,128)(2,1)S(1)}, u32[]{:S(2)}, u32[]{:S(2)}) async-start(bf16[4,160,1280]{2,1,0:T(8,128)(2,1)} %tie.2), calls=%async_computation.2 | async-start | bytes 3276800 | tf_op jit(solution)/shard_map/all_to_all | solution.py:573
  64.1 2.2 %collective-permute-start.3 = (bf16[256,1280]{1,0:T(8,128)(2,1)S(1)}, bf16[256,1280]{1,0:T(8,128)(2,1)S(1)}, u32[]{:S(2)}, u32[]{:S(2)}) collective-permute-start(bf16[256,1280]{1,0:T(8,128)(2,1)S(1)} %copy-done.7), channel_id=1, source_target_pairs={{0,4},{4,0},{8,12},{12,8},{16,20},{20,16},{24,28},{28,24},{1,5},{5... | collective-permute-start | bytes 1966088 | tf_op jit(solution)/shard_map/ppermute | solution.py:541
  68.4 20.2 %collective-permute-start.4 = (bf16[64,1280]{1,0:T(8,128)(2,1)S(1)}, bf16[64,1280]{1,0:T(8,128)(2,1)S(1)}, u32[]{:S(2)}, u32[]{:S(2)}) collective-permute-start(bf16[64,1280]{1,0:T(8,128)(2,1)S(1)} %get-tuple-element.79.refs_7_), channel_id=1, source_target_pairs={{0,8},{4,12},{8,0},{12,4},{16,24},{20,28},{24,16},{28,20},{1,9},{5... | collective-permute-start | bytes 491528 | tf_op jit(solution)/shard_map/ppermute | solution.py:538
  70.0 18.7 %collective-permute-start.5 = (bf16[64,1280]{1,0:T(8,128)(2,1)S(1)}, bf16[64,1280]{1,0:T(8,128)(2,1)S(1)}, u32[]{:S(2)}, u32[]{:S(2)}) collective-permute-start(bf16[64,1280]{1,0:T(8,128)(2,1)S(1)} %get-tuple-element.80.refs_8_), channel_id=1, source_target_pairs={{0,16},{4,20},{8,24},{12,28},{16,0},{20,4},{24,8},{28,12},{1,17},{... | collective-permute-start | bytes 491528 | tf_op jit(solution)/shard_map/ppermute | solution.py:538
  72.1 16.6 %collective-permute-start.6 = (bf16[64,1280]{1,0:T(8,128)(2,1)S(1)}, bf16[64,1280]{1,0:T(8,128)(2,1)S(1)}, u32[]{:S(2)}, u32[]{:S(2)}) collective-permute-start(bf16[64,1280]{1,0:T(8,128)(2,1)S(1)} %get-tuple-element.81.refs_9_), channel_id=1, source_target_pairs={{0,24},{4,28},{8,16},{12,20},{16,8},{20,12},{24,0},{28,4},{1,25},{... | collective-permute-start | bytes 491528 | tf_op jit(solution)/shard_map/ppermute | solution.py:538
  88.7 1.7 %copy-start = (bf16[4,160,2048]{2,1,0:T(8,128)(2,1)S(1)}, bf16[4,160,2048]{2,1,0:T(8,128)(2,1)}, u32[]{:S(2)}) copy-start(bf16[4,160,2048]{2,1,0:T(8,128)(2,1)} %get-tuple-element.90.refs_1_.refs_0_) | copy-start | bytes 7864324
  92.7 4.2 %copy-start.9 = (s32[64]{0:T(128)S(1)}, s32[64]{0:T(128)}, u32[]{:S(2)}) copy-start(s32[64]{0:T(128)} %param.27) | copy-start | bytes 772
  92.7 17.8 %copy-start.6 = (f32[2,128]{1,0:T(2,128)S(1)}, f32[2,128]{1,0:T(2,128)}, u32[]{:S(2)}) copy-start(f32[2,128]{1,0:T(2,128)} %refs_3_.11) | copy-start | bytes 3076
  92.7 52.5 %all-to-all-start.3 = ((bf16[4,160,2048]{2,1,0:T(8,128)(2,1)}), bf16[4,160,2048]{2,1,0:T(8,128)(2,1)S(1)}, u32[]{:S(2)}, u32[]{:S(2)}) async-start(bf16[4,160,2048]{2,1,0:T(8,128)(2,1)} %tie.3), calls=%async_computation.3 | async-start | bytes 5242880 | tf_op jit(solution)/shard_map/all_to_all | solution.py:594
  97.0 2.3 %collective-permute-start.7 = (bf16[256,1280]{1,0:T(8,128)(2,1)}, bf16[256,1280]{1,0:T(8,128)(2,1)S(1)}, u32[]{:S(2)}, u32[]{:S(2)}) collective-permute-start(bf16[256,1280]{1,0:T(8,128)(2,1)} %get-tuple-element.92.refs_1_), channel_id=1, source_target_pairs={{0,4},{4,0},{8,12},{12,8},{16,20},{20,16},{24,28},{28,24},{1,5},{5... | collective-permute-start | bytes 1966088 | tf_op jit(solution)/shard_map/ppermute | solution.py:541
  101.4 9.1 %collective-permute-start.8 = (bf16[64,1280]{1,0:T(8,128)(2,1)S(1)}, bf16[64,1280]{1,0:T(8,128)(2,1)S(1)}, u32[]{:S(2)}, u32[]{:S(2)}) collective-permute-start(bf16[64,1280]{1,0:T(8,128)(2,1)S(1)} %get-tuple-element.93), channel_id=1, source_target_pairs={{0,8},{4,12},{8,0},{12,4},{16,24},{20,28},{24,16},{28,20},{1,9},{5... | collective-permute-start | bytes 491528 | tf_op jit(solution)/shard_map/ppermute | solution.py:538
  102.3 17.5 %collective-permute-start.13 = (bf16[64,1280]{1,0:T(8,128)(2,1)S(1)}, bf16[64,1280]{1,0:T(8,128)(2,1)S(1)}, u32[]{:S(2)}, u32[]{:S(2)}) collective-permute-start(bf16[64,1280]{1,0:T(8,128)(2,1)S(1)} %get-tuple-element.96), channel_id=1, source_target_pairs={{0,16},{4,20},{8,24},{12,28},{16,0},{20,4},{24,8},{28,12},{1,17},{... | collective-permute-start | bytes 491528 | tf_op jit(solution)/shard_map/ppermute | solution.py:538
  105.4 14.4 %collective-permute-start.14 = (bf16[64,1280]{1,0:T(8,128)(2,1)S(1)}, bf16[64,1280]{1,0:T(8,128)(2,1)S(1)}, u32[]{:S(2)}, u32[]{:S(2)}) collective-permute-start(bf16[64,1280]{1,0:T(8,128)(2,1)S(1)} %get-tuple-element.97), channel_id=1, source_target_pairs={{0,24},{4,28},{8,16},{12,20},{16,8},{20,12},{24,0},{28,4},{1,25},{... | collective-permute-start | bytes 491528 | tf_op jit(solution)/shard_map/ppermute | solution.py:538
  115.4 5.6 %collective-permute-start.9 = (bf16[64,1024]{1,0:T(8,128)(2,1)}, bf16[64,1024]{1,0:T(8,128)(2,1)S(1)}, u32[]{:S(2)}, u32[]{:S(2)}) collective-permute-start(bf16[64,1024]{1,0:T(8,128)(2,1)} %get-tuple-element.94.refs_0_), channel_id=1, source_target_pairs={{0,8},{4,12},{8,0},{12,4},{16,24},{20,28},{24,16},{28,20},{1,9},{5... | collective-permute-start | bytes 393224 | tf_op jit(solution)/shard_map/ppermute | solution.py:538
  115.4 18.9 %collective-permute-start.10 = (bf16[64,1024]{1,0:T(8,128)(2,1)}, bf16[64,1024]{1,0:T(8,128)(2,1)S(1)}, u32[]{:S(2)}, u32[]{:S(2)}) collective-permute-start(bf16[64,1024]{1,0:T(8,128)(2,1)} %get-tuple-element.94.refs_0_), channel_id=1, source_target_pairs={{0,16},{4,20},{8,24},{12,28},{16,0},{20,4},{24,8},{28,12},{1,17},{... | collective-permute-start | bytes 393224 | tf_op jit(solution)/shard_map/ppermute | solution.py:538
  118.0 16.4 %collective-permute-start.11 = (bf16[64,1024]{1,0:T(8,128)(2,1)}, bf16[64,1024]{1,0:T(8,128)(2,1)S(1)}, u32[]{:S(2)}, u32[]{:S(2)}) collective-permute-start(bf16[64,1024]{1,0:T(8,128)(2,1)} %get-tuple-element.94.refs_0_), channel_id=1, source_target_pairs={{0,24},{4,28},{8,16},{12,20},{16,8},{20,12},{24,0},{28,4},{1,25},{... | collective-permute-start | bytes 393224 | tf_op jit(solution)/shard_map/ppermute | solution.py:538
  121.0 13.3 %copy-start.3 = (bf16[64,1024]{1,0:T(8,128)(2,1)S(1)}, bf16[64,1024]{1,0:T(8,128)(2,1)}, u32[]{:S(2)}) copy-start(bf16[64,1024]{1,0:T(8,128)(2,1)} %get-tuple-element.94.refs_0_) | copy-start | bytes 393220
  125.8 10.5 %collective-permute-start.15 = (bf16[64,1024]{1,0:T(8,128)(2,1)}, bf16[64,1024]{1,0:T(8,128)(2,1)S(1)}, u32[]{:S(2)}, u32[]{:S(2)}) collective-permute-start(bf16[64,1024]{1,0:T(8,128)(2,1)} %get-tuple-element.98.refs_0_), channel_id=1, source_target_pairs={{0,8},{4,12},{8,0},{12,4},{16,24},{20,28},{24,16},{28,20},{1,9},{5... | collective-permute-start | bytes 393224 | tf_op jit(solution)/shard_map/ppermute | solution.py:538
  132.0 9.3 %collective-permute-start.16 = (bf16[64,1024]{1,0:T(8,128)(2,1)}, bf16[64,1024]{1,0:T(8,128)(2,1)S(1)}, u32[]{:S(2)}, u32[]{:S(2)}) collective-permute-start(bf16[64,1024]{1,0:T(8,128)(2,1)} %get-tuple-element.98.refs_0_), channel_id=1, source_target_pairs={{0,16},{4,20},{8,24},{12,28},{16,0},{20,4},{24,8},{28,12},{1,17},{... | collective-permute-start | bytes 393224 | tf_op jit(solution)/shard_map/ppermute | solution.py:538
  132.9 8.4 %collective-permute-start.17 = (bf16[64,1024]{1,0:T(8,128)(2,1)}, bf16[64,1024]{1,0:T(8,128)(2,1)S(1)}, u32[]{:S(2)}, u32[]{:S(2)}) collective-permute-start(bf16[64,1024]{1,0:T(8,128)(2,1)} %get-tuple-element.98.refs_0_), channel_id=1, source_target_pairs={{0,24},{4,28},{8,16},{12,20},{16,8},{20,12},{24,0},{28,4},{1,25},{... | collective-permute-start | bytes 393224 | tf_op jit(solution)/shard_map/ppermute | solution.py:538
  135.2 7.9 %collective-permute-start.12 = (bf16[256,1024]{1,0:T(8,128)(2,1)}, bf16[256,1024]{1,0:T(8,128)(2,1)S(1)}, u32[]{:S(2)}, u32[]{:S(2)}) collective-permute-start(bf16[256,1024]{1,0:T(8,128)(2,1)} %stack_rows.2.refs_0_), channel_id=1, source_target_pairs={{0,4},{4,0},{8,12},{12,8},{16,20},{20,16},{24,28},{28,24},{1,5},{5... | collective-permute-start | bytes 1572872 | tf_op jit(solution)/shard_map/ppermute | solution.py:541
  141.2 0.9 copy-start.4
  143.0 2.3 %collective-permute-start.18 = (bf16[256,1024]{1,0:T(8,128)(2,1)}, bf16[256,1024]{1,0:T(8,128)(2,1)}, u32[]{:S(2)}, u32[]{:S(2)}) collective-permute-start(bf16[256,1024]{1,0:T(8,128)(2,1)} %stack_rows.3.refs_2_), channel_id=1, source_target_pairs={{0,4},{4,0},{8,12},{12,8},{16,20},{20,16},{24,28},{28,24},{1,5},{5... | collective-permute-start | bytes 1572872 | tf_op jit(solution)/shard_map/ppermute | solution.py:541
  143.1 0.8 copy-start.8
  148.7 7.1 %collective-permute-start.19 = (bf16[8,16,640]{2,1,0:T(8,128)(2,1)S(1)}, bf16[8,16,640]{2,1,0:T(8,128)(2,1)S(1)}, u32[]{:S(2)}, u32[]{:S(2)}) collective-permute-start(bf16[8,16,640]{2,1,0:T(8,128)(2,1)S(1)} %get-tuple-element.100), channel_id=1, source_target_pairs={{0,1},{1,0},{2,3},{3,2},{4,5},{5,4},{6,7},{7,6},{8,9},{9,8},{10,11... | collective-permute-start | bytes 491528 | tf_op jit(solution)/shard_map/ppermute | solution.py:535
  150.8 9.5 %collective-permute-start.20 = (bf16[8,16,640]{2,1,0:T(8,128)(2,1)S(1)}, bf16[8,16,640]{2,1,0:T(8,128)(2,1)S(1)}, u32[]{:S(2)}, u32[]{:S(2)}) collective-permute-start(bf16[8,16,640]{2,1,0:T(8,128)(2,1)S(1)} %get-tuple-element.101), channel_id=1, source_target_pairs={{0,2},{1,3},{2,0},{3,1},{4,6},{5,7},{6,4},{7,5},{8,10},{9,11},{10,... | collective-permute-start | bytes 491528 | tf_op jit(solution)/shard_map/ppermute | solution.py:535
  152.3 8.0 %collective-permute-start.21 = (bf16[8,16,640]{2,1,0:T(8,128)(2,1)S(1)}, bf16[8,16,640]{2,1,0:T(8,128)(2,1)S(1)}, u32[]{:S(2)}, u32[]{:S(2)}) collective-permute-start(bf16[8,16,640]{2,1,0:T(8,128)(2,1)S(1)} %get-tuple-element.102), channel_id=1, source_target_pairs={{0,3},{1,2},{2,1},{3,0},{4,7},{5,6},{6,5},{7,4},{8,11},{9,10},{10,... | collective-permute-start | bytes 491528 | tf_op jit(solution)/shard_map/ppermute | solution.py:535
  161.0 11.4 %all-to-all-start.4 = ((bf16[8,16,640]{2,1,0:T(8,128)(2,1)}), bf16[8,16,640]{2,1,0:T(8,128)(2,1)S(1)}, u32[]{:S(2)}, u32[]{:S(2)}) async-start(bf16[8,16,640]{2,1,0:T(8,128)(2,1)} %member_sum.1), calls=%async_computation.4 | async-start | bytes 327680 | tf_op jit(solution)/shard_map/all_to_all | solution.py:599
